TPU v7x, 32 devices: a whole 2x2x4 slice. The times are simulated.
32 devices in a mesh: dp: 16 (over z, x, core), tensor: 2 (over y).
Axes of the slice: x: 2, y: 2, z: 4, core: 2. Of those that a mesh axis runs over, the one named last changes fastest.
Arguments:
- tokens: bfloat16 [4096, 2048], P('dp'), may hold values from -6 to 6
- cotangent: bfloat16 [4096, 2048], P('dp'), may hold values from -6 to 6
- dealing: int32 [4096], replicated, may hold values from 0 to 4095, as said below
- lengths: int32 [16, 4], P('dp'), may hold values from 1 to 128, 256 in all within a row
- routes: int32 [4096, 8], P('dp'), may hold values from 0 to 15, all different within a row; in each aligned block of 256 rows (0 to 255, 256 to 511, ...) at most 160 rows name the same one
- attention_gain: float32 [2048], P('dp'), may hold values from 0.25 to 1.75
- query_weight: float32 [2048, 2048], P('dp', 'tensor'), may hold values from -0.125 to 0.125
- key_weight: float32 [2048, 2048], P('dp', 'tensor'), may hold values from -0.125 to 0.125
- value_weight: float32 [2048, 2048], P('dp', 'tensor'), may hold values from -0.125 to 0.125
- output_weight: float32 [2048, 2048], P('tensor', 'dp'), may hold values from -0.5 to 0.5
- query_gain: float32 [2, 1024], P('tensor', 'dp'), may hold values from 0.25 to 1.75
- key_gain: float32 [2, 1024], P('tensor', 'dp'), may hold values from 0.25 to 1.75
- ffn_gain: float32 [2048], P('dp'), may hold values from 0.25 to 1.75
- router_weight: float32 [2048, 16], P('dp'), may hold values from -0.0625 to 0.0625
- gate_weight: float32 [16, 2048, 1024], P(None, 'dp', 'tensor'), may hold values from -0.125 to 0.125
- up_weight: float32 [16, 2048, 1024], P(None, 'dp', 'tensor'), may hold values from -0.125 to 0.125
- down_weight: float32 [16, 1024, 2048], P(None, 'tensor', 'dp'), may hold values from -1.5 to 1.5
Outputs:
- block_out: bfloat16 [4096, 2048], P('dp')
- token_grad: bfloat16 [4096, 2048], P('dp')
- attention_gain_grad: float32 [2048], P('dp')
- query_weight_grad: float32 [2048, 2048], P('dp', 'tensor')
- key_weight_grad: float32 [2048, 2048], P('dp', 'tensor')
- value_weight_grad: float32 [2048, 2048], P('dp', 'tensor')
- output_weight_grad: float32 [2048, 2048], P('tensor', 'dp')
- query_gain_grad: float32 [2, 1024], P('tensor', 'dp')
- key_gain_grad: float32 [2, 1024], P('tensor', 'dp')
- ffn_gain_grad: float32 [2048], P('dp')
- router_weight_grad: float32 [2048, 16], P('dp')
- gate_weight_grad: float32 [16, 2048, 1024], P(None, 'dp', 'tensor')
- up_weight_grad: float32 [16, 2048, 1024], P(None, 'dp', 'tensor')
- down_weight_grad: float32 [16, 1024, 2048], P(None, 'tensor', 'dp')
Inputs may be any that keep to these rules, and one draw needn't show every extreme that they name: dealing is a permutation; the 256 processed rows of each block take exactly 16 given rows from each block of 256 given rows. `lengths`: each row sums to 256; the longest sequence of each block has 128 rows. `routes`: a row names 8 different experts; among the rows of one device no expert is named more than 160 times, and in some blocks one is named exactly 160 times.
All inputs are finite; a program needn't handle non-finite values.
Results may differ from a plain program's by a relative error of at most 0.018.
The roundings to bfloat16 on the way count: a program that leaves them out, or rounds other values in their place, can miss the bound.
Values may be sent and summed in bfloat16 or wider, within the bound.
No kernel may reach another device: no remote copies, remote signals or barrier semaphores. Data moves between devices by JAX's collectives and lax.ppermute only.
A program may use at most 320 MiB of HBM per device.

v0:
```python
import jax
import jax.numpy as jnp
from jax import lax
from jax.sharding import PartitionSpec as P

HEAD_DIM = 128
EXPERTS = 16
CAP = 160


EPS = 1e-05
ROPE_BASE = 10000.0
MASKED = -1e30


def row_scale(values):
    return lax.rsqrt(jnp.mean(values * values, -1, keepdims=True) + EPS)


def softmax_rows(values):
    peak_value = jnp.max(values, -1, keepdims=True)
    powered = jnp.exp(values - peak_value)
    return powered / jnp.sum(powered, -1, keepdims=True)


def inner_rows(left, right):
    return lax.dot_general(
        left, right, (((0,), (0,)), ((), ())), preferred_element_type=jnp.float32
    )


def outer_cols(left, right):
    return lax.dot_general(
        left, right, (((1,), (1,)), ((), ())), preferred_element_type=jnp.float32
    )


def segment_layout(seq_lengths, row_count):
    finish_at = jnp.cumsum(seq_lengths)
    start_at = finish_at - seq_lengths
    places = jnp.arange(row_count, dtype=jnp.int32)
    segment_ids = jnp.sum((places[:, None] >= finish_at[None, :]).astype(jnp.int32), -1)
    numbers = jnp.arange(seq_lengths.shape[0], dtype=jnp.int32)
    begins = jnp.sum(jnp.where(segment_ids[:, None] == numbers[None, :], start_at[None, :], 0), -1)
    return (segment_ids, places - begins)


def rope_tables(positions, head_size):
    half_size = head_size // 2
    freq_table = ROPE_BASE ** (-2.0 * jnp.arange(half_size, dtype=jnp.float32) / head_size)
    angles = positions[:, None] * freq_table[None, :]
    angles = jnp.concatenate([angles, angles], -1)
    return (jnp.cos(angles), jnp.sin(angles))


def rotate_heads(values, cosine_table, sine_table):
    half_size = values.shape[-1] // 2
    turned = jnp.concatenate([-values[..., half_size:], values[..., :half_size]], -1)
    return values * cosine_table[:, None, :] + turned * sine_table[:, None, :]


def unrotate_heads(grads, cosine_table, sine_table):
    half_size = grads.shape[-1] // 2
    scaled = grads * sine_table[:, None, :]
    turned = jnp.concatenate([scaled[..., half_size:], -scaled[..., :half_size]], -1)
    return grads * cosine_table[:, None, :] + turned


def slot_table(expert_rows, expert_count, capacity):
    row_count, route_count = expert_rows.shape
    flat_ids = expert_rows.reshape(-1)
    matches = (flat_ids[:, None] == jnp.arange(expert_count, dtype=jnp.int32)[None, :]).astype(
        jnp.int32
    )
    earlier = jnp.cumsum(matches, 0) - matches
    slots = jnp.sum(earlier * matches, -1)
    cell_ids = flat_ids * capacity + slots
    owners = jnp.arange(row_count * route_count, dtype=jnp.int32) // route_count
    slot_owner = jnp.full((expert_count * capacity,), row_count, jnp.int32).at[cell_ids].set(owners)
    return (slot_owner, cell_ids)


def expert_front(inputs_rows, gate_full, up_full, down_full):
    gate_pre = jnp.einsum(
        "ecd,edf->ecf", inputs_rows, gate_full, preferred_element_type=jnp.float32
    )
    up_pre = jnp.einsum("ecd,edf->ecf", inputs_rows, up_full, preferred_element_type=jnp.float32)
    active = (gate_pre / (1.0 + jnp.exp(-gate_pre)) * up_pre).astype(jnp.bfloat16)
    produced = jnp.einsum("ecf,efd->ecd", active, down_full, preferred_element_type=jnp.float32)
    return (gate_pre, up_pre, active, produced)


def body(
    tokens,
    cotangent,
    dealing,
    lengths,
    routes,
    attention_gain,
    query_weight,
    key_weight,
    value_weight,
    output_weight,
    query_gain,
    key_gain,
    ffn_gain,
    router_weight,
    gate_weight,
    up_weight,
    down_weight,
):
    groups = lax.axis_size("dp")
    own_index = lax.axis_index("dp")
    rows_here, model_width = tokens.shape
    per_peer = rows_here // groups
    dealt_blocks = dealing.reshape(groups, rows_here)
    ranked = jnp.argsort(dealt_blocks // rows_here, axis=1, stable=True)
    chosen = lax.dynamic_slice_in_dim(ranked, own_index * per_peer, per_peer, 1)
    outgoing = (jnp.take_along_axis(dealt_blocks, chosen, 1) - own_index * rows_here).reshape(-1)
    own_order = lax.dynamic_index_in_dim(ranked, own_index, 0, keepdims=False)
    arrival = jnp.argsort(own_order)
    sent_rows = tokens[outgoing].reshape(groups, per_peer, model_width)
    sent_grads = cotangent[outgoing].reshape(groups, per_peer, model_width)
    got_rows, got_grads = (
        lax.all_to_all(sent_rows, "dp", split_axis=0, concat_axis=0, tiled=True),
        lax.all_to_all(sent_grads, "dp", split_axis=0, concat_axis=0, tiled=True),
    )
    rows_in = got_rows.reshape(rows_here, model_width)[arrival].astype(jnp.float32)
    out_grad = got_grads.reshape(rows_here, model_width)[arrival]
    out_grad_full = out_grad.astype(jnp.float32)
    fetched = (
        lax.all_gather(attention_gain.astype(jnp.bfloat16), "dp", axis=0, tiled=True),
        lax.all_gather(query_weight.astype(jnp.bfloat16), "dp", axis=0, tiled=True),
        lax.all_gather(key_weight.astype(jnp.bfloat16), "dp", axis=0, tiled=True),
        lax.all_gather(value_weight.astype(jnp.bfloat16), "dp", axis=0, tiled=True),
        lax.all_gather(output_weight.astype(jnp.bfloat16), "dp", axis=1, tiled=True),
        lax.all_gather(query_gain.astype(jnp.bfloat16), "dp", axis=1, tiled=True),
        lax.all_gather(key_gain.astype(jnp.bfloat16), "dp", axis=1, tiled=True),
        lax.all_gather(ffn_gain.astype(jnp.bfloat16), "dp", axis=0, tiled=True),
        lax.all_gather(router_weight.astype(jnp.bfloat16), "dp", axis=0, tiled=True),
    )
    first_gain = fetched[0].astype(jnp.float32)
    query_full, key_full, value_full, output_full = (fetched[1], fetched[2], fetched[3], fetched[4])
    query_scale_gain = fetched[5].reshape(-1).astype(jnp.float32)
    key_scale_gain = fetched[6].reshape(-1).astype(jnp.float32)
    second_gain = fetched[7].astype(jnp.float32)
    router_full = fetched[8]
    segment_ids, positions = segment_layout(lengths[0], rows_here)
    cosine_table, sine_table = rope_tables(positions.astype(jnp.float32), HEAD_DIM)
    places = jnp.arange(rows_here, dtype=jnp.int32)
    allowed = (segment_ids[:, None] == segment_ids[None, :]) & (places[None, :] <= places[:, None])
    head_scale = HEAD_DIM ** (-0.5)
    norm_one = row_scale(rows_in)
    normed_one = (rows_in * norm_one * first_gain).astype(jnp.bfloat16)
    query_raw = jnp.dot(normed_one, query_full, preferred_element_type=jnp.float32)
    key_raw = jnp.dot(normed_one, key_full, preferred_element_type=jnp.float32)
    value_rows = jnp.dot(normed_one, value_full, preferred_element_type=jnp.float32).astype(
        jnp.bfloat16
    )
    query_total, key_total = lax.psum(
        (jnp.sum(query_raw * query_raw, -1), jnp.sum(key_raw * key_raw, -1)), "tensor"
    )
    query_scale = lax.rsqrt(query_total / model_width + EPS)[:, None]
    key_scale = lax.rsqrt(key_total / model_width + EPS)[:, None]
    heads_here = query_raw.shape[1] // HEAD_DIM
    query_normed = query_raw * query_scale * query_scale_gain
    key_normed = key_raw * key_scale * key_scale_gain
    query_heads = rotate_heads(
        query_normed.reshape(rows_here, heads_here, HEAD_DIM), cosine_table, sine_table
    ).astype(jnp.bfloat16)
    key_heads = rotate_heads(
        key_normed.reshape(rows_here, heads_here, HEAD_DIM), cosine_table, sine_table
    ).astype(jnp.bfloat16)
    value_heads = value_rows.reshape(rows_here, heads_here, HEAD_DIM)

    def attention_scores(query_part, key_part):
        raw_scores = (
            jnp.einsum("qhd,khd->hqk", query_part, key_part, preferred_element_type=jnp.float32)
            * head_scale
        )
        return jnp.where(allowed[None], raw_scores, MASKED)

    masked_scores = attention_scores(query_heads, key_heads)
    peak_value = jnp.max(masked_scores, -1, keepdims=True)
    powered = jnp.exp(masked_scores - peak_value)
    total_weight = jnp.sum(powered, -1, keepdims=True)
    probs = powered / total_weight
    log_total = peak_value + jnp.log(total_weight)
    context = jnp.einsum(
        "hqk,khd->qhd", probs.astype(jnp.bfloat16), value_heads, preferred_element_type=jnp.float32
    )
    context = context.reshape(rows_here, -1).astype(jnp.bfloat16)
    attention = lax.psum(
        jnp.dot(context, output_full, preferred_element_type=jnp.float32), "tensor"
    )
    hidden = rows_in + attention
    norm_two = row_scale(hidden)
    normed_two = (hidden * norm_two * second_gain).astype(jnp.bfloat16)
    logits = jnp.dot(normed_two, router_full, preferred_element_type=jnp.float32)
    router_probs = softmax_rows(logits)
    gate_values = jnp.take_along_axis(router_probs, routes, 1)
    slot_owner, cell_ids = slot_table(routes, EXPERTS, CAP)
    padded_rows = jnp.concatenate([normed_two, jnp.zeros((1, model_width), jnp.bfloat16)], 0)
    dispatched = padded_rows[slot_owner].reshape(EXPERTS, CAP, model_width)
    padded_grad = jnp.concatenate([out_grad, jnp.zeros((1, model_width), jnp.bfloat16)], 0)
    grad_cells = padded_grad[slot_owner].reshape(EXPERTS, CAP, model_width)
    gate_cells = (
        jnp.zeros((EXPERTS * CAP,), jnp.float32)
        .at[cell_ids]
        .set(gate_values.reshape(-1))
        .reshape(EXPERTS, CAP)
    )
    empty_rows = jnp.zeros((rows_here + 1, model_width), jnp.float32)
    group_size = 4
    group_count = EXPERTS // group_size
    owner_groups = slot_owner.reshape(group_count, group_size * CAP)
    gate_stack = gate_weight.astype(jnp.bfloat16).reshape(
        group_count, group_size, gate_weight.shape[1], gate_weight.shape[2]
    )
    up_stack = up_weight.astype(jnp.bfloat16).reshape(
        group_count, group_size, up_weight.shape[1], up_weight.shape[2]
    )
    down_stack = down_weight.astype(jnp.bfloat16).reshape(
        group_count, group_size, down_weight.shape[1], down_weight.shape[2]
    )
    group_inputs = (
        gate_stack,
        up_stack,
        down_stack,
        dispatched.reshape(group_count, group_size, CAP, model_width),
        gate_cells.reshape(group_count, group_size, CAP),
        grad_cells.reshape(group_count, group_size, CAP, model_width),
        owner_groups,
    )

    def gather_experts(gate_part, up_part, down_part):
        return (
            lax.all_gather(gate_part, "dp", axis=1, tiled=True),
            lax.all_gather(up_part, "dp", axis=1, tiled=True),
            lax.all_gather(down_part, "dp", axis=2, tiled=True),
        )

    def expert_back(
        inputs_rows,
        weights_cells,
        grad_rows,
        gate_full,
        up_full,
        down_full,
        gate_pre,
        up_pre,
        active,
    ):
        out_cells = (grad_rows.astype(jnp.float32) * weights_cells[..., None]).astype(jnp.bfloat16)
        active_grad = jnp.einsum(
            "ecd,efd->ecf", out_cells, down_full, preferred_element_type=jnp.float32
        )
        sigmoid_gate = 1.0 / (1.0 + jnp.exp(-gate_pre))
        gate_grad = (
            active_grad * up_pre * sigmoid_gate * (1.0 + gate_pre * (1.0 - sigmoid_gate))
        ).astype(jnp.bfloat16)
        up_grad = (active_grad * gate_pre * sigmoid_gate).astype(jnp.bfloat16)
        down_wgrad = jnp.einsum(
            "ecf,ecd->efd", active, out_cells, preferred_element_type=jnp.float32
        )
        gate_wgrad = jnp.einsum(
            "ecd,ecf->edf", inputs_rows, gate_grad, preferred_element_type=jnp.float32
        )
        up_wgrad = jnp.einsum(
            "ecd,ecf->edf", inputs_rows, up_grad, preferred_element_type=jnp.float32
        )
        input_grad = jnp.einsum(
            "ecf,edf->ecd", gate_grad, gate_full, preferred_element_type=jnp.float32
        )
        input_grad = input_grad + jnp.einsum(
            "ecf,edf->ecd", up_grad, up_full, preferred_element_type=jnp.float32
        )
        shard_grads = (
            lax.psum_scatter(gate_wgrad, "dp", scatter_dimension=1, tiled=True),
            lax.psum_scatter(up_wgrad, "dp", scatter_dimension=1, tiled=True),
            lax.psum_scatter(down_wgrad, "dp", scatter_dimension=2, tiled=True),
        )
        return (input_grad, shard_grads)

    def mixing_of(produced, grad_rows):
        return jnp.einsum("ecd,ecd->ec", produced, grad_rows.astype(jnp.float32))

    def forward_group(moe_sum, pieces):
        gate_part, up_part, down_part, inputs_rows, weights_cells, grad_rows, owners = pieces
        gate_full, up_full, down_full = gather_experts(gate_part, up_part, down_part)
        gate_pre, up_pre, active, produced = expert_front(
            inputs_rows, gate_full, up_full, down_full
        )
        moe_sum = moe_sum.at[owners].add(
            (produced * weights_cells[..., None]).reshape(-1, model_width)
        )
        return (moe_sum, None)

    moe_sum, unused = lax.scan(forward_group, empty_rows, group_inputs)

    def backward_group(row_grads, pieces):
        gate_part, up_part, down_part, inputs_rows, weights_cells, grad_rows, owners = pieces
        gate_full, up_full, down_full = gather_experts(gate_part, up_part, down_part)
        gate_pre, up_pre, active, produced = expert_front(
            inputs_rows, gate_full, up_full, down_full
        )
        mixing_grad = mixing_of(produced, grad_rows)
        input_grad, shard_grads = expert_back(
            inputs_rows,
            weights_cells,
            grad_rows,
            gate_full,
            up_full,
            down_full,
            gate_pre,
            up_pre,
            active,
        )
        row_grads = row_grads.at[owners].add(input_grad.reshape(-1, model_width))
        return (row_grads, (mixing_grad, shard_grads))

    row_grads, (mixing_grad, shard_grads) = lax.scan(backward_group, empty_rows, group_inputs)
    mixing_flat = mixing_grad.reshape(-1)
    gate_weight_grad = shard_grads[0].reshape(gate_weight.shape)
    up_weight_grad = shard_grads[1].reshape(up_weight.shape)
    down_weight_grad = shard_grads[2].reshape(down_weight.shape)
    mixture = lax.psum(moe_sum[:rows_here].astype(jnp.bfloat16), "tensor").astype(jnp.float32)
    out_rows = (hidden + mixture).astype(jnp.bfloat16)
    mixing_tokens = mixing_flat[cell_ids].reshape(rows_here, -1)
    expert_rows_grad, mixing_tokens = lax.psum((row_grads[:rows_here], mixing_tokens), "tensor")
    expert_ids = jnp.arange(EXPERTS, dtype=jnp.int32)
    route_match = (routes[:, :, None] == expert_ids[None, None, :]).astype(jnp.float32)
    prob_grad = jnp.sum(route_match * mixing_tokens[:, :, None], 1)
    logit_grad = (
        router_probs * (prob_grad - jnp.sum(router_probs * prob_grad, -1, keepdims=True))
    ).astype(jnp.bfloat16)
    router_wgrad = inner_rows(normed_two, logit_grad)
    normed_two_grad = expert_rows_grad + outer_cols(logit_grad, router_full)
    ffn_gain_grad = jnp.sum(normed_two_grad * hidden * norm_two, 0)
    scaled_two = normed_two_grad * second_gain
    hidden_grad = out_grad_full + norm_two * (
        scaled_two - hidden * norm_two * norm_two * jnp.mean(scaled_two * hidden, -1, keepdims=True)
    )
    attn_grad = hidden_grad.astype(jnp.bfloat16)
    output_wgrad = inner_rows(context, attn_grad)
    context_grad = (
        outer_cols(attn_grad, output_full)
        .astype(jnp.bfloat16)
        .reshape(rows_here, heads_here, HEAD_DIM)
    )
    recomputed = jnp.exp(attention_scores(query_heads, key_heads) - log_total)
    prob_pair_grad = jnp.einsum(
        "qhd,khd->hqk", context_grad, value_heads, preferred_element_type=jnp.float32
    )
    value_grad = jnp.einsum(
        "hqk,qhd->khd",
        recomputed.astype(jnp.bfloat16),
        context_grad,
        preferred_element_type=jnp.float32,
    )
    value_grad = value_grad.reshape(rows_here, -1).astype(jnp.bfloat16)
    score_grad = (
        recomputed * (prob_pair_grad - jnp.sum(recomputed * prob_pair_grad, -1, keepdims=True))
    ).astype(jnp.bfloat16)
    query_rot_grad = (
        jnp.einsum("hqk,khd->qhd", score_grad, key_heads, preferred_element_type=jnp.float32)
        * head_scale
    )
    key_rot_grad = (
        jnp.einsum("hqk,qhd->khd", score_grad, query_heads, preferred_element_type=jnp.float32)
        * head_scale
    )
    query_norm_grad = unrotate_heads(query_rot_grad, cosine_table, sine_table).reshape(
        rows_here, -1
    )
    key_norm_grad = unrotate_heads(key_rot_grad, cosine_table, sine_table).reshape(rows_here, -1)
    query_inner, key_inner = lax.psum(
        (
            jnp.sum(query_norm_grad * query_scale_gain * query_raw, -1),
            jnp.sum(key_norm_grad * key_scale_gain * key_raw, -1),
        ),
        "tensor",
    )
    query_gain_grad = jnp.sum(query_norm_grad * query_raw * query_scale, 0)
    key_gain_grad = jnp.sum(key_norm_grad * key_raw * key_scale, 0)
    query_raw_grad = (
        query_scale * query_scale_gain * query_norm_grad
        - query_raw * query_scale**3 * query_inner[:, None] / model_width
    ).astype(jnp.bfloat16)
    key_raw_grad = (
        key_scale * key_scale_gain * key_norm_grad
        - key_raw * key_scale**3 * key_inner[:, None] / model_width
    ).astype(jnp.bfloat16)
    query_wgrad = inner_rows(normed_one, query_raw_grad)
    key_wgrad = inner_rows(normed_one, key_raw_grad)
    value_wgrad = inner_rows(normed_one, value_grad)
    normed_one_grad = (
        outer_cols(query_raw_grad, query_full)
        + outer_cols(key_raw_grad, key_full)
        + outer_cols(value_grad, value_full)
    )
    normed_one_grad = lax.psum(normed_one_grad.astype(jnp.bfloat16), "tensor").astype(jnp.float32)
    attention_gain_grad = jnp.sum(normed_one_grad * rows_in * norm_one, 0)
    scaled_one = normed_one_grad * first_gain
    rows_grad = hidden_grad + norm_one * (
        scaled_one
        - rows_in * norm_one * norm_one * jnp.mean(scaled_one * rows_in, -1, keepdims=True)
    )
    summed = (
        lax.psum_scatter(attention_gain_grad, "dp", scatter_dimension=0, tiled=True),
        lax.psum_scatter(query_wgrad, "dp", scatter_dimension=0, tiled=True),
        lax.psum_scatter(key_wgrad, "dp", scatter_dimension=0, tiled=True),
        lax.psum_scatter(value_wgrad, "dp", scatter_dimension=0, tiled=True),
        lax.psum_scatter(output_wgrad, "dp", scatter_dimension=1, tiled=True),
        lax.psum_scatter(query_gain_grad[None], "dp", scatter_dimension=1, tiled=True),
        lax.psum_scatter(key_gain_grad[None], "dp", scatter_dimension=1, tiled=True),
        lax.psum_scatter(ffn_gain_grad, "dp", scatter_dimension=0, tiled=True),
        lax.psum_scatter(router_wgrad, "dp", scatter_dimension=0, tiled=True),
    )
    back_rows = out_rows[own_order].reshape(groups, per_peer, model_width)
    back_grads = rows_grad.astype(jnp.bfloat16)[own_order].reshape(groups, per_peer, model_width)
    got_out, got_grad = (
        lax.all_to_all(back_rows, "dp", split_axis=0, concat_axis=0, tiled=True),
        lax.all_to_all(back_grads, "dp", split_axis=0, concat_axis=0, tiled=True),
    )
    restore = jnp.argsort(outgoing)
    block_out = got_out.reshape(rows_here, model_width)[restore]
    token_grad = got_grad.reshape(rows_here, model_width)[restore]
    return (
        block_out,
        token_grad,
        summed[0],
        summed[1],
        summed[2],
        summed[3],
        summed[4],
        summed[5],
        summed[6],
        summed[7],
        summed[8],
        gate_weight_grad,
        up_weight_grad,
        down_weight_grad,
    )


def solution(mesh):
    return jax.shard_map(
        body,
        mesh=mesh,
        in_specs=(
            P("dp", None),
            P("dp", None),
            P(),
            P("dp", None),
            P("dp", None),
            P("dp"),
            P("dp", "tensor"),
            P("dp", "tensor"),
            P("dp", "tensor"),
            P("tensor", "dp"),
            P("tensor", "dp"),
            P("tensor", "dp"),
            P("dp"),
            P("dp", None),
            P(None, "dp", "tensor"),
            P(None, "dp", "tensor"),
            P(None, "tensor", "dp"),
        ),
        out_specs=(
            P("dp", None),
            P("dp", None),
            P("dp"),
            P("dp", "tensor"),
            P("dp", "tensor"),
            P("dp", "tensor"),
            P("tensor", "dp"),
            P("tensor", "dp"),
            P("tensor", "dp"),
            P("dp"),
            P("dp", None),
            P(None, "dp", "tensor"),
            P(None, "dp", "tensor"),
            P(None, "tensor", "dp"),
        ),
        check_vma=False,
    )
```

profile of v0, /device:TPU:17, one launch (start us, length us, event | category | flops | bytes accessed | tf_op | source)
XLA Modules:
  0.0 5295.9 jit_solution(18342522129769676956)
XLA Ops:
  354.5 3181.3 %while.29 = (s32[]{:T(128)}, f32[257,2048]{1,0:T(8,128)S(1)}, f32[4,4,160]{2,1,0:T(4,128)S(1)}, f32[4,4,128,512]{3,2,1,0:T(8,128)}, f32[4,4,128,512]{3,2,1,0:T(8...) while((s32[]{:T(128)}, f32[257,2048]{1,0:T(8,128)S(1)}, ...), condition=%wide.region_31.32_spmd, body=%wide.region_26.31_spmd.sunk | while | flops 12099258368 | bytes 419590720 | solution.py:322
  360.7 74.4 %all-gather.45.cloned.1.call-done = bf16[1,4,2048,512]{3,2,1,0:T(8,128)(2,1)} async-done(((bf16[1,4,128,512]{3,2,1,0:T(8,128)(2,1)}), bf16[1,4,2048,512]{3,2,1,0:T(8,128)(2,1)}) %all-gather.45.cloned.1.call-update) | async-done | bytes 8388624 | tf_op jit(solution)/shard_map/while/body/eval_jaxpr/all_gather | solution.py:238
  441.9 72.1 %all-gather.47.cloned.1.call-done = bf16[1,4,512,2048]{3,2,1,0:T(8,128)(2,1)} async-done(((bf16[1,4,512,128]{3,2,1,0:T(8,128)(2,1)}), bf16[1,4,512,2048]{3,2,1,0:T(8,128)(2,1)}) %all-gather.47.cloned.1.call-update) | async-done | bytes 8388624 | tf_op jit(solution)/shard_map/while/body/eval_jaxpr/all_gather | solution.py:240
  670.9 113.0 %reduce-scatter.31.cloned.1.call-done = f32[4,128,512]{2,1,0:T(8,128)} async-done(((f32[4,2048,512]{2,1,0:T(8,128)}), f32[4,128,512]{2,1,0:T(8,128)}) %reduce-scatter.31.cloned.1.call-update) | async-done | bytes 1048592 | tf_op jit(solution)/shard_map/while/body/eval_jaxpr/reduce_scatter | solution.py:280
  786.2 179.4 %reduce-scatter.29.cloned.1.call-done = f32[4,128,512]{2,1,0:T(8,128)} async-done(((f32[4,2048,512]{2,1,0:T(8,128)}), f32[4,128,512]{2,1,0:T(8,128)}) %reduce-scatter.29.cloned.1.call-update) | async-done | bytes 1048592 | tf_op jit(solution)/shard_map/while/body/eval_jaxpr/reduce_scatter | solution.py:279
  967.9 179.5 %reduce-scatter.33.cloned.1.call-done = f32[4,512,128]{2,1,0:T(8,128)} async-done(((f32[4,512,2048]{2,1,0:T(8,128)}), f32[4,512,128]{2,1,0:T(8,128)}) %reduce-scatter.33.cloned.1.call-update) | async-done | bytes 1048592 | tf_op jit(solution)/shard_map/while/body/eval_jaxpr/reduce_scatter | solution.py:281
  1155.5 72.3 %all-gather.45.cloned.1.call-done = bf16[1,4,2048,512]{3,2,1,0:T(8,128)(2,1)} async-done(((bf16[1,4,128,512]{3,2,1,0:T(8,128)(2,1)}), bf16[1,4,2048,512]{3,2,1,0:T(8,128)(2,1)}) %all-gather.45.cloned.1.call-update) | async-done | bytes 8388624 | tf_op jit(solution)/shard_map/while/body/eval_jaxpr/all_gather | solution.py:238
  1463.8 112.9 %reduce-scatter.31.cloned.1.call-done = f32[4,128,512]{2,1,0:T(8,128)} async-done(((f32[4,2048,512]{2,1,0:T(8,128)}), f32[4,128,512]{2,1,0:T(8,128)}) %reduce-scatter.31.cloned.1.call-update) | async-done | bytes 1048592 | tf_op jit(solution)/shard_map/while/body/eval_jaxpr/reduce_scatter | solution.py:280
  1579.0 179.4 %reduce-scatter.29.cloned.1.call-done = f32[4,128,512]{2,1,0:T(8,128)} async-done(((f32[4,2048,512]{2,1,0:T(8,128)}), f32[4,128,512]{2,1,0:T(8,128)}) %reduce-scatter.29.cloned.1.call-update) | async-done | bytes 1048592 | tf_op jit(solution)/shard_map/while/body/eval_jaxpr/reduce_scatter | solution.py:279
  1760.7 179.3 %reduce-scatter.33.cloned.1.call-done = f32[4,512,128]{2,1,0:T(8,128)} async-done(((f32[4,512,2048]{2,1,0:T(8,128)}), f32[4,512,128]{2,1,0:T(8,128)}) %reduce-scatter.33.cloned.1.call-update) | async-done | bytes 1048592 | tf_op jit(solution)/shard_map/while/body/eval_jaxpr/reduce_scatter | solution.py:281
  2027.0 72.1 %all-gather.47.cloned.1.call-done = bf16[1,4,512,2048]{3,2,1,0:T(8,128)(2,1)} async-done(((bf16[1,4,512,128]{3,2,1,0:T(8,128)(2,1)}), bf16[1,4,512,2048]{3,2,1,0:T(8,128)(2,1)}) %all-gather.47.cloned.1.call-update) | async-done | bytes 8388624 | tf_op jit(solution)/shard_map/while/body/eval_jaxpr/all_gather | solution.py:240
  2256.0 113.0 %reduce-scatter.31.cloned.1.call-done = f32[4,128,512]{2,1,0:T(8,128)} async-done(((f32[4,2048,512]{2,1,0:T(8,128)}), f32[4,128,512]{2,1,0:T(8,128)}) %reduce-scatter.31.cloned.1.call-update) | async-done | bytes 1048592 | tf_op jit(solution)/shard_map/while/body/eval_jaxpr/reduce_scatter | solution.py:280
  2371.3 179.5 %reduce-scatter.29.cloned.1.call-done = f32[4,128,512]{2,1,0:T(8,128)} async-done(((f32[4,2048,512]{2,1,0:T(8,128)}), f32[4,128,512]{2,1,0:T(8,128)}) %reduce-scatter.29.cloned.1.call-update) | async-done | bytes 1048592 | tf_op jit(solution)/shard_map/while/body/eval_jaxpr/reduce_scatter | solution.py:279
  2553.1 179.3 %reduce-scatter.33.cloned.1.call-done = f32[4,512,128]{2,1,0:T(8,128)} async-done(((f32[4,512,2048]{2,1,0:T(8,128)}), f32[4,512,128]{2,1,0:T(8,128)}) %reduce-scatter.33.cloned.1.call-update) | async-done | bytes 1048592 | tf_op jit(solution)/shard_map/while/body/eval_jaxpr/reduce_scatter | solution.py:281
  2740.6 72.3 %all-gather.45.cloned.1.call-done = bf16[1,4,2048,512]{3,2,1,0:T(8,128)(2,1)} async-done(((bf16[1,4,128,512]{3,2,1,0:T(8,128)(2,1)}), bf16[1,4,2048,512]{3,2,1,0:T(8,128)(2,1)}) %all-gather.45.cloned.1.call-update) | async-done | bytes 8388624 | tf_op jit(solution)/shard_map/while/body/eval_jaxpr/all_gather | solution.py:238
  2819.7 72.3 %all-gather.47.cloned.1.call-done = bf16[1,4,512,2048]{3,2,1,0:T(8,128)(2,1)} async-done(((bf16[1,4,512,128]{3,2,1,0:T(8,128)(2,1)}), bf16[1,4,512,2048]{3,2,1,0:T(8,128)(2,1)}) %all-gather.47.cloned.1.call-update) | async-done | bytes 8388624 | tf_op jit(solution)/shard_map/while/body/eval_jaxpr/all_gather | solution.py:240
  3049.1 113.0 %reduce-scatter.31.cloned.1.call-done = f32[4,128,512]{2,1,0:T(8,128)} async-done(((f32[4,2048,512]{2,1,0:T(8,128)}), f32[4,128,512]{2,1,0:T(8,128)}) %reduce-scatter.31.cloned.1.call-update) | async-done | bytes 1048592 | tf_op jit(solution)/shard_map/while/body/eval_jaxpr/reduce_scatter | solution.py:280
  3164.3 179.5 %reduce-scatter.29.cloned.1.call-done = f32[4,128,512]{2,1,0:T(8,128)} async-done(((f32[4,2048,512]{2,1,0:T(8,128)}), f32[4,128,512]{2,1,0:T(8,128)}) %reduce-scatter.29.cloned.1.call-update) | async-done | bytes 1048592 | tf_op jit(solution)/shard_map/while/body/eval_jaxpr/reduce_scatter | solution.py:279
  3346.0 179.3 %reduce-scatter.33.cloned.1.call-done = f32[4,512,128]{2,1,0:T(8,128)} async-done(((f32[4,512,2048]{2,1,0:T(8,128)}), f32[4,512,128]{2,1,0:T(8,128)}) %reduce-scatter.33.cloned.1.call-update) | async-done | bytes 1048592 | tf_op jit(solution)/shard_map/while/body/eval_jaxpr/reduce_scatter | solution.py:281
  3537.6 1036.1 %while.28 = (s32[]{:T(128)}, f32[257,2048]{1,0:T(8,128)S(1)}, s32[4,640]{1,0:T(4,128)S(1)}, bf16[4,4,160,2048]{3,2,1,0:T(8,128)(2,1)}, bf16[4,4,128,512]{3,2,1,0...) while((s32[]{:T(128)}, f32[257,2048]{1,0:T(8,128)S(1)}, ...), condition=%wide.region_23.24_spmd, body=%wide.region_21.23_spmd.sunk | while | flops 4030793728 | bytes 137379056 | solution.py:299
  3621.7 72.3 %all-gather.39.cloned.1.call-done = bf16[1,4,512,2048]{3,2,1,0:T(8,128)(2,1)} async-done(((bf16[1,4,512,128]{3,2,1,0:T(8,128)(2,1)}), bf16[1,4,512,2048]{3,2,1,0:T(8,128)(2,1)}) %all-gather.39.cloned.1.call-update) | async-done | bytes 8388624 | tf_op jit(solution)/shard_map/while/body/eval_jaxpr/all_gather | solution.py:240
  3694.0 76.0 %all-gather.41.cloned.1.call-done = bf16[1,4,2048,512]{3,2,1,0:T(8,128)(2,1)} async-done(((bf16[1,4,128,512]{3,2,1,0:T(8,128)(2,1)}), bf16[1,4,2048,512]{3,2,1,0:T(8,128)(2,1)}) %all-gather.41.cloned.1.call-update) | async-done | bytes 8388624 | tf_op jit(solution)/shard_map/while/body/eval_jaxpr/all_gather | solution.py:239
  3880.4 72.3 %all-gather.39.cloned.1.call-done = bf16[1,4,512,2048]{3,2,1,0:T(8,128)(2,1)} async-done(((bf16[1,4,512,128]{3,2,1,0:T(8,128)(2,1)}), bf16[1,4,512,2048]{3,2,1,0:T(8,128)(2,1)}) %all-gather.39.cloned.1.call-update) | async-done | bytes 8388624 | tf_op jit(solution)/shard_map/while/body/eval_jaxpr/all_gather | solution.py:240
  3952.7 76.0 %all-gather.41.cloned.1.call-done = bf16[1,4,2048,512]{3,2,1,0:T(8,128)(2,1)} async-done(((bf16[1,4,128,512]{3,2,1,0:T(8,128)(2,1)}), bf16[1,4,2048,512]{3,2,1,0:T(8,128)(2,1)}) %all-gather.41.cloned.1.call-update) | async-done | bytes 8388624 | tf_op jit(solution)/shard_map/while/body/eval_jaxpr/all_gather | solution.py:239
  4139.1 72.3 %all-gather.39.cloned.1.call-done = bf16[1,4,512,2048]{3,2,1,0:T(8,128)(2,1)} async-done(((bf16[1,4,512,128]{3,2,1,0:T(8,128)(2,1)}), bf16[1,4,512,2048]{3,2,1,0:T(8,128)(2,1)}) %all-gather.39.cloned.1.call-update) | async-done | bytes 8388624 | tf_op jit(solution)/shard_map/while/body/eval_jaxpr/all_gather | solution.py:240
  4211.4 76.0 %all-gather.41.cloned.1.call-done = bf16[1,4,2048,512]{3,2,1,0:T(8,128)(2,1)} async-done(((bf16[1,4,128,512]{3,2,1,0:T(8,128)(2,1)}), bf16[1,4,2048,512]{3,2,1,0:T(8,128)(2,1)}) %all-gather.41.cloned.1.call-update) | async-done | bytes 8388624 | tf_op jit(solution)/shard_map/while/body/eval_jaxpr/all_gather | solution.py:239
  4397.8 72.1 %all-gather.39.cloned.1.call-done = bf16[1,4,512,2048]{3,2,1,0:T(8,128)(2,1)} async-done(((bf16[1,4,512,128]{3,2,1,0:T(8,128)(2,1)}), bf16[1,4,512,2048]{3,2,1,0:T(8,128)(2,1)}) %all-gather.39.cloned.1.call-update) | async-done | bytes 8388624 | tf_op jit(solution)/shard_map/while/body/eval_jaxpr/all_gather | solution.py:240
  4470.0 76.0 %all-gather.41.cloned.1.call-done = bf16[1,4,2048,512]{3,2,1,0:T(8,128)(2,1)} async-done(((bf16[1,4,128,512]{3,2,1,0:T(8,128)(2,1)}), bf16[1,4,2048,512]{3,2,1,0:T(8,128)(2,1)}) %all-gather.41.cloned.1.call-update) | async-done | bytes 8388624 | tf_op jit(solution)/shard_map/while/body/eval_jaxpr/all_gather | solution.py:239
  4855.7 109.6 %reduce-scatter.21.cloned.1.call-done = f32[1024,128]{1,0:T(8,128)} async-done(((f32[1024,2048]{1,0:T(8,128)}), f32[1024,128]{1,0:T(8,128)}) %reduce-scatter.21.cloned.1.call-update) | async-done | bytes 524304 | tf_op jit(solution)/shard_map/reduce_scatter | solution.py:414
  4965.3 107.5 %reduce-scatter.19.cloned.1.call-done = f32[128,1024]{1,0:T(8,128)} async-done(((f32[2048,1024]{1,0:T(8,128)}), f32[128,1024]{1,0:T(8,128)}) %reduce-scatter.19.cloned.1.call-update) | async-done | bytes 524304 | tf_op jit(solution)/shard_map/reduce_scatter | solution.py:413
  5072.7 107.6 %reduce-scatter.17.cloned.1.call-done = f32[128,1024]{1,0:T(8,128)} async-done(((f32[2048,1024]{1,0:T(8,128)}), f32[128,1024]{1,0:T(8,128)}) %reduce-scatter.17.cloned.1.call-update) | async-done | bytes 524304 | tf_op jit(solution)/shard_map/reduce_scatter | solution.py:412
  5180.4 107.5 %reduce-scatter.15.cloned.1.call-done = f32[128,1024]{1,0:T(8,128)} async-done(((f32[2048,1024]{1,0:T(8,128)}), f32[128,1024]{1,0:T(8,128)}) %reduce-scatter.15.cloned.1.call-update) | async-done | bytes 524304 | tf_op jit(solution)/shard_map/reduce_scatter | solution.py:411
  (625 shorter events, 1919.9 us)
Async XLA Ops:
  14.0 161.3 %all-gather.31.cloned.1.call-start = ((), (), s32[]{:S(2)}) async-start(), calls=%async_computation.14 | async-start | bytes 4456448 | tf_op jit(solution)/shard_map/all_gather | solution.py:135
  14.8 214.1 %all-gather.37.cloned.1.call-start = ((), (), s32[]{:S(2)}) async-start(), calls=%async_computation.17 | async-start | bytes 4456448 | tf_op jit(solution)/shard_map/all_gather | solution.py:136
  61.8 252.3 %all-reduce.15.cloned.1.call-start = ((), (), s32[]{:S(2)}) async-start(), calls=%async_computation.18 | async-start | bytes 4194304 | tf_op jit(solution)/shard_map/psum | solution.py:193
  356.7 157.3 %all-gather.47.cloned.1.call-start = ((), (), s32[]{:S(2)}) async-start(), calls=%async_computation.32 | async-start | bytes 8912896 | tf_op jit(solution)/shard_map/while/body/eval_jaxpr/all_gather | solution.py:240
  358.6 230.5 %all-gather.49.cloned.1.call-start = ((), (), s32[]{:S(2)}) async-start(), calls=%async_computation.33 | async-start | bytes 8912896 | tf_op jit(solution)/shard_map/while/body/eval_jaxpr/all_gather | solution.py:239
  360.6 423.3 %reduce-scatter.31.cloned.1.call-start = ((), (), s32[]{:S(2)}) async-start(), calls=%async_computation.35 | async-start | bytes 17825792 | tf_op jit(solution)/shard_map/while/body/eval_jaxpr/reduce_scatter | solution.py:280
  607.6 358.0 %reduce-scatter.29.cloned.1.call-start = ((), (), s32[]{:S(2)}) async-start(), calls=%async_computation.34 | async-start | bytes 17825792 | tf_op jit(solution)/shard_map/while/body/eval_jaxpr/reduce_scatter | solution.py:279
  620.5 526.9 %reduce-scatter.33.cloned.1.call-start = ((), (), s32[]{:S(2)}) async-start(), calls=%async_computation.36 | async-start | bytes 17825792 | tf_op jit(solution)/shard_map/while/body/eval_jaxpr/reduce_scatter | solution.py:281
  1151.5 155.2 %all-gather.47.cloned.1.call-start = ((), (), s32[]{:S(2)}) async-start(), calls=%async_computation.32 | async-start | bytes 8912896 | tf_op jit(solution)/shard_map/while/body/eval_jaxpr/all_gather | solution.py:240
  1153.4 228.6 %all-gather.49.cloned.1.call-start = ((), (), s32[]{:S(2)}) async-start(), calls=%async_computation.33 | async-start | bytes 8912896 | tf_op jit(solution)/shard_map/while/body/eval_jaxpr/all_gather | solution.py:239
  1155.4 421.3 %reduce-scatter.31.cloned.1.call-start = ((), (), s32[]{:S(2)}) async-start(), calls=%async_computation.35 | async-start | bytes 17825792 | tf_op jit(solution)/shard_map/while/body/eval_jaxpr/reduce_scatter | solution.py:280
  1400.5 358.0 %reduce-scatter.29.cloned.1.call-start = ((), (), s32[]{:S(2)}) async-start(), calls=%async_computation.34 | async-start | bytes 17825792 | tf_op jit(solution)/shard_map/while/body/eval_jaxpr/reduce_scatter | solution.py:279
  1413.3 526.7 %reduce-scatter.33.cloned.1.call-start = ((), (), s32[]{:S(2)}) async-start(), calls=%async_computation.36 | async-start | bytes 17825792 | tf_op jit(solution)/shard_map/while/body/eval_jaxpr/reduce_scatter | solution.py:281
  1946.1 228.2 %all-gather.49.cloned.1.call-start = ((), (), s32[]{:S(2)}) async-start(), calls=%async_computation.33 | async-start | bytes 8912896 | tf_op jit(solution)/shard_map/while/body/eval_jaxpr/all_gather | solution.py:239
  1948.1 421.0 %reduce-scatter.31.cloned.1.call-start = ((), (), s32[]{:S(2)}) async-start(), calls=%async_computation.35 | async-start | bytes 17825792 | tf_op jit(solution)/shard_map/while/body/eval_jaxpr/reduce_scatter | solution.py:280
  2192.7 358.1 %reduce-scatter.29.cloned.1.call-start = ((), (), s32[]{:S(2)}) async-start(), calls=%async_computation.34 | async-start | bytes 17825792 | tf_op jit(solution)/shard_map/while/body/eval_jaxpr/reduce_scatter | solution.py:279
  2205.6 526.8 %reduce-scatter.33.cloned.1.call-start = ((), (), s32[]{:S(2)}) async-start(), calls=%async_computation.36 | async-start | bytes 17825792 | tf_op jit(solution)/shard_map/while/body/eval_jaxpr/reduce_scatter | solution.py:281
  2736.6 155.3 %all-gather.47.cloned.1.call-start = ((), (), s32[]{:S(2)}) async-start(), calls=%async_computation.32 | async-start | bytes 8912896 | tf_op jit(solution)/shard_map/while/body/eval_jaxpr/all_gather | solution.py:240
  2738.6 228.8 %all-gather.49.cloned.1.call-start = ((), (), s32[]{:S(2)}) async-start(), calls=%async_computation.33 | async-start | bytes 8912896 | tf_op jit(solution)/shard_map/while/body/eval_jaxpr/all_gather | solution.py:239
  2740.5 421.5 %reduce-scatter.31.cloned.1.call-start = ((), (), s32[]{:S(2)}) async-start(), calls=%async_computation.35 | async-start | bytes 17825792 | tf_op jit(solution)/shard_map/while/body/eval_jaxpr/reduce_scatter | solution.py:280
  2985.7 358.0 %reduce-scatter.29.cloned.1.call-start = ((), (), s32[]{:S(2)}) async-start(), calls=%async_computation.34 | async-start | bytes 17825792 | tf_op jit(solution)/shard_map/while/body/eval_jaxpr/reduce_scatter | solution.py:279
  2998.6 526.7 %reduce-scatter.33.cloned.1.call-start = ((), (), s32[]{:S(2)}) async-start(), calls=%async_computation.36 | async-start | bytes 17825792 | tf_op jit(solution)/shard_map/while/body/eval_jaxpr/reduce_scatter | solution.py:281
  3541.5 228.4 %all-gather.41.cloned.1.call-start = ((), (), s32[]{:S(2)}) async-start(), calls=%async_computation.29 | async-start | bytes 8912896 | tf_op jit(solution)/shard_map/while/body/eval_jaxpr/all_gather | solution.py:239
  3801.7 227.0 %all-gather.41.cloned.1.call-start = ((), (), s32[]{:S(2)}) async-start(), calls=%async_computation.29 | async-start | bytes 8912896 | tf_op jit(solution)/shard_map/while/body/eval_jaxpr/all_gather | solution.py:239
  4060.4 227.0 %all-gather.41.cloned.1.call-start = ((), (), s32[]{:S(2)}) async-start(), calls=%async_computation.29 | async-start | bytes 8912896 | tf_op jit(solution)/shard_map/while/body/eval_jaxpr/all_gather | solution.py:239
  4319.1 226.8 %all-gather.41.cloned.1.call-start = ((), (), s32[]{:S(2)}) async-start(), calls=%async_computation.29 | async-start | bytes 8912896 | tf_op jit(solution)/shard_map/while/body/eval_jaxpr/all_gather | solution.py:239
  4574.3 165.2 %all-reduce.19.cloned.1.call-start = ((), (), s32[]{:S(2)}) async-start(), calls=%async_computation.27 | async-start | bytes 4194304 | tf_op jit(solution)/shard_map/psum | solution.py:327
  4677.4 178.2 %reduce-scatter.23.cloned.1.call-start = ((), (), s32[]{:S(2)}) async-start(), calls=%async_computation.24 | async-start | bytes 139264 | tf_op jit(solution)/shard_map/reduce_scatter | solution.py:418
  4678.7 286.6 %reduce-scatter.21.cloned.1.call-start = ((), (), s32[]{:S(2)}) async-start(), calls=%async_computation.23 | async-start | bytes 8912896 | tf_op jit(solution)/shard_map/reduce_scatter | solution.py:414
  4684.6 388.2 %reduce-scatter.19.cloned.1.call-start = ((), (), s32[]{:S(2)}) async-start(), calls=%async_computation.22 | async-start | bytes 8912896 | tf_op jit(solution)/shard_map/reduce_scatter | solution.py:413
  4690.5 489.8 %reduce-scatter.17.cloned.1.call-start = ((), (), s32[]{:S(2)}) async-start(), calls=%async_computation.21 | async-start | bytes 8912896 | tf_op jit(solution)/shard_map/reduce_scatter | solution.py:412
  4696.3 591.6 %reduce-scatter.15.cloned.1.call-start = ((), (), s32[]{:S(2)}) async-start(), calls=%async_computation.20 | async-start | bytes 8912896 | tf_op jit(solution)/shard_map/reduce_scatter | solution.py:411
  (127 other events, 4215.0 us)
Sparse Core Ops, SparseCore 0:
  358.3 76.6 all-gather.44
  437.7 76.2 all-gather.46
  516.0 73.1 all-gather.48
  607.7 176.1 reduce-scatter.30
  788.0 177.5 reduce-scatter.28
  969.7 177.5 reduce-scatter.32
  1153.2 74.5 all-gather.44
  1230.4 76.2 all-gather.46
  1308.9 73.1 all-gather.48
  1400.6 176.0 reduce-scatter.30
  1580.8 177.5 reduce-scatter.28
  1762.4 177.5 reduce-scatter.32
  1945.6 74.5 all-gather.44
  2022.8 76.2 all-gather.46
  2101.1 73.1 all-gather.48
  2192.9 176.1 reduce-scatter.30
  2373.2 177.5 reduce-scatter.28
  2554.8 177.6 reduce-scatter.32
  2738.3 74.5 all-gather.44
  2815.6 76.2 all-gather.46
  2985.9 176.1 reduce-scatter.30
  3166.1 177.5 reduce-scatter.28
  3347.7 177.5 reduce-scatter.32
  3540.3 74.5 all-gather.42
  3617.7 76.2 all-gather.38
  3696.7 73.1 all-gather.40
  3876.4 76.2 all-gather.38
  3955.5 73.1 all-gather.40
  4135.1 76.2 all-gather.38
  4214.2 73.1 all-gather.40
  4393.6 76.2 all-gather.38
  4472.7 73.1 all-gather.40
  (9 shorter events, 484.7 us)
Sparse Core Ops, SparseCore 1:
  13.5 51.3 all-gather.32
  67.4 56.0 all-gather.34
  126.1 49.1 all-gather.30
  178.0 50.9 all-gather.36
  4679.9 54.1 reduce-scatter.26
  4737.7 60.0 reduce-scatter.24
  4801.8 53.4 reduce-scatter.22
  4859.8 105.4 reduce-scatter.20
  4969.8 102.9 reduce-scatter.18
  5077.4 102.9 reduce-scatter.16
  5184.9 102.9 reduce-scatter.14
where the time goes:
time: 5310 us; the launch traced here: 5300 us
  waiting for transfers between devices  4240 us (80%)
  matrix products  446 us (8%)
  local copies, waits for them, and re-layouts  205 us (4%)
  blocking collectives  169 us (3%)
  other arithmetic  168 us (3%)
    reduce_scatter x4, waiting for transfers between devices, expert_back(): lax.psum_scatter(gate_wgrad, 'dp', scatter_dimension=1, tiled=True)  718 us
    reduce_scatter x4, waiting for transfers between devices, expert_back(): lax.psum_scatter(down_wgrad, 'dp', scatter_dimension=2, tiled=True)  717 us
    all_gather x8, waiting for transfers between devices, gather_experts(): lax.all_gather(down_part, 'dp', axis=2, tiled=True)  578 us
    all_gather x8, waiting for transfers between devices, gather_experts(): lax.all_gather(gate_part, 'dp', axis=1, tiled=True)  572 us
    all_gather x8, waiting for transfers between devices, gather_experts(): lax.all_gather(up_part, 'dp', axis=1, tiled=True)  572 us
    reduce_scatter x4, waiting for transfers between devices, expert_back(): lax.psum_scatter(up_wgrad, 'dp', scatter_dimension=1, tiled=True)  452 us
    reduce_scatter x1, waiting for transfers between devices, body(): lax.psum_scatter(output_wgrad, 'dp', scatter_dimension=1, tiled=True)  110 us
    reduce_scatter x1, waiting for transfers between devices, body(): lax.psum_scatter(key_wgrad, 'dp', scatter_dimension=0, tiled=True)  108 us
  transfers between devices with their start and end apart: 54, of which 47 were waited for; matrix products, arithmetic and copies ran while one was open for 10% of the time, Pallas kernels for 0%

commit v1 on v0

v1 whole, which is shorter than its diff:
```python
import jax
import jax.numpy as jnp
from jax import lax
from jax.sharding import PartitionSpec as P

HEAD_DIM = 128
EXPERTS = 16
EPS = 1e-05
ROPE_BASE = 10000.0
MASKED = -1e30
F32 = jnp.float32
BF16 = jnp.bfloat16


def row_scale(values):
    return lax.rsqrt(jnp.mean(values * values, -1, keepdims=True) + EPS)


def mm(left, right):
    return lax.dot_general(left, right, (((1,), (0,)), ((), ())), preferred_element_type=F32)


def inner_rows(left, right):
    return lax.dot_general(left, right, (((0,), (0,)), ((), ())), preferred_element_type=F32)


def outer_cols(left, right):
    return lax.dot_general(left, right, (((1,), (1,)), ((), ())), preferred_element_type=F32)


def rope_tables(positions, head_size):
    half_size = head_size // 2
    freq_table = ROPE_BASE ** (-2.0 * jnp.arange(half_size, dtype=F32) / head_size)
    angles = positions[:, None] * freq_table[None, :]
    angles = jnp.concatenate([angles, angles], -1)
    return (jnp.cos(angles), jnp.sin(angles))


def rotate_heads(values, cosine_table, sine_table):
    half_size = values.shape[-1] // 2
    turned = jnp.concatenate([-values[..., half_size:], values[..., :half_size]], -1)
    return values * cosine_table[:, None, :] + turned * sine_table[:, None, :]


def unrotate_heads(grads, cosine_table, sine_table):
    half_size = grads.shape[-1] // 2
    scaled = grads * sine_table[:, None, :]
    turned = jnp.concatenate([scaled[..., half_size:], -scaled[..., :half_size]], -1)
    return grads * cosine_table[:, None, :] + turned


def ring_chip(place, chips):
    return 2 * place if place < chips // 2 else 2 * (chips - 1 - place) + 1


def ring_pairs(chips, step):
    pairs = []
    for first in range(0, lax.axis_size("dp"), 2 * chips):
        for place in range(chips):
            here = ring_chip(place, chips)
            there = ring_chip((place + step) % chips, chips)
            for core in range(2):
                pairs.append((first + 2 * here + core, first + 2 * there + core))
    return pairs


def ring_place(chips):
    chip = (lax.axis_index("dp") // 2) % chips
    return jnp.where(chip % 2 == 0, chip // 2, chips - 1 - chip // 2)


def to_sibling(values):
    pairs = [(index, index ^ 1) for index in range(lax.axis_size("dp"))]
    return lax.ppermute(values, "dp", pairs)


def to_peer(values):
    return lax.ppermute(values, "tensor", [(0, 1), (1, 0)])


def ring_gather(block, chips):
    upward, downward = ring_pairs(chips, 1), ring_pairs(chips, -1)
    lane = [block] + [None] * (chips - 1)
    rising = falling = block
    for step in range(1, chips // 2):
        rising = lax.ppermute(rising, "dp", upward)
        falling = lax.ppermute(falling, "dp", downward)
        lane[chips - step] = rising
        lane[step] = falling
    half = block.shape[0] // 2
    rising = lax.ppermute(rising[:half], "dp", upward)
    falling = lax.ppermute(falling[half:], "dp", downward)
    lane[chips // 2] = jnp.concatenate([rising, falling], 0)
    return [(mine, to_sibling(mine)) for mine in lane]


def ring_scatter(parts, chips, wire):
    upward, downward = ring_pairs(chips, 1), ring_pairs(chips, -1)
    total = [None] * chips
    half_way = chips // 2
    farthest_first = [half_way]
    for step in range(half_way - 1, 0, -1):
        farthest_first += [step, chips - step]
    for offset in farthest_first + [0]:
        mine, other = parts[offset]
        total[offset] = mine.astype(F32) + to_sibling(other.astype(wire)).astype(F32)
    half = total[0].shape[0] // 2
    rising = lax.ppermute(total[half_way][:half].astype(wire), "dp", upward)
    falling = lax.ppermute(total[half_way][half:].astype(wire), "dp", downward)
    for step in range(half_way - 1, -1, -1):
        above, below = total[step], total[(chips - step) % chips]
        rising, falling = rising.astype(F32), falling.astype(F32)
        if step == half_way - 1:
            pad = jnp.zeros_like(rising)
            rising = jnp.concatenate([rising, pad], 0)
            falling = jnp.concatenate([pad, falling], 0)
        if step == 0:
            return above + rising + falling
        rising = lax.ppermute((above + rising).astype(wire), "dp", upward)
        falling = lax.ppermute((below + falling).astype(wire), "dp", downward)


def roll_columns(values, start):
    width = values.shape[1]
    return lax.dynamic_slice_in_dim(jnp.concatenate([values, values], 1), start, width, 1)


def swap_cores(values, chips):
    rows, width = values.shape
    piece = width // (2 * chips)
    pieces = [values[:, at * piece : (at + 1) * piece] for at in range(2 * chips)]
    swapped = jnp.concatenate([pieces[at ^ 1] for at in range(2 * chips)], 1)
    return jnp.where(lax.axis_index("dp") % 2 == 0, values, swapped)


def to_ring_order(values, chips):
    piece = values.shape[1] // chips
    order = [ring_chip(place, chips) for place in range(chips)]
    placed = jnp.concatenate([values[:, at * piece : (at + 1) * piece] for at in order], 1)
    return swap_cores(roll_columns(placed, ring_place(chips) * piece), chips)


def from_ring_order(values, chips):
    piece = values.shape[1] // chips
    order = [ring_chip(place, chips) for place in range(chips)]
    back = [order.index(chip) for chip in range(chips)]
    place = ring_place(chips)
    placed = roll_columns(swap_cores(values, chips), lax.rem(chips - place, chips) * piece)
    return jnp.concatenate([placed[:, at * piece : (at + 1) * piece] for at in back], 1)


def stacked(pairs):
    return jnp.concatenate([block for pair in pairs for block in pair], 0)


def unstacked(values, chips):
    size = values.shape[0] // (2 * chips)
    pieces = [values[at * size : (at + 1) * size] for at in range(2 * chips)]
    return [(pieces[2 * at], pieces[2 * at + 1]) for at in range(chips)]


def expert_exchange(chunks):
    count = lax.axis_size("dp")
    groups = [list(range(at, at + EXPERTS)) for at in range(0, count, EXPERTS)]
    kwargs = {} if len(groups) == 1 else {"axis_index_groups": groups}
    return lax.all_to_all(chunks, "dp", split_axis=0, concat_axis=0, tiled=True, **kwargs)


def body(
    tokens,
    cotangent,
    dealing,
    lengths,
    routes,
    attention_gain,
    query_weight,
    key_weight,
    value_weight,
    output_weight,
    query_gain,
    key_gain,
    ffn_gain,
    router_weight,
    gate_weight,
    up_weight,
    down_weight,
):
    groups = lax.axis_size("dp")
    me = lax.axis_index("dp")
    side = lax.axis_index("tensor")
    rows_here, model_width = tokens.shape
    per_peer = rows_here // groups
    half_peer = per_peer // 2
    half_rows = rows_here // 2
    chips = groups // 2
    moe_chips = EXPERTS // 2
    replicas = groups // EXPERTS
    expert = lax.rem(me, EXPERTS)

    dealt = dealing.reshape(groups, rows_here)
    places = jnp.arange(rows_here, dtype=jnp.int32)
    source_block = dealt // rows_here
    packed = (source_block * rows_here + places[None, :]) * rows_here + lax.rem(dealt, rows_here)
    packed = jnp.sort(packed, axis=1)
    leaving = lax.rem(
        lax.dynamic_slice_in_dim(packed, me * per_peer, per_peer, 1), rows_here
    ).reshape(groups, 2, half_peer)
    own_order = lax.rem(
        lax.dynamic_index_in_dim(packed, me, 0, keepdims=False) // rows_here, rows_here
    ).reshape(groups, 2, half_peer)

    def by_side(table):
        first, second = table[:, 0].reshape(-1), table[:, 1].reshape(-1)
        return jnp.concatenate(
            [jnp.where(side == 0, first, second), jnp.where(side == 0, second, first)]
        )

    leaving = by_side(leaving)
    own_order = by_side(own_order)
    pick = (leaving[:half_rows, None] == places[None, :]).astype(BF16)
    sent = jnp.concatenate(
        [
            mm(pick, tokens).astype(BF16).reshape(groups, half_peer, model_width),
            mm(pick, cotangent).astype(BF16).reshape(groups, half_peer, model_width),
        ],
        1,
    )
    got = lax.all_to_all(sent, "dp", split_axis=0, concat_axis=0, tiled=True)
    rows = got[:, :half_peer].reshape(half_rows, model_width).astype(F32)
    cot_rows = got[:, half_peer:].reshape(half_rows, model_width)

    small = jnp.concatenate(
        [
            attention_gain,
            ffn_gain,
            query_gain.reshape(-1),
            key_gain.reshape(-1),
            router_weight.reshape(-1),
        ]
    ).astype(BF16)
    small = lax.all_gather(small[None], "dp", axis=0, tiled=True)
    shard = attention_gain.shape[0]
    gain_shard = query_gain.shape[1]
    first_gain = small[:, :shard].reshape(-1).astype(F32)
    second_gain = small[:, shard : 2 * shard].reshape(-1).astype(F32)
    at = 2 * shard
    query_scale_gain = small[:, at : at + gain_shard].reshape(-1).astype(F32)
    key_scale_gain = small[:, at + gain_shard : at + 2 * gain_shard].reshape(-1).astype(F32)
    router_full = small[:, at + 2 * gain_shard :].reshape(model_width, EXPERTS)

    qkv_block = jnp.concatenate([query_weight, key_weight, value_weight], 1).astype(BF16)
    qkv_full = stacked(ring_gather(qkv_block, chips))
    output_full = stacked(ring_gather(output_weight.T.astype(BF16), chips))
    heads_width = query_weight.shape[1]

    expert_block = jnp.concatenate(
        [gate_weight.astype(BF16), up_weight.astype(BF16), down_weight.astype(BF16).swapaxes(1, 2)],
        2,
    )
    hidden_half = gate_weight.shape[2]
    expert_own = expert_exchange(expert_block).reshape(-1, 3 * hidden_half)
    across = [list(range(at, groups, EXPERTS)) for at in range(EXPERTS)]
    if replicas > 1:
        expert_own = lax.all_gather(
            expert_own, "dp", axis=0, tiled=True, axis_index_groups=across
        )
    expert_peer = to_peer(expert_own)

    cot_all = stacked(ring_gather(cot_rows, moe_chips))

    finish_at = jnp.cumsum(lengths[0])
    start_at = finish_at - lengths[0]
    segment_ids = jnp.sum((own_order[:, None] >= finish_at[None, :]).astype(jnp.int32), -1)
    numbers = jnp.arange(lengths.shape[1], dtype=jnp.int32)
    begins = jnp.sum(jnp.where(segment_ids[:, None] == numbers[None, :], start_at[None, :], 0), -1)
    cosine_table, sine_table = rope_tables((own_order - begins).astype(F32), HEAD_DIM)
    allowed = (segment_ids[:, None] == segment_ids[None, :]) & (
        own_order[None, :] <= own_order[:, None]
    )
    head_scale = HEAD_DIM ** (-0.5)

    expert_ids = jnp.arange(EXPERTS, dtype=jnp.int32)
    uses = jnp.sum((routes[:, :, None] == expert_ids[None, None, :]).astype(F32), 1)
    reorder = (own_order[:half_rows, None] == places[None, :]).astype(BF16)
    used = mm(reorder, uses.astype(BF16))

    norm_one = row_scale(rows)
    normed_own = (rows * norm_one * first_gain).astype(BF16)
    normed_one = to_ring_order(jnp.concatenate([normed_own, to_peer(normed_own)], 0), chips)
    qkv = mm(normed_one, qkv_full)
    query_raw, key_raw = qkv[:, :heads_width], qkv[:, heads_width : 2 * heads_width]
    value_rows = qkv[:, 2 * heads_width :].astype(BF16)

    def over_sides(values):
        theirs = to_peer(values)
        return values + jnp.concatenate([theirs[:, half_rows:], theirs[:, :half_rows]], 1)

    squares = over_sides(
        jnp.stack([jnp.sum(query_raw * query_raw, -1), jnp.sum(key_raw * key_raw, -1)])
    )
    query_scale = lax.rsqrt(squares[0] / model_width + EPS)[:, None]
    key_scale = lax.rsqrt(squares[1] / model_width + EPS)[:, None]
    heads_here = heads_width // HEAD_DIM
    query_normed = query_raw * query_scale * query_scale_gain
    key_normed = key_raw * key_scale * key_scale_gain
    query_heads = rotate_heads(
        query_normed.reshape(rows_here, heads_here, HEAD_DIM), cosine_table, sine_table
    ).astype(BF16)
    key_heads = rotate_heads(
        key_normed.reshape(rows_here, heads_here, HEAD_DIM), cosine_table, sine_table
    ).astype(BF16)
    value_heads = value_rows.reshape(rows_here, heads_here, HEAD_DIM)

    def attention_scores(query_part, key_part):
        raw_scores = (
            jnp.einsum("qhd,khd->hqk", query_part, key_part, preferred_element_type=F32)
            * head_scale
        )
        return jnp.where(allowed[None], raw_scores, MASKED)

    masked_scores = attention_scores(query_heads, key_heads)
    peak_value = jnp.max(masked_scores, -1, keepdims=True)
    powered = jnp.exp(masked_scores - peak_value)
    total_weight = jnp.sum(powered, -1, keepdims=True)
    probs = powered / total_weight
    log_total = peak_value + jnp.log(total_weight)
    context = jnp.einsum(
        "hqk,khd->qhd", probs.astype(BF16), value_heads, preferred_element_type=F32
    )
    context = context.reshape(rows_here, -1).astype(BF16)
    attention = outer_cols(context, output_full)
    attention = attention[:half_rows] + to_peer(attention[half_rows:].astype(BF16)).astype(F32)
    hidden = rows + from_ring_order(attention, chips)

    norm_two = row_scale(hidden)
    normed_two = (hidden * norm_two * second_gain).astype(BF16)
    logits = mm(normed_two, router_full)
    powered_two = jnp.exp(logits - jnp.max(logits, -1, keepdims=True))
    router_probs = powered_two / jnp.sum(powered_two, -1, keepdims=True)
    gate_table = (router_probs * used).T

    inputs_all = stacked(ring_gather(normed_two, moe_chips))
    gate_blocks = jnp.stack([b for pair in ring_gather(gate_table, moe_chips) for b in pair])
    gates = lax.dynamic_index_in_dim(gate_blocks, expert, 1, keepdims=False).reshape(-1, 1)
    out_cells = (cot_all.astype(F32) * gates).astype(BF16)
    halves = []
    for weights in (expert_own, expert_peer):
        front = mm(inputs_all, weights[:, : 2 * hidden_half])
        gate_pre, up_pre = front[:, :hidden_half], front[:, hidden_half:]
        sigmoid_gate = 1.0 / (1.0 + jnp.exp(-gate_pre))
        active = (gate_pre * sigmoid_gate * up_pre).astype(BF16)
        active_grad = mm(out_cells, weights[:, 2 * hidden_half :])
        gate_grad = (
            active_grad * up_pre * sigmoid_gate * (1.0 + gate_pre * (1.0 - sigmoid_gate))
        ).astype(BF16)
        up_grad = (active_grad * gate_pre * sigmoid_gate).astype(BF16)
        halves.append((active, jnp.concatenate([gate_grad, up_grad], 1), weights))
    input_grad = sum(outer_cols(grad, w[:, : 2 * hidden_half]) for _, grad, w in halves)
    produced = sum(outer_cols(active, w[:, 2 * hidden_half :]) for active, _, w in halves)
    mixing = jnp.sum(produced * cot_all.astype(F32), -1)
    expert_wgrads = [
        jnp.concatenate([inner_rows(inputs_all, grad), inner_rows(out_cells, active)], 1)
        for active, grad, _ in halves
    ]

    normed_two_grad = ring_scatter(unstacked(input_grad, moe_chips), moe_chips, BF16)
    mine = (expert_ids == expert).astype(F32)[None, :, None]
    mixing_table = (mixing.reshape(EXPERTS, 1, half_rows) * mine).reshape(-1, half_rows)
    mixing_table = ring_scatter(unstacked(mixing_table, moe_chips), moe_chips, F32)
    mixture = ring_scatter(unstacked(produced * gates, moe_chips), moe_chips, BF16)
    out_rows = (hidden + mixture).astype(BF16)

    expert_wgrad = expert_wgrads[0] + to_peer(expert_wgrads[1].astype(BF16)).astype(F32)
    expert_wgrad = expert_wgrad.astype(BF16)
    if replicas > 1:
        expert_wgrad = lax.psum_scatter(
            expert_wgrad, "dp", scatter_dimension=0, tiled=True, axis_index_groups=across
        )
    wgrads = expert_exchange(expert_wgrad.reshape(EXPERTS, -1, 3 * hidden_half))
    gate_weight_grad = wgrads[:, :, :hidden_half].astype(F32)
    up_weight_grad = wgrads[:, :, hidden_half : 2 * hidden_half].astype(F32)
    down_weight_grad = wgrads[:, :, 2 * hidden_half :].swapaxes(1, 2).astype(F32)

    prob_grad = mixing_table.T * used
    logit_grad = (
        router_probs * (prob_grad - jnp.sum(router_probs * prob_grad, -1, keepdims=True))
    ).astype(BF16)
    router_wgrad = inner_rows(normed_two, logit_grad)
    normed_two_grad = normed_two_grad + outer_cols(logit_grad, router_full)
    ffn_gain_grad = jnp.sum(normed_two_grad * hidden * norm_two, 0)
    scaled_two = normed_two_grad * second_gain
    hidden_grad = cot_rows.astype(F32) + norm_two * (
        scaled_two - hidden * norm_two * norm_two * jnp.mean(scaled_two * hidden, -1, keepdims=True)
    )

    attn_own = hidden_grad.astype(BF16)
    attn_grad = to_ring_order(jnp.concatenate([attn_own, to_peer(attn_own)], 0), chips)
    output_wgrad = inner_rows(attn_grad, context)
    output_wgrad = ring_scatter(unstacked(output_wgrad, chips), chips, BF16)
    context_grad = mm(attn_grad, output_full).astype(BF16)
    context_grad = context_grad.reshape(rows_here, heads_here, HEAD_DIM)
    recomputed = jnp.exp(attention_scores(query_heads, key_heads) - log_total)
    prob_pair_grad = jnp.einsum(
        "qhd,khd->hqk", context_grad, value_heads, preferred_element_type=F32
    )
    value_grad = jnp.einsum(
        "hqk,qhd->khd", recomputed.astype(BF16), context_grad, preferred_element_type=F32
    )
    value_grad = value_grad.reshape(rows_here, -1).astype(BF16)
    score_grad = (
        recomputed * (prob_pair_grad - jnp.sum(recomputed * prob_pair_grad, -1, keepdims=True))
    ).astype(BF16)
    query_rot_grad = (
        jnp.einsum("hqk,khd->qhd", score_grad, key_heads, preferred_element_type=F32) * head_scale
    )
    key_rot_grad = (
        jnp.einsum("hqk,qhd->khd", score_grad, query_heads, preferred_element_type=F32)
        * head_scale
    )
    query_norm_grad = unrotate_heads(query_rot_grad, cosine_table, sine_table).reshape(
        rows_here, -1
    )
    key_norm_grad = unrotate_heads(key_rot_grad, cosine_table, sine_table).reshape(rows_here, -1)
    inners = over_sides(
        jnp.stack(
            [
                jnp.sum(query_norm_grad * query_scale_gain * query_raw, -1),
                jnp.sum(key_norm_grad * key_scale_gain * key_raw, -1),
            ]
        )
    )
    query_gain_grad = jnp.sum(query_norm_grad * query_raw * query_scale, 0)
    key_gain_grad = jnp.sum(key_norm_grad * key_raw * key_scale, 0)
    query_raw_grad = (
        query_scale * query_scale_gain * query_norm_grad
        - query_raw * query_scale**3 * inners[0][:, None] / model_width
    ).astype(BF16)
    key_raw_grad = (
        key_scale * key_scale_gain * key_norm_grad
        - key_raw * key_scale**3 * inners[1][:, None] / model_width
    ).astype(BF16)
    qkv_grad = jnp.concatenate([query_raw_grad, key_raw_grad, value_grad], 1)
    qkv_wgrad = ring_scatter(
        unstacked(inner_rows(normed_one, qkv_grad), chips), chips, BF16
    )
    normed_one_grad = outer_cols(qkv_grad, qkv_full)
    normed_one_grad = normed_one_grad[:half_rows] + to_peer(
        normed_one_grad[half_rows:].astype(BF16)
    ).astype(F32)
    normed_one_grad = from_ring_order(normed_one_grad, chips)
    attention_gain_grad = jnp.sum(normed_one_grad * rows * norm_one, 0)
    scaled_one = normed_one_grad * first_gain
    rows_grad = hidden_grad + norm_one * (
        scaled_one - rows * norm_one * norm_one * jnp.mean(scaled_one * rows, -1, keepdims=True)
    )

    small_grad = jnp.concatenate(
        [
            query_gain_grad.reshape(groups, -1),
            key_gain_grad.reshape(groups, -1),
            attention_gain_grad.reshape(groups, -1),
            ffn_gain_grad.reshape(groups, -1),
            router_wgrad.reshape(groups, -1),
        ],
        1,
    )
    small_grad = jnp.sum(
        lax.all_to_all(small_grad, "dp", split_axis=0, concat_axis=0, tiled=True), 0
    )
    at = 2 * gain_shard
    by_rows = small_grad[at:]
    by_rows = by_rows + to_peer(by_rows)

    place_back = (places[:, None] == leaving[None, :]).astype(BF16)

    def send_back(values):
        back = values.reshape(groups, half_peer, model_width)
        back = lax.all_to_all(back, "dp", split_axis=0, concat_axis=0, tiled=True)
        back = back.reshape(half_rows, model_width)
        return mm(place_back, jnp.concatenate([back, to_peer(back)], 0)).astype(BF16)

    return (
        send_back(out_rows),
        send_back(rows_grad.astype(BF16)),
        by_rows[:shard],
        qkv_wgrad[:, :heads_width],
        qkv_wgrad[:, heads_width : 2 * heads_width],
        qkv_wgrad[:, 2 * heads_width :],
        output_wgrad.T,
        small_grad[:gain_shard][None],
        small_grad[gain_shard:at][None],
        by_rows[shard : 2 * shard],
        by_rows[2 * shard :].reshape(router_weight.shape),
        gate_weight_grad,
        up_weight_grad,
        down_weight_grad,
    )


def solution(mesh):
    rows = P("dp", None)
    columns = P("tensor", "dp")
    inputs = (rows, rows, P(), rows, rows, P("dp"))
    inputs += (P("dp", "tensor"),) * 3 + (columns,) * 3 + (P("dp"), rows)
    inputs += (P(None, "dp", "tensor"),) * 2 + (P(None, "tensor", "dp"),)
    outputs = (rows, rows, P("dp")) + (P("dp", "tensor"),) * 3 + (columns,) * 3
    outputs += (P("dp"), rows) + (P(None, "dp", "tensor"),) * 2 + (P(None, "tensor", "dp"),)
    return jax.shard_map(body, mesh=mesh, in_specs=inputs, out_specs=outputs, check_vma=False)
```

time: 5310 us -> 1390 us (0.26)
  waiting for transfers between devices: 4240 us -> 684 us
  matrix products: 446 us -> 214 us
  starting transfers between devices: 37.5 us -> 205 us
  blocking collectives: 169 us -> 30.9 us
  local copies, waits for them, and re-layouts: 205 us -> 109 us
  other arithmetic: 168 us -> 101 us
    reduce_scatter x17 -> x0, waiting for transfers between devices: 2320 us -> none  [the longest x4 718 us: expert_back(): lax.psum_scatter(gate_wgrad, 'dp', scatter_dimension=1, tiled=True)]
    all_gather x28 -> x0, waiting for transfers between devices: 1810 us -> none  [the longest x8 578 us: gather_experts(): lax.all_gather(down_part, 'dp', axis=2, tiled=True)]
    ppermute x0 -> x171, waiting for transfers between devices: none -> 680 us  [the longest x11 170 us: to_peer(): return lax.ppermute(values, 'tensor', [(0, 1), (1, 0)])]
    dot_general x52 -> x15, matrix products: 415 us -> 78.1 us  [the longest x12 74 us: mm(): lax.dot_general(left, right, (((1,), (0,)), ((), ())), preferred_element_...]
    ppermute x0 -> x171, starting transfers between devices: none -> 157 us  [the longest x80 84.2 us: to_sibling(): return lax.ppermute(values, 'dp', pairs)]
    scatter-add x8 -> x0, other arithmetic: 124 us -> none  [the longest x4 62 us: backward_group(): row_grads = row_grads.at[owners].add(input_grad.reshape(-1, model_width))]
    psum x3 -> x0, waiting for transfers between devices: 78.1 us -> none  [the longest x1 41.2 us: body(): lax.psum((row_grads[:rows_here], mixing_tokens), 'tensor')]
    unnamed x2 -> x0, blocking collectives: 74.1 us -> none
  transfers between devices with their start and end apart: 54 -> 177, of which waited for: 47 -> 51; matrix products, arithmetic and copies ran while one was open for 10% -> 25% of each run, Pallas kernels for 0% -> 0%
where the time goes in v1:
time: 1390 us; the launch traced here: 1360 us
  waiting for transfers between devices  684 us (49%)
  matrix products  214 us (15%)
  starting transfers between devices  205 us (15%)
  local copies, waits for them, and re-layouts  109 us (8%)
  other arithmetic  101 us (7%)
  blocking collectives  30.9 us (2%)
  between operations  17.7 us (1%)
    ppermute x11, waiting for transfers between devices, to_peer(): return lax.ppermute(values, 'tensor', [(0, 1), (1, 0)])  170 us
    ppermute x5, waiting for transfers between devices, ring_scatter(): rising = lax.ppermute(total[half_way][:half].astype(wire), 'dp', upward)  164 us
    ppermute x5, waiting for transfers between devices, ring_gather(): rising = lax.ppermute(rising[:half], 'dp', upward)  111 us
    ppermute x15, waiting for transfers between devices, ring_gather(): falling = lax.ppermute(falling, 'dp', downward)  86.2 us
    ppermute x80, starting transfers between devices, to_sibling(): return lax.ppermute(values, 'dp', pairs)  84.2 us
    dot_general x12, matrix products, mm(): lax.dot_general(left, right, (((1,), (0,)), ((), ())), preferred_element_...  74 us
    dot_general x7, matrix products, outer_cols(): lax.dot_general(left, right, (((1,), (1,)), ((), ())), preferred_element_...  71.8 us
    unnamed x432, local copies, waits for them, and re-layouts  67.7 us
  transfers between devices with their start and end apart: 177, of which 51 were waited for; matrix products, arithmetic and copies ran while one was open for 25% of the time, Pallas kernels for 0%

profile of v1, /device:TPU:17, one launch (start us, length us, event | category | flops | bytes accessed | tf_op | source)
XLA Modules:
  0.0 1361.4 jit_solution(12519136445739715238)
XLA Ops:
  17.1 30.9 %all-gather = bf16[16,1,2432]{2,1,0:T(2,128)(2,1)S(1)} all-gather(bf16[1,1,2432]{2,1,0:T(2,128)(2,1)S(1)} %bitcast.349), channel_id=1, replica_groups=mesh['dp'=16,'tensor'=2] {'dp'}, dimensions={0}, use_global_device_ids=true | all-gather | bytes 82688 | tf_op jit(solution)/shard_map/all_gather | solution.py:241
  70.1 10.0 all-to-all-start
  82.2 26.4 %collective-permute-done.21 = bf16[128,1024]{0,1:T(8,128)(2,1)S(1)} collective-permute-done((bf16[128,1024]{0,1:T(8,128)(2,1)}, bf16[128,1024]{0,1:T(8,128)(2,1)S(1)}, u32[]{:S(2)}, u32[]{:S(2)}) %collective-permute-start.21) | collective-permute-done | bytes 262176 | tf_op jit(solution)/shard_map/ppermute | solution.py:87
  129.1 11.0 collective-permute-done.4
  164.1 30.1 %collective-permute-done.6 = bf16[128,3072]{1,0:T(8,128)(2,1)S(1)} collective-permute-done((bf16[128,3072]{1,0:T(8,128)(2,1)}, bf16[128,3072]{1,0:T(8,128)(2,1)S(1)}, u32[]{:S(2)}, u32[]{:S(2)}) %collective-permute-start.6) | collective-permute-done | bytes 786464 | tf_op jit(solution)/shard_map/ppermute | solution.py:87
  202.3 103.6 %collective-permute-done.11 = bf16[64,3072]{1,0:T(8,128)(2,1)S(1)} collective-permute-done((bf16[64,3072]{1,0:T(8,128)(2,1)S(1)}, bf16[64,3072]{1,0:T(8,128)(2,1)S(1)}, u32[]{:S(2)}, u32[]{:S(2)}) %collective-permute-start.11) | collective-permute-done | bytes 393248 | tf_op jit(solution)/shard_map/ppermute | solution.py:91
  447.7 10.2 collective-permute-done.44
  476.1 23.0 %fusion.9 = f32[2048,1024]{0,1:T(8,128)} fusion(bf16[2048,2048]{1,0:T(8,128)(2,1)} %constant_dynamic-update-slice_fusion.78, bf16[2048,1536]{1,0:T(8,128)(2,1)} %bitcast.28), kind=kOutput, calls=%fused_computation.30 | convolution fusion | flops 8589934592 | bytes 20971520 | tf_op jit(solution)/shard_map/dot_general | solution.py:20
  499.1 11.3 multiply_convert_fusion.3
  518.5 10.0 fusion.20
  528.5 15.1 %fusion.7 = f32[2048,2048]{1,0:T(8,128)} fusion(bf16[2048,1536]{1,0:T(8,128)(2,1)} %bitcast.28, bf16[2048,512]{0,1:T(8,128)(2,1)} %get-tuple-element.141, bf16[2048,512]{0,1:T(8,128)(2,1)S(1)} %copy-done.128), kind=kOutput, calls=%fused_computation.28 | convolution fusion | flops 8598323200 | bytes 25165824 | tf_op jit(solution)/shard_map/dot_general | solution.py:28
  543.6 13.8 %fusion.11 = f32[2048,1024]{0,1:T(8,128)} fusion(bf16[2048,2048]{1,0:T(8,128)(2,1)} %constant_dynamic-update-slice_fusion.78, bf16[2048,512]{0,1:T(8,128)(2,1)} %get-tuple-element.141, bf16[2048,512]{0,1:T(8,128)(2,1)S(1)} %copy-done.128), kind=kOutput, calls=%fused_computation.33 | convolution fusion | flops 8598323200 | bytes 20971520 | tf_op jit(solution)/shard_map/dot_general | solution.py:24
  557.4 55.8 %collective-permute-done.51 = bf16[2048,1536]{1,0:T(8,128)(2,1)S(1)} collective-permute-done((bf16[2048,1536]{1,0:T(8,128)(2,1)}, bf16[2048,1536]{1,0:T(8,128)(2,1)S(1)}, u32[]{:S(2)}, u32[]{:S(2)}) %collective-permute-start.51) | collective-permute-done | bytes 6291488 | tf_op jit(solution)/shard_map/ppermute | solution.py:78
  615.9 14.0 %fusion.5 = f32[2048,1024]{0,1:T(8,128)} fusion(bf16[2048,2048]{1,0:T(8,128)(2,1)} %constant_dynamic-update-slice_fusion.78, bf16[2048,1536]{1,0:T(8,128)(2,1)S(1)} %collective-permute-done.51), kind=kOutput, calls=%fused_computation.26 | convolution fusion | flops 8589934592 | bytes 20971520 | tf_op jit(solution)/shard_map/dot_general | solution.py:20
  629.8 11.0 multiply_convert_fusion.1
  640.8 17.9 %fusion.206 = (bf16[2048,2048]{1,0:T(8,128)(2,1)}, f32[2048,2048]{1,0:T(8,128)}, f32[2048]{0:T(1024)S(1)}) fusion(f32[2048]{0:T(1024)S(1)} %bitcast.347, bf16[2048,2048]{1,0:T(8,128)(2,1)} %copy-done.8, f32[2048,2048]{1,0:T(8,128)} %fusion.20, bf16[2048,512]{0,1:T(8,128)(2,1)S(1)} %get-tuple-element.152, bf16[2048,1536]{1,0:T(8,128)(2,1)} %copy-done.42), kind=kOutput, calls=%fused_computation.617 | convolution fusion | flops 4320131072 | bytes 54542336 | tf_op jit(solution)/shard_map/dot_general | solution.py:28
  660.7 13.8 %convolution_convert_fusion = bf16[2048,1024]{0,1:T(8,128)(2,1)} fusion(bf16[2048,2048]{1,0:T(8,128)(2,1)} %constant_dynamic-update-slice_fusion.78, bf16[2048,512]{0,1:T(8,128)(2,1)} %get-tuple-element.139, bf16[2048,512]{0,1:T(8,128)(2,1)} %get-tuple-element.138), kind=kOutput, calls=%fused_computation.24 | convolution fusion | flops 8600420352 | bytes 16777216 | tf_op jit(solution)/shard_map/dot_general | solution.py:24
  674.8 18.9 %fusion.225 = (bf16[2048,2048]{1,0:T(8,128)(2,1)}, f32[2048,2048]{1,0:T(8,128)}) fusion(f32[2048,2048]{1,0:T(8,128)} %fusion.7, bf16[2048,1536]{1,0:T(8,128)(2,1)} %copy-done.42, bf16[2048,512]{0,1:T(8,128)(2,1)} %get-tuple-element.139, bf16[2048,512]{0,1:T(8,128)(2,1)} %get-tuple-element.138), kind=kOutput, calls=%fused_computation.636 | convolution fusion | flops 8606711808 | bytes 50331648 | tf_op jit(solution)/shard_map/dot_general | solution.py:28
  701.1 10.0 convolution_convert_fusion.1
  725.7 11.8 collective-permute-done.107
  791.6 9.6 collective-permute-done.115
  814.2 9.5 collective-permute-done.116
  825.7 9.2 collective-permute-done.83
  844.7 10.0 all-to-all-start.2
  876.7 105.5 %collective-permute-done.134 = f32[2,256]{1,0:T(2,128)S(1)} collective-permute-done((f32[2,256]{1,0:T(2,128)S(1)}, f32[2,256]{1,0:T(2,128)S(1)}, u32[]{:S(2)}, u32[]{:S(2)}) %collective-permute-start.134) | collective-permute-done | bytes 2080 | tf_op jit(solution)/shard_map/ppermute | solution.py:78
  992.2 14.5 %fusion.226 = (bf16[2048,3072]{1,0:T(8,128)(2,1)}, f32[2048,3072]{1,0:T(8,128)}) fusion(bf16[256,1024]{1,0:T(8,128)(2,1)S(1)} %copy.214, bf16[256,1024]{1,0:T(8,128)(2,1)S(1)} %get-tuple-element.174, bf16[256,1024]{1,0:T(8,128)(2,1)S(1)} %get-tuple-element.173, bf16[256,2048]{1,0:T(8,128)(2,1)S(1)} %copy-done.34, bf16[256,4096]{1,0:T(8,128)(2,1)S(1)} %copy-done.28, ...), kind=kOutput, calls=%fused_computation.637 | convolution fusion | flops 3232759808 | bytes 41418756 | tf_op jit(solution)/shard_map/dot_general | solution.py:24
  1014.2 9.1 all-to-all-start.4
  1059.4 140.5 %collective-permute-done.143 = bf16[64,3072]{1,0:T(8,128)(2,1)S(1)} collective-permute-done((bf16[64,3072]{1,0:T(8,128)(2,1)S(1)}, bf16[64,3072]{1,0:T(8,128)(2,1)S(1)}, u32[]{:S(2)}, u32[]{:S(2)}) %collective-permute-start.143) | collective-permute-done | bytes 393248 | tf_op jit(solution)/shard_map/ppermute | solution.py:108
  1206.3 13.4 collective-permute-done.144
  1224.0 17.5 %collective-permute-done.159 = bf16[64,1024]{1,0:T(8,128)(2,1)S(1)} collective-permute-done((bf16[64,1024]{1,0:T(8,128)(2,1)S(1)}, bf16[64,1024]{1,0:T(8,128)(2,1)S(1)}, u32[]{:S(2)}, u32[]{:S(2)}) %collective-permute-start.159) | collective-permute-done | bytes 131104 | tf_op jit(solution)/shard_map/ppermute | solution.py:108
  1257.7 12.2 collective-permute-done.166
  1287.9 16.2 %collective-permute-done.168 = bf16[128,1024]{1,0:T(8,128)(2,1)S(1)} collective-permute-done((bf16[128,1024]{1,0:T(8,128)(2,1)S(1)}, bf16[128,1024]{1,0:T(8,128)(2,1)S(1)}, u32[]{:S(2)}, u32[]{:S(2)}) %collective-permute-start.168) | collective-permute-done | bytes 262176 | tf_op jit(solution)/shard_map/ppermute | solution.py:120
  (1009 shorter events, 527.9 us)
Async XLA Ops:
  12.0 106.0 %collective-permute-start.2 = (bf16[128,3072]{1,0:T(8,128)(2,1)}, bf16[128,3072]{1,0:T(8,128)(2,1)}, u32[]{:S(2)}, u32[]{:S(2)}) collective-permute-start(bf16[128,3072]{1,0:T(8,128)(2,1)} %get-tuple-element.192), channel_id=1, source_target_pairs={{0,4},{2,6},{8,0},{10,2},{16,8},{18,10},{24,16},{26,18},{28,24},{3... | collective-permute-start | bytes 2359304 | tf_op jit(solution)/shard_map/ppermute | solution.py:87
  12.2 108.0 %collective-permute-start.1 = (bf16[128,3072]{1,0:T(8,128)(2,1)}, bf16[128,3072]{1,0:T(8,128)(2,1)}, u32[]{:S(2)}, u32[]{:S(2)}) collective-permute-start(bf16[128,3072]{1,0:T(8,128)(2,1)} %get-tuple-element.192), channel_id=1, source_target_pairs={{0,2},{2,0},{4,6},{6,4},{8,10},{10,8},{12,14},{14,12},{16,18},{18,... | collective-permute-start | bytes 2359304 | tf_op jit(solution)/shard_map/ppermute | solution.py:74
  13.2 108.7 %collective-permute-start.8 = (bf16[128,3072]{1,0:T(8,128)(2,1)}, bf16[128,3072]{1,0:T(8,128)(2,1)}, u32[]{:S(2)}, u32[]{:S(2)}) collective-permute-start(bf16[128,3072]{1,0:T(8,128)(2,1)} %get-tuple-element.192), channel_id=1, source_target_pairs={{0,8},{2,10},{8,16},{10,18},{16,24},{18,26},{24,28},{26,30},{28,20... | collective-permute-start | bytes 2359304 | tf_op jit(solution)/shard_map/ppermute | solution.py:86
  14.5 66.1 %collective-permute-start.19 = (bf16[128,1024]{0,1:T(8,128)(2,1)S(1)}, bf16[128,1024]{0,1:T(8,128)(2,1)}, u32[]{:S(2)}, u32[]{:S(2)}) collective-permute-start(bf16[128,1024]{0,1:T(8,128)(2,1)S(1)} %convert_bitcast_fusion.3), channel_id=1, source_target_pairs={{0,4},{2,6},{8,0},{10,2},{16,8},{18,10},{24,16},{26,18},{28,24},{3... | collective-permute-start | bytes 786440 | tf_op jit(solution)/shard_map/ppermute | solution.py:87
  14.7 66.2 %collective-permute-start.25 = (bf16[128,1024]{0,1:T(8,128)(2,1)S(1)}, bf16[128,1024]{0,1:T(8,128)(2,1)}, u32[]{:S(2)}, u32[]{:S(2)}) collective-permute-start(bf16[128,1024]{0,1:T(8,128)(2,1)S(1)} %convert_bitcast_fusion.3), channel_id=1, source_target_pairs={{0,8},{2,10},{8,16},{10,18},{16,24},{18,26},{24,28},{26,30},{28,20... | collective-permute-start | bytes 786440 | tf_op jit(solution)/shard_map/ppermute | solution.py:86
  70.1 76.5 %all-to-all-start = ((bf16[16,16,2048]{2,1,0:T(8,128)(2,1)}), bf16[16,16,2048]{2,1,0:T(8,128)(2,1)S(1)}, u32[]{:S(2)}, u32[]{:S(2)}) async-start(bf16[16,16,2048]{2,1,0:T(8,128)(2,1)} %pad_maximum_fusion.9), calls=%async_computation | async-start | bytes 2097152 | tf_op jit(solution)/shard_map/all_to_all | solution.py:228
  126.0 190.8 %collective-permute-start.18 = (bf16[128,1024]{0,1:T(8,128)(2,1)S(1)}, bf16[128,1024]{0,1:T(8,128)(2,1)}, u32[]{:S(2)}, u32[]{:S(2)}) collective-permute-start(bf16[128,1024]{0,1:T(8,128)(2,1)S(1)} %convert_bitcast_fusion.3), channel_id=1, source_target_pairs={{0,2},{2,0},{4,6},{6,4},{8,10},{10,8},{12,14},{14,12},{16,18},{18,... | collective-permute-start | bytes 786440 | tf_op jit(solution)/shard_map/ppermute | solution.py:74
  126.4 190.4 %collective-permute-start.20 = (bf16[128,1024]{0,1:T(8,128)(2,1)}, bf16[128,1024]{0,1:T(8,128)(2,1)}, u32[]{:S(2)}, u32[]{:S(2)}) collective-permute-start(bf16[128,1024]{0,1:T(8,128)(2,1)} %collective-permute-done.19), channel_id=1, source_target_pairs={{0,2},{2,0},{4,6},{6,4},{8,10},{10,8},{12,14},{14,12},{16,18},{18,... | collective-permute-start | bytes 786440 | tf_op jit(solution)/shard_map/ppermute | solution.py:74
  140.1 54.1 %collective-permute-start.5 = (bf16[128,3072]{1,0:T(8,128)(2,1)}, bf16[128,3072]{1,0:T(8,128)(2,1)}, u32[]{:S(2)}, u32[]{:S(2)}) collective-permute-start(bf16[128,3072]{1,0:T(8,128)(2,1)} %collective-permute-done.4), channel_id=1, source_target_pairs={{0,2},{2,0},{4,6},{6,4},{8,10},{10,8},{12,14},{14,12},{16,18},{18,... | collective-permute-start | bytes 2359304 | tf_op jit(solution)/shard_map/ppermute | solution.py:74
  141.5 52.6 %collective-permute-start.6 = (bf16[128,3072]{1,0:T(8,128)(2,1)}, bf16[128,3072]{1,0:T(8,128)(2,1)S(1)}, u32[]{:S(2)}, u32[]{:S(2)}) collective-permute-start(bf16[128,3072]{1,0:T(8,128)(2,1)} %collective-permute-done.4), channel_id=1, source_target_pairs={{0,4},{2,6},{8,0},{10,2},{16,8},{18,10},{24,16},{26,18},{28,24},{3... | collective-permute-start | bytes 2359304 | tf_op jit(solution)/shard_map/ppermute | solution.py:87
  146.7 329.1 %all-to-all-start.1 = ((bf16[16,128,1536]{2,1,0:T(8,128)(2,1)}), bf16[16,128,1536]{2,1,0:T(8,128)(2,1)}, u32[]{:S(2)}, u32[]{:S(2)}) async-start(bf16[16,128,1536]{2,1,0:T(8,128)(2,1)} %pad_maximum_fusion), calls=%async_computation.1 | async-start | bytes 12582912 | tf_op jit(solution)/shard_map/all_to_all | solution.py:166
  162.8 37.0 %collective-permute-start = (bf16[128,2048]{1,0:T(8,128)(2,1)S(1)}, bf16[128,2048]{1,0:T(8,128)(2,1)S(1)}, u32[]{:S(2)}, u32[]{:S(2)}) collective-permute-start(bf16[128,2048]{1,0:T(8,128)(2,1)S(1)} %fusion.42), channel_id=1, source_target_pairs={{0,1},{1,0},{2,3},{3,2},{4,5},{5,4},{6,7},{7,6},{8,9},{9,8},{10,11... | collective-permute-start | bytes 1572872 | tf_op jit(solution)/shard_map/ppermute | solution.py:78
  194.2 111.8 %collective-permute-start.11 = (bf16[64,3072]{1,0:T(8,128)(2,1)S(1)}, bf16[64,3072]{1,0:T(8,128)(2,1)S(1)}, u32[]{:S(2)}, u32[]{:S(2)}) collective-permute-start(bf16[64,3072]{1,0:T(8,128)(2,1)S(1)} %slice.1126), channel_id=1, source_target_pairs={{0,8},{2,10},{8,16},{10,18},{16,24},{18,26},{24,28},{26,30},{28,20... | collective-permute-start | bytes 1179656 | tf_op jit(solution)/shard_map/ppermute | solution.py:91
  194.2 112.9 %collective-permute-start.12 = (bf16[64,3072]{1,0:T(8,128)(2,1)S(1)}, bf16[64,3072]{1,0:T(8,128)(2,1)S(1)}, u32[]{:S(2)}, u32[]{:S(2)}) collective-permute-start(bf16[64,3072]{1,0:T(8,128)(2,1)S(1)} %slice.1127), channel_id=1, source_target_pairs={{0,4},{2,6},{8,0},{10,2},{16,8},{18,10},{24,16},{26,18},{28,24},{3... | collective-permute-start | bytes 1179656 | tf_op jit(solution)/shard_map/ppermute | solution.py:92
  199.8 107.3 %collective-permute-start.7 = (bf16[128,3072]{1,0:T(8,128)(2,1)S(1)}, bf16[128,3072]{1,0:T(8,128)(2,1)S(1)}, u32[]{:S(2)}, u32[]{:S(2)}) collective-permute-start(bf16[128,3072]{1,0:T(8,128)(2,1)S(1)} %collective-permute-done.6), channel_id=1, source_target_pairs={{0,2},{2,0},{4,6},{6,4},{8,10},{10,8},{12,14},{14,12},{16,18},{18,... | collective-permute-start | bytes 2359304 | tf_op jit(solution)/shard_map/ppermute | solution.py:74
  346.2 36.8 %collective-permute-start.87 = (bf16[128,2048]{1,0:T(8,128)(2,1)}, bf16[128,2048]{1,0:T(8,128)(2,1)}, u32[]{:S(2)}, u32[]{:S(2)}) collective-permute-start(bf16[128,2048]{1,0:T(8,128)(2,1)} %collective-permute-done.86), channel_id=1, source_target_pairs={{0,2},{2,0},{4,6},{6,4},{8,10},{10,8},{12,14},{14,12},{16,18},{18,... | collective-permute-start | bytes 1572872 | tf_op jit(solution)/shard_map/ppermute | solution.py:74
  370.2 62.5 %collective-permute-start.100 = (bf16[128,2048]{1,0:T(8,128)(2,1)}, bf16[128,2048]{1,0:T(8,128)(2,1)}, u32[]{:S(2)}, u32[]{:S(2)}) collective-permute-start(bf16[128,2048]{1,0:T(8,128)(2,1)} %collective-permute-done.92), channel_id=1, source_target_pairs={{0,2},{2,0},{4,6},{6,4},{8,10},{10,8},{12,14},{14,12},{16,18},{18,... | collective-permute-start | bytes 1572872 | tf_op jit(solution)/shard_map/ppermute | solution.py:74
  374.3 45.6 %collective-permute-start.99 = (bf16[128,2048]{1,0:T(8,128)(2,1)}, bf16[128,2048]{1,0:T(8,128)(2,1)}, u32[]{:S(2)}, u32[]{:S(2)}) collective-permute-start(bf16[128,2048]{1,0:T(8,128)(2,1)} %collective-permute-done.93), channel_id=1, source_target_pairs={{0,2},{2,0},{4,6},{6,4},{8,10},{10,8},{12,14},{14,12},{16,18},{18,... | collective-permute-start | bytes 1572872 | tf_op jit(solution)/shard_map/ppermute | solution.py:74
  433.7 41.2 %collective-permute-start.50 = (bf16[128,2048]{1,0:T(8,128)(2,1)S(1)}, bf16[128,2048]{1,0:T(8,128)(2,1)S(1)}, u32[]{:S(2)}, u32[]{:S(2)}) collective-permute-start(bf16[128,2048]{1,0:T(8,128)(2,1)S(1)} %collective-permute-done.42), channel_id=1, source_target_pairs={{0,2},{2,0},{4,6},{6,4},{8,10},{10,8},{12,14},{14,12},{16,18},{18,... | collective-permute-start | bytes 1572872 | tf_op jit(solution)/shard_map/ppermute | solution.py:74
  475.8 137.3 %collective-permute-start.51 = (bf16[2048,1536]{1,0:T(8,128)(2,1)}, bf16[2048,1536]{1,0:T(8,128)(2,1)S(1)}, u32[]{:S(2)}, u32[]{:S(2)}) collective-permute-start(bf16[2048,1536]{1,0:T(8,128)(2,1)} %bitcast.28), channel_id=1, source_target_pairs={{0,1},{1,0},{2,3},{3,2},{4,5},{5,4},{6,7},{7,6},{8,9},{9,8},{10,11... | collective-permute-start | bytes 18874376 | tf_op jit(solution)/shard_map/ppermute | solution.py:78
  659.8 39.8 %collective-permute-start.119 = (f32[16,128]{1,0:T(8,128)S(1)}, f32[16,128]{1,0:T(8,128)S(1)}, u32[]{:S(2)}, u32[]{:S(2)}) collective-permute-start(f32[16,128]{1,0:T(8,128)S(1)} %get-tuple-element.212), channel_id=1, source_target_pairs={{0,2},{2,0},{4,6},{6,4},{8,10},{10,8},{12,14},{14,12},{16,18},{18,... | collective-permute-start | bytes 24584 | tf_op jit(solution)/shard_map/ppermute | solution.py:74
  660.2 50.9 %collective-permute-start.118 = (f32[16,128]{1,0:T(8,128)S(1)}, f32[16,128]{1,0:T(8,128)S(1)}, u32[]{:S(2)}, u32[]{:S(2)}) collective-permute-start(f32[16,128]{1,0:T(8,128)S(1)} %get-tuple-element.213), channel_id=1, source_target_pairs={{0,2},{2,0},{4,6},{6,4},{8,10},{10,8},{12,14},{14,12},{16,18},{18,... | collective-permute-start | bytes 24584 | tf_op jit(solution)/shard_map/ppermute | solution.py:74
  660.3 51.5 %collective-permute-start.128 = (f32[16,128]{1,0:T(8,128)S(1)}, f32[16,128]{1,0:T(8,128)S(1)}, u32[]{:S(2)}, u32[]{:S(2)}) collective-permute-start(f32[16,128]{1,0:T(8,128)S(1)} %get-tuple-element.207), channel_id=1, source_target_pairs={{0,2},{2,0},{4,6},{6,4},{8,10},{10,8},{12,14},{14,12},{16,18},{18,... | collective-permute-start | bytes 24584 | tf_op jit(solution)/shard_map/ppermute | solution.py:74
  843.0 198.1 %collective-permute-start.170 = (bf16[2048,1536]{0,1:T(8,128)(2,1)}, bf16[2048,1536]{0,1:T(8,128)(2,1)}, u32[]{:S(2)}, u32[]{:S(2)}) collective-permute-start(bf16[2048,1536]{0,1:T(8,128)(2,1)} %pad_maximum_fusion.1), channel_id=1, source_target_pairs={{0,1},{1,0},{2,3},{3,2},{4,5},{5,4},{6,7},{7,6},{8,9},{9,8},{10,11... | collective-permute-start | bytes 18874376 | tf_op jit(solution)/shard_map/ppermute | solution.py:78
  844.7 169.6 %all-to-all-start.2 = ((bf16[16,8,2048]{2,1,0:T(8,128)(2,1)}), bf16[16,8,2048]{2,1,0:T(8,128)(2,1)}, u32[]{:S(2)}, u32[]{:S(2)}) async-start(bf16[16,8,2048]{2,1,0:T(8,128)(2,1)} %get-tuple-element.177), calls=%async_computation.2 | async-start | bytes 1048576 | tf_op jit(solution)/shard_map/all_to_all | solution.py:478
  873.7 108.4 %collective-permute-start.134 = (f32[2,256]{1,0:T(2,128)S(1)}, f32[2,256]{1,0:T(2,128)S(1)}, u32[]{:S(2)}, u32[]{:S(2)}) collective-permute-start(f32[2,256]{1,0:T(2,128)S(1)} %pad_maximum_fusion.27), channel_id=1, source_target_pairs={{0,1},{1,0},{2,3},{3,2},{4,5},{5,4},{6,7},{7,6},{8,9},{9,8},{10,11... | collective-permute-start | bytes 6152 | tf_op jit(solution)/shard_map/ppermute | solution.py:78
  1049.4 286.2 %all-to-all-start.5 = ((bf16[16,128,1536]{1,2,0:T(8,128)(2,1)}), bf16[16,128,1536]{1,2,0:T(8,128)(2,1)}, u32[]{:S(2)}, u32[]{:S(2)}) async-start(bf16[16,128,1536]{1,2,0:T(8,128)(2,1)} %copy_bitcast_fusion), calls=%async_computation.5 | async-start | bytes 12582912 | tf_op jit(solution)/shard_map/all_to_all | solution.py:166
  1057.8 142.1 %collective-permute-start.143 = (bf16[64,3072]{1,0:T(8,128)(2,1)S(1)}, bf16[64,3072]{1,0:T(8,128)(2,1)S(1)}, u32[]{:S(2)}, u32[]{:S(2)}) collective-permute-start(bf16[64,3072]{1,0:T(8,128)(2,1)S(1)} %get-tuple-element.190), channel_id=1, source_target_pairs={{0,8},{2,10},{8,16},{10,18},{16,24},{18,26},{24,28},{26,30},{28,20... | collective-permute-start | bytes 1179656 | tf_op jit(solution)/shard_map/ppermute | solution.py:108
  1059.0 146.4 %collective-permute-start.140 = (bf16[128,3072]{1,0:T(8,128)(2,1)S(1)}, bf16[128,3072]{1,0:T(8,128)(2,1)S(1)}, u32[]{:S(2)}, u32[]{:S(2)}) collective-permute-start(bf16[128,3072]{1,0:T(8,128)(2,1)S(1)} %copy-done.41), channel_id=1, source_target_pairs={{0,2},{2,0},{4,6},{6,4},{8,10},{10,8},{12,14},{14,12},{16,18},{18,... | collective-permute-start | bytes 2359304 | tf_op jit(solution)/shard_map/ppermute | solution.py:74
  1204.9 39.4 %collective-permute-start.139 = (bf16[128,3072]{1,0:T(8,128)(2,1)S(1)}, bf16[128,3072]{1,0:T(8,128)(2,1)S(1)}, u32[]{:S(2)}, u32[]{:S(2)}) collective-permute-start(bf16[128,3072]{1,0:T(8,128)(2,1)S(1)} %copy-done.40), channel_id=1, source_target_pairs={{0,2},{2,0},{4,6},{6,4},{8,10},{10,8},{12,14},{14,12},{16,18},{18,... | collective-permute-start | bytes 2359304 | tf_op jit(solution)/shard_map/ppermute | solution.py:74
  1205.5 38.9 %collective-permute-start.149 = (bf16[128,3072]{1,0:T(8,128)(2,1)S(1)}, bf16[128,3072]{1,0:T(8,128)(2,1)S(1)}, u32[]{:S(2)}, u32[]{:S(2)}) collective-permute-start(bf16[128,3072]{1,0:T(8,128)(2,1)S(1)} %copy-done.39), channel_id=1, source_target_pairs={{0,2},{2,0},{4,6},{6,4},{8,10},{10,8},{12,14},{14,12},{16,18},{18,... | collective-permute-start | bytes 2359304 | tf_op jit(solution)/shard_map/ppermute | solution.py:74
  1287.8 42.2 %collective-permute-start.138 = (bf16[128,3072]{1,0:T(8,128)(2,1)S(1)}, bf16[128,3072]{1,0:T(8,128)(2,1)S(1)}, u32[]{:S(2)}, u32[]{:S(2)}) collective-permute-start(bf16[128,3072]{1,0:T(8,128)(2,1)S(1)} %get-tuple-element.130), channel_id=1, source_target_pairs={{0,2},{2,0},{4,6},{6,4},{8,10},{10,8},{12,14},{14,12},{16,18},{18,... | collective-permute-start | bytes 2359304 | tf_op jit(solution)/shard_map/ppermute | solution.py:74
  (283 other events, 6057.3 us)
Sparse Core Ops, SparseCore 0:
  16.8 2.8 sort.12.cloned.1.call-done
  (1 shorter events, 0.0 us)

commit v2 on v1

--- a/solution.py
+++ b/solution.py
@@ -1,6 +1,8 @@
 import jax
 import jax.numpy as jnp
 from jax import lax
+from jax.experimental import pallas as pl
+from jax.experimental.pallas import tpu as pltpu
 from jax.sharding import PartitionSpec as P
 
 HEAD_DIM = 128
@@ -49,24 +51,70 @@
     return grads * cosine_table[:, None, :] + turned
 
 
+class Wire:
+    def __init__(self, depth):
+        self.depth = depth
+        self.sent = []
+
+    def __call__(self, values, axis, pairs):
+        if len(self.sent) >= self.depth:
+            values, _ = lax.optimization_barrier((values, self.sent[-self.depth]))
+        self.sent.append(lax.ppermute(values, axis, pairs))
+        return self.sent[-1]
+
+
+def weave(*transfers):
+    results = [None] * len(transfers)
+    going = list(enumerate(transfers))
+    while going:
+        still = []
+        for number, transfer in going:
+            try:
+                next(transfer)
+                still.append((number, transfer))
+            except StopIteration as ended:
+                results[number] = ended.value
+        going = still
+    return results
+
+
 def ring_chip(place, chips):
     return 2 * place if place < chips // 2 else 2 * (chips - 1 - place) + 1
 
 
-def ring_pairs(chips, step):
+def core_index():
+    return lax.axis_index("dp") % 2
+
+
+def flow_pairs(chips):
     pairs = []
     for first in range(0, lax.axis_size("dp"), 2 * chips):
         for place in range(chips):
             here = ring_chip(place, chips)
-            there = ring_chip((place + step) % chips, chips)
-            for core in range(2):
+            for core, step in ((0, 1), (1, -1)):
+                there = ring_chip((place + step) % chips, chips)
                 pairs.append((first + 2 * here + core, first + 2 * there + core))
     return pairs
 
 
-def ring_place(chips):
+def ring_order(chips):
     chip = (lax.axis_index("dp") // 2) % chips
-    return jnp.where(chip % 2 == 0, chip // 2, chips - 1 - chip // 2)
+    place = jnp.where(chip % 2 == 0, chip // 2, chips - 1 - chip // 2)
+    toward = jnp.where(core_index() == 0, -1, 1)
+    offsets = [0]
+    for step in range(1, chips // 2):
+        offsets += [toward * step, -toward * step]
+    offsets.append(chips // 2)
+    places = [lax.rem(place + offset + chips, chips) for offset in offsets]
+    return jnp.stack(
+        [jnp.where(at < chips // 2, 2 * at, 2 * (chips - 1 - at) + 1) for at in places]
+    )
+
+
+def ring_order_back(chips):
+    order = ring_order(chips)
+    numbers = jnp.arange(chips, dtype=order.dtype)
+    return jnp.sum(jnp.where(order[None, :] == numbers[:, None], numbers[None, :], 0), 1)
 
 
 def to_sibling(values):
@@ -74,96 +122,117 @@
     return lax.ppermute(values, "dp", pairs)
 
 
-def to_peer(values):
-    return lax.ppermute(values, "tensor", [(0, 1), (1, 0)])
-
-
-def ring_gather(block, chips):
-    upward, downward = ring_pairs(chips, 1), ring_pairs(chips, -1)
-    lane = [block] + [None] * (chips - 1)
-    rising = falling = block
-    for step in range(1, chips // 2):
-        rising = lax.ppermute(rising, "dp", upward)
-        falling = lax.ppermute(falling, "dp", downward)
-        lane[chips - step] = rising
-        lane[step] = falling
-    half = block.shape[0] // 2
-    rising = lax.ppermute(rising[:half], "dp", upward)
-    falling = lax.ppermute(falling[half:], "dp", downward)
-    lane[chips // 2] = jnp.concatenate([rising, falling], 0)
-    return [(mine, to_sibling(mine)) for mine in lane]
-
-
-def ring_scatter(parts, chips, wire):
-    upward, downward = ring_pairs(chips, 1), ring_pairs(chips, -1)
-    total = [None] * chips
-    half_way = chips // 2
-    farthest_first = [half_way]
-    for step in range(half_way - 1, 0, -1):
-        farthest_first += [step, chips - step]
-    for offset in farthest_first + [0]:
-        mine, other = parts[offset]
-        total[offset] = mine.astype(F32) + to_sibling(other.astype(wire)).astype(F32)
-    half = total[0].shape[0] // 2
-    rising = lax.ppermute(total[half_way][:half].astype(wire), "dp", upward)
-    falling = lax.ppermute(total[half_way][half:].astype(wire), "dp", downward)
-    for step in range(half_way - 1, -1, -1):
-        above, below = total[step], total[(chips - step) % chips]
-        rising, falling = rising.astype(F32), falling.astype(F32)
-        if step == half_way - 1:
-            pad = jnp.zeros_like(rising)
-            rising = jnp.concatenate([rising, pad], 0)
-            falling = jnp.concatenate([pad, falling], 0)
-        if step == 0:
-            return above + rising + falling
-        rising = lax.ppermute((above + rising).astype(wire), "dp", upward)
-        falling = lax.ppermute((below + falling).astype(wire), "dp", downward)
-
-
-def roll_columns(values, start):
-    width = values.shape[1]
-    return lax.dynamic_slice_in_dim(jnp.concatenate([values, values], 1), start, width, 1)
-
-
-def swap_cores(values, chips):
-    rows, width = values.shape
-    piece = width // (2 * chips)
-    pieces = [values[:, at * piece : (at + 1) * piece] for at in range(2 * chips)]
-    swapped = jnp.concatenate([pieces[at ^ 1] for at in range(2 * chips)], 1)
-    return jnp.where(lax.axis_index("dp") % 2 == 0, values, swapped)
-
-
-def to_ring_order(values, chips):
-    piece = values.shape[1] // chips
-    order = [ring_chip(place, chips) for place in range(chips)]
-    placed = jnp.concatenate([values[:, at * piece : (at + 1) * piece] for at in order], 1)
-    return swap_cores(roll_columns(placed, ring_place(chips) * piece), chips)
-
-
-def from_ring_order(values, chips):
-    piece = values.shape[1] // chips
-    order = [ring_chip(place, chips) for place in range(chips)]
-    back = [order.index(chip) for chip in range(chips)]
-    place = ring_place(chips)
-    placed = roll_columns(swap_cores(values, chips), lax.rem(chips - place, chips) * piece)
-    return jnp.concatenate([placed[:, at * piece : (at + 1) * piece] for at in back], 1)
-
-
-def stacked(pairs):
-    return jnp.concatenate([block for pair in pairs for block in pair], 0)
-
-
-def unstacked(values, chips):
-    size = values.shape[0] // (2 * chips)
-    pieces = [values[at * size : (at + 1) * size] for at in range(2 * chips)]
-    return [(pieces[2 * at], pieces[2 * at + 1]) for at in range(chips)]
-
-
-def expert_exchange(chunks):
-    count = lax.axis_size("dp")
-    groups = [list(range(at, at + EXPERTS)) for at in range(0, count, EXPERTS)]
-    kwargs = {} if len(groups) == 1 else {"axis_index_groups": groups}
-    return lax.all_to_all(chunks, "dp", split_axis=0, concat_axis=0, tiled=True, **kwargs)
+def to_peer(wire, values):
+    return wire(values, "tensor", [(0, 1), (1, 0)])
+
+
+def by_core(mine, sibling, axis=0):
+    return jnp.where(
+        core_index() == 0,
+        jnp.concatenate([mine, sibling], axis),
+        jnp.concatenate([sibling, mine], axis),
+    )
+
+
+def core_part(values, core):
+    size = values.shape[0] // 2
+    return lax.dynamic_slice_in_dim(values, core * size, size, 0)
+
+
+def ring_gather(wire, block, chips):
+    core, pairs = core_index(), flow_pairs(chips)
+    flow = by_core(block, to_sibling(block))
+    gathered = [flow]
+    for _ in range(1, chips // 2):
+        flow = wire(flow, "dp", pairs)
+        gathered += [flow, to_sibling(flow)]
+        yield
+    flow = wire(core_part(flow, core), "dp", pairs)
+    yield
+    gathered.append(by_core(flow, to_sibling(flow)))
+    return gathered
+
+
+def ring_scatter(wire, parts, chips, kind):
+    core, pairs = core_index(), flow_pairs(chips)
+    theirs = to_sibling(core_part(parts[-1], 1 - core).astype(kind)).astype(F32)
+    flow = wire((core_part(parts[-1], core) + theirs).astype(kind), "dp", pairs)
+    yield
+    none = jnp.zeros_like(flow)
+    flow = by_core(flow, none).astype(F32)
+    for step in range(chips // 2 - 1, 0, -1):
+        theirs = to_sibling(parts[2 * step - 1].astype(kind)).astype(F32)
+        flow = wire((parts[2 * step] + theirs + flow).astype(kind), "dp", pairs).astype(F32)
+        yield
+    total = parts[0] + flow
+    theirs = to_sibling(core_part(total, 1 - core).astype(kind)).astype(F32)
+    return core_part(total, core) + theirs
+
+
+def pieces_of(values, count, axis=0):
+    size = values.shape[axis] // count
+    return [lax.slice_in_dim(values, at * size, (at + 1) * size, axis=axis) for at in range(count)]
+
+
+def columns_in(values, order, count):
+    size = values.shape[1] // count
+    blocks = [lax.dynamic_slice_in_dim(values, order[at] * size, size, 1) for at in range(count)]
+    return jnp.concatenate(blocks, 1)
+
+
+def pack_kernel(place_ref, gate_ref, up_ref, down_ref, own_ref, sibling_ref):
+    width = gate_ref.shape[2]
+    for out_ref, core in ((own_ref, place_ref[1]), (sibling_ref, 1 - place_ref[1])):
+        out_ref[0, :, :width] = gate_ref[core].astype(BF16)
+        out_ref[0, :, width : 2 * width] = up_ref[core].astype(BF16)
+        out_ref[0, :, 2 * width :] = down_ref[core].T.astype(BF16)
+
+
+def pack_experts(place, gate_weight, up_weight, down_weight):
+    count, shard, width = gate_weight.shape
+    side_in = pl.BlockSpec((2, shard, width), lambda k, p: (p[0] ^ k, 0, 0))
+    down_in = pl.BlockSpec((2, width, shard), lambda k, p: (p[0] ^ k, 0, 0))
+    out = pl.BlockSpec((1, shard, 3 * width), lambda k, p: (k, 0, 0))
+    return pl.pallas_call(
+        pack_kernel,
+        grid_spec=pltpu.PrefetchScalarGridSpec(
+            num_scalar_prefetch=1,
+            grid=(count // 2,),
+            in_specs=[side_in, side_in, down_in],
+            out_specs=[out, out],
+        ),
+        out_shape=[jax.ShapeDtypeStruct((count // 2, shard, 3 * width), BF16)] * 2,
+    )(place, gate_weight, up_weight, down_weight)
+
+
+def unpack_kernel(place_ref, own_ref, sibling_ref, gate_ref, up_ref, down_ref):
+    width = gate_ref.shape[2]
+    for chunk, core in ((own_ref[0, 0], place_ref[1]), (sibling_ref[0], 1 - place_ref[1])):
+        chunk = chunk.astype(F32)
+        gate_ref[core] = chunk[:, :width]
+        up_ref[core] = chunk[:, width : 2 * width]
+        down_ref[core] = chunk[:, 2 * width :].T
+
+
+def unpack_experts(place, own, sibling):
+    chips, _, shard, width = own.shape
+    width = width // 3
+    side_out = pl.BlockSpec((2, shard, width), lambda k, p: (p[0] ^ k, 0, 0))
+    down_out = pl.BlockSpec((2, width, shard), lambda k, p: (p[0] ^ k, 0, 0))
+    sides = jax.ShapeDtypeStruct((2 * chips, shard, width), F32)
+    return pl.pallas_call(
+        unpack_kernel,
+        grid_spec=pltpu.PrefetchScalarGridSpec(
+            num_scalar_prefetch=1,
+            grid=(chips,),
+            in_specs=[
+                pl.BlockSpec((1, 1, shard, 3 * width), lambda k, p: (k, p[1], 0, 0)),
+                pl.BlockSpec((1, shard, 3 * width), lambda k, p: (k, 0, 0)),
+            ],
+            out_specs=[side_out, side_out, down_out],
+        ),
+        out_shape=[sides, sides, jax.ShapeDtypeStruct((2 * chips, width, shard), F32)],
+    )(place, own, sibling)
 
 
 def body(
@@ -196,6 +265,9 @@
     moe_chips = EXPERTS // 2
     replicas = groups // EXPERTS
     expert = lax.rem(me, EXPERTS)
+    expert_chip, core = expert // 2, core_index()
+    expert_place = jnp.stack([expert_chip, core]).astype(jnp.int32)
+    long_wire, side_wire = Wire(3), Wire(2)
 
     dealt = dealing.reshape(groups, rows_here)
     places = jnp.arange(rows_here, dtype=jnp.int32)
@@ -238,7 +310,8 @@
             router_weight.reshape(-1),
         ]
     ).astype(BF16)
-    small = lax.all_gather(small[None], "dp", axis=0, tiled=True)
+    small = jnp.broadcast_to(small[None], (groups, small.shape[0]))
+    small = lax.all_to_all(small, "dp", split_axis=0, concat_axis=0, tiled=True)
     shard = attention_gain.shape[0]
     gain_shard = query_gain.shape[1]
     first_gain = small[:, :shard].reshape(-1).astype(F32)
@@ -248,25 +321,32 @@
     key_scale_gain = small[:, at + gain_shard : at + 2 * gain_shard].reshape(-1).astype(F32)
     router_full = small[:, at + 2 * gain_shard :].reshape(model_width, EXPERTS)
 
+    norm_one = row_scale(rows)
+    normed_own = (rows * norm_one * first_gain).astype(BF16)
+    normed_peer = to_peer(side_wire, normed_own)
+
+    hidden_half = gate_weight.shape[2]
+    packed_own, packed_sibling = pack_experts(expert_place, gate_weight, up_weight, down_weight)
+    packed_experts = by_core(packed_own, to_sibling(packed_sibling), 1)
+    across = [list(range(at, groups, EXPERTS)) for at in range(EXPERTS)]
+    own_chunks = [packed_experts[0]] + [None] * (moe_chips - 1)
+    peer_chunks = [None] * moe_chips
+
+    def chip_pairs(step):
+        return [(index, index ^ (2 * step)) for index in range(groups)]
+
+    def fetch_experts(steps):
+        for step in steps:
+            if step > 0:
+                own_chunks[step] = long_wire(packed_experts[step], "dp", chip_pairs(step))
+            peer_chunks[step] = to_peer(side_wire, own_chunks[step])
+            yield
+
     qkv_block = jnp.concatenate([query_weight, key_weight, value_weight], 1).astype(BF16)
-    qkv_full = stacked(ring_gather(qkv_block, chips))
-    output_full = stacked(ring_gather(output_weight.T.astype(BF16), chips))
+    qkv_full, _ = weave(ring_gather(long_wire, qkv_block, chips), fetch_experts([0, 4, 1, 6, 2]))
+    qkv_full = jnp.concatenate(qkv_full, 0)
     heads_width = query_weight.shape[1]
-
-    expert_block = jnp.concatenate(
-        [gate_weight.astype(BF16), up_weight.astype(BF16), down_weight.astype(BF16).swapaxes(1, 2)],
-        2,
-    )
-    hidden_half = gate_weight.shape[2]
-    expert_own = expert_exchange(expert_block).reshape(-1, 3 * hidden_half)
-    across = [list(range(at, groups, EXPERTS)) for at in range(EXPERTS)]
-    if replicas > 1:
-        expert_own = lax.all_gather(
-            expert_own, "dp", axis=0, tiled=True, axis_index_groups=across
-        )
-    expert_peer = to_peer(expert_own)
-
-    cot_all = stacked(ring_gather(cot_rows, moe_chips))
+    order, order_back = ring_order(chips), ring_order_back(chips)
 
     finish_at = jnp.cumsum(lengths[0])
     start_at = finish_at - lengths[0]
@@ -284,20 +364,21 @@
     reorder = (own_order[:half_rows, None] == places[None, :]).astype(BF16)
     used = mm(reorder, uses.astype(BF16))
 
-    norm_one = row_scale(rows)
-    normed_own = (rows * norm_one * first_gain).astype(BF16)
-    normed_one = to_ring_order(jnp.concatenate([normed_own, to_peer(normed_own)], 0), chips)
+    normed_one = columns_in(jnp.concatenate([normed_own, normed_peer], 0), order, chips)
     qkv = mm(normed_one, qkv_full)
     query_raw, key_raw = qkv[:, :heads_width], qkv[:, heads_width : 2 * heads_width]
     value_rows = qkv[:, 2 * heads_width :].astype(BF16)
 
     def over_sides(values):
-        theirs = to_peer(values)
+        theirs = to_peer(side_wire, values)
         return values + jnp.concatenate([theirs[:, half_rows:], theirs[:, :half_rows]], 1)
 
     squares = over_sides(
         jnp.stack([jnp.sum(query_raw * query_raw, -1), jnp.sum(key_raw * key_raw, -1)])
     )
+    output_block = output_weight.T.astype(BF16)
+    output_full, _ = weave(ring_gather(long_wire, output_block, chips), fetch_experts([5]))
+    output_full = jnp.concatenate(output_full, 0)
     query_scale = lax.rsqrt(squares[0] / model_width + EPS)[:, None]
     key_scale = lax.rsqrt(squares[1] / model_width + EPS)[:, None]
     heads_here = heads_width // HEAD_DIM
@@ -329,8 +410,11 @@
     )
     context = context.reshape(rows_here, -1).astype(BF16)
     attention = outer_cols(context, output_full)
-    attention = attention[:half_rows] + to_peer(attention[half_rows:].astype(BF16)).astype(F32)
-    hidden = rows + from_ring_order(attention, chips)
+    attention = attention[:half_rows] + to_peer(
+        side_wire, attention[half_rows:].astype(BF16)
+    ).astype(F32)
+    weave(fetch_experts([3, 7]))
+    hidden = rows + columns_in(attention, order_back, chips)
 
     norm_two = row_scale(hidden)
     normed_two = (hidden * norm_two * second_gain).astype(BF16)
@@ -339,9 +423,37 @@
     router_probs = powered_two / jnp.sum(powered_two, -1, keepdims=True)
     gate_table = (router_probs * used).T
 
-    inputs_all = stacked(ring_gather(normed_two, moe_chips))
-    gate_blocks = jnp.stack([b for pair in ring_gather(gate_table, moe_chips) for b in pair])
-    gates = lax.dynamic_index_in_dim(gate_blocks, expert, 1, keepdims=False).reshape(-1, 1)
+    inputs_all, cot_all = (
+        jnp.concatenate(weave(ring_gather(long_wire, block, moe_chips))[0], 0)
+        for block in (normed_two, cot_rows)
+    )
+    moe_order, moe_order_back = ring_order(moe_chips), ring_order_back(moe_chips)
+
+    def to_experts(table):
+        kwargs = {}
+        if replicas > 1:
+            kwargs["axis_index_groups"] = [
+                list(range(at, at + EXPERTS)) for at in range(0, groups, EXPERTS)
+            ]
+        return lax.all_to_all(table, "dp", split_axis=0, concat_axis=0, tiled=True, **kwargs)
+
+    gates = to_experts(gate_table).reshape(moe_chips, -1)
+    gates = jnp.take(gates, moe_order, axis=0).reshape(-1, 1)
+
+    def placed(chunks):
+        size, width = chunks[0].shape
+        whole = jnp.zeros((moe_chips * size, width), chunks[0].dtype)
+        for step, chunk in enumerate(chunks):
+            at = (expert_chip ^ step) * size
+            whole = lax.dynamic_update_slice_in_dim(whole, chunk, at, 0)
+        return whole
+
+    expert_own, expert_peer = placed(own_chunks), placed(peer_chunks)
+    if replicas > 1:
+        expert_own, expert_peer = (
+            lax.all_gather(part, "dp", axis=0, tiled=True, axis_index_groups=across)
+            for part in (expert_own, expert_peer)
+        )
     out_cells = (cot_all.astype(F32) * gates).astype(BF16)
     halves = []
     for weights in (expert_own, expert_peer):
@@ -363,23 +475,43 @@
         for active, grad, _ in halves
     ]
 
-    normed_two_grad = ring_scatter(unstacked(input_grad, moe_chips), moe_chips, BF16)
-    mine = (expert_ids == expert).astype(F32)[None, :, None]
-    mixing_table = (mixing.reshape(EXPERTS, 1, half_rows) * mine).reshape(-1, half_rows)
-    mixing_table = ring_scatter(unstacked(mixing_table, moe_chips), moe_chips, F32)
-    mixture = ring_scatter(unstacked(produced * gates, moe_chips), moe_chips, BF16)
+    normed_two_grad = weave(
+        ring_scatter(long_wire, pieces_of(input_grad, moe_chips), moe_chips, BF16)
+    )[0]
+    mixing_table = jnp.take(mixing.reshape(moe_chips, -1), moe_order_back, axis=0)
+    mixing_table = to_experts(mixing_table.reshape(EXPERTS, -1))
+    mixture = weave(
+        ring_scatter(long_wire, pieces_of(produced * gates, moe_chips), moe_chips, BF16)
+    )[0]
     out_rows = (hidden + mixture).astype(BF16)
 
-    expert_wgrad = expert_wgrads[0] + to_peer(expert_wgrads[1].astype(BF16)).astype(F32)
-    expert_wgrad = expert_wgrad.astype(BF16)
+    wgrad_own, wgrad_peer = expert_wgrads[0], expert_wgrads[1].astype(BF16)
     if replicas > 1:
-        expert_wgrad = lax.psum_scatter(
-            expert_wgrad, "dp", scatter_dimension=0, tiled=True, axis_index_groups=across
+        wgrad_own, wgrad_peer = (
+            lax.psum_scatter(
+                part.astype(BF16), "dp", scatter_dimension=0, tiled=True, axis_index_groups=across
+            )
+            for part in (wgrad_own, wgrad_peer)
         )
-    wgrads = expert_exchange(expert_wgrad.reshape(EXPERTS, -1, 3 * hidden_half))
-    gate_weight_grad = wgrads[:, :, :hidden_half].astype(F32)
-    up_weight_grad = wgrads[:, :, hidden_half : 2 * hidden_half].astype(F32)
-    down_weight_grad = wgrads[:, :, 2 * hidden_half :].swapaxes(1, 2).astype(F32)
+    chip_rows = wgrad_own.shape[0] // moe_chips
+
+    def wgrad_chunk(values, step):
+        return lax.dynamic_slice_in_dim(values, (expert_chip ^ step) * chip_rows, chip_rows, 0)
+
+    summed_chunks, wgrad_chunks = [None] * moe_chips, [None] * moe_chips
+
+    def sum_wgrads(steps):
+        for step in steps:
+            theirs = to_peer(side_wire, wgrad_chunk(wgrad_peer, step)).astype(F32)
+            chunk = wgrad_chunk(wgrad_own, step).astype(F32) + theirs
+            summed_chunks[step] = chunk.astype(BF16)
+
+    def return_wgrads(steps):
+        for step in steps:
+            wgrad_chunks[step] = long_wire(summed_chunks[step], "dp", chip_pairs(step))
+            yield
+
+    sum_wgrads([4, 1, 6, 2, 5])
 
     prob_grad = mixing_table.T * used
     logit_grad = (
@@ -394,9 +526,13 @@
     )
 
     attn_own = hidden_grad.astype(BF16)
-    attn_grad = to_ring_order(jnp.concatenate([attn_own, to_peer(attn_own)], 0), chips)
-    output_wgrad = inner_rows(attn_grad, context)
-    output_wgrad = ring_scatter(unstacked(output_wgrad, chips), chips, BF16)
+    attn_peer = to_peer(side_wire, attn_own)
+    sum_wgrads([3, 7, 0])
+    attn_grad = columns_in(jnp.concatenate([attn_own, attn_peer], 0), order, chips)
+    output_wgrad = pieces_of(inner_rows(attn_grad, context), chips)
+    output_wgrad, _ = weave(
+        ring_scatter(long_wire, output_wgrad, chips, BF16), return_wgrads([4, 1, 6, 2])
+    )
     context_grad = mm(attn_grad, output_full).astype(BF16)
     context_grad = context_grad.reshape(rows_here, heads_here, HEAD_DIM)
     recomputed = jnp.exp(attention_scores(query_heads, key_heads) - log_total)
@@ -440,14 +576,21 @@
         - key_raw * key_scale**3 * inners[1][:, None] / model_width
     ).astype(BF16)
     qkv_grad = jnp.concatenate([query_raw_grad, key_raw_grad, value_grad], 1)
-    qkv_wgrad = ring_scatter(
-        unstacked(inner_rows(normed_one, qkv_grad), chips), chips, BF16
+    qkv_wgrad = pieces_of(inner_rows(normed_one, qkv_grad), chips)
+    qkv_wgrad, _ = weave(
+        ring_scatter(long_wire, qkv_wgrad, chips, BF16), return_wgrads([5, 3, 7])
+    )
+    wgrad_chunks[0] = summed_chunks[0]
+    returned = jnp.stack(wgrad_chunks).reshape(moe_chips, 2, -1, 3 * hidden_half)
+    of_sibling = to_sibling(lax.dynamic_index_in_dim(returned, 1 - core, 1, keepdims=False))
+    gate_weight_grad, up_weight_grad, down_weight_grad = unpack_experts(
+        expert_place, returned, of_sibling
     )
     normed_one_grad = outer_cols(qkv_grad, qkv_full)
     normed_one_grad = normed_one_grad[:half_rows] + to_peer(
-        normed_one_grad[half_rows:].astype(BF16)
+        side_wire, normed_one_grad[half_rows:].astype(BF16)
     ).astype(F32)
-    normed_one_grad = from_ring_order(normed_one_grad, chips)
+    normed_one_grad = columns_in(normed_one_grad, order_back, chips)
     attention_gain_grad = jnp.sum(normed_one_grad * rows * norm_one, 0)
     scaled_one = normed_one_grad * first_gain
     rows_grad = hidden_grad + norm_one * (
@@ -469,7 +612,7 @@
     )
     at = 2 * gain_shard
     by_rows = small_grad[at:]
-    by_rows = by_rows + to_peer(by_rows)
+    by_rows = by_rows + to_peer(side_wire, by_rows)
 
     place_back = (places[:, None] == leaving[None, :]).astype(BF16)
 
@@ -477,7 +620,7 @@
         back = values.reshape(groups, half_peer, model_width)
         back = lax.all_to_all(back, "dp", split_axis=0, concat_axis=0, tiled=True)
         back = back.reshape(half_rows, model_width)
-        return mm(place_back, jnp.concatenate([back, to_peer(back)], 0)).astype(BF16)
+        return mm(place_back, jnp.concatenate([back, to_peer(side_wire, back)], 0)).astype(BF16)
 
     return (
         send_back(out_rows),

time: 1390 us -> 1140 us (0.82); the launches traced: 1360 us -> 1130 us
  waiting for transfers between devices: 684 us -> 440 us
  blocking collectives: 30.9 us -> 0 us
  local copies, waits for them, and re-layouts: 109 us -> 137 us
  starting transfers between devices: 205 us -> 181 us
  Pallas kernels: 0 us -> 19.5 us
  other arithmetic: 101 us -> 119 us
    ppermute x91 -> x71, waiting for transfers between devices: 672 us -> 416 us  [__call__(): self.sent.append(lax.ppermute(values, axis, pairs))]
    all_gather x1 -> x0, blocking collectives: 30.9 us -> none  [body(): small = lax.all_gather(small[None], 'dp', axis=0, tiled=True)]
    ppermute x80 -> x42, starting transfers between devices: 84.2 us -> 53.8 us  [to_sibling(): return lax.ppermute(values, 'dp', pairs)]
    dynamic_update_slice x0 -> x16, local copies, waits for them, and re-layouts: none -> 25.9 us  [placed(): whole = lax.dynamic_update_slice_in_dim(whole, chunk, at, 0)]
    pallas_call x0 -> x2, Pallas kernels: none -> 19.5 us  [the longest x1 9.96 us: pack_experts(): pl.pallas_call(pack_kernel, grid_spec=pltpu.PrefetchScalarGridSpec(num_sc...]
    unnamed x432 -> x302, local copies, waits for them, and re-layouts: 67.7 us -> 50.2 us
    unnamed x25 -> x24, other arithmetic: 1.41 us -> 16.3 us
    convert_element_type x24 -> x19, other arithmetic: 36.4 us -> 48.3 us  [the longest x12 36.6 us: ring_scatter(): (parts[2 * step] + theirs + flow).astype(kind)]
  transfers between devices with their start and end apart: 177 -> 120, of which waited for: 51 -> 47; matrix products, arithmetic and copies ran while one was open for 25% -> 35% of each run, Pallas kernels for 0% -> 1%
where the time goes in v2:
time: 1140 us; the launch traced here: 1130 us
  waiting for transfers between devices  440 us (39%)
  matrix products  211 us (19%)
  starting transfers between devices  181 us (16%)
  local copies, waits for them, and re-layouts  137 us (12%)
  other arithmetic  119 us (10%)
  between operations  21.9 us (2%)
  Pallas kernels  19.5 us (2%)
    ppermute x71, waiting for transfers between devices, __call__(): self.sent.append(lax.ppermute(values, axis, pairs))  416 us
    ppermute x71, starting transfers between devices, __call__(): self.sent.append(lax.ppermute(values, axis, pairs))  77.3 us
    dot_general x7, matrix products, outer_cols(): lax.dot_general(left, right, (((1,), (1,)), ((), ())), preferred_element_...  73.3 us
    dot_general x12, matrix products, mm(): lax.dot_general(left, right, (((1,), (0,)), ((), ())), preferred_element_...  69.2 us
    dot_general x7, matrix products, inner_rows(): lax.dot_general(left, right, (((0,), (0,)), ((), ())), preferred_element_...  60 us
    ppermute x42, starting transfers between devices, to_sibling(): return lax.ppermute(values, 'dp', pairs)  53.8 us
    unnamed x302, local copies, waits for them, and re-layouts  50.2 us
    convert_element_type x12, other arithmetic, ring_scatter(): (parts[2 * step] + theirs + flow).astype(kind)  36.6 us
  transfers between devices with their start and end apart: 120, of which 47 were waited for; matrix products, arithmetic and copies ran while one was open for 35% of the time, Pallas kernels for 1%

profile of v2, /device:TPU:17, one launch (start us, length us, event | category | flops | bytes accessed | tf_op | source)
XLA Modules:
  0.0 1130.7 jit_solution(17811227640714728134)
XLA Ops:
  27.8 10.0 shard_map.272
  57.1 10.4 constant_dynamic-update-slice_fusion.14
  82.0 15.1 %collective-permute-done.2 = bf16[256,3072]{1,0:T(8,128)(2,1)} collective-permute-done((bf16[256,3072]{1,0:T(8,128)(2,1)S(1)}, bf16[256,3072]{1,0:T(8,128)(2,1)}, u32[]{:S(2)}, u32[]{:S(2)}) %collective-permute-start.2) | collective-permute-done | bytes 1572896 | tf_op jit(solution)/shard_map/ppermute | solution.py:62
  129.1 13.3 %collective-permute-done.19 = bf16[256,1536]{1,0:T(8,128)(2,1)S(1)} collective-permute-done((bf16[256,1536]{1,0:T(8,128)(2,1)S(1)}, bf16[256,1536]{1,0:T(8,128)(2,1)S(1)}, u32[]{:S(2)}, u32[]{:S(2)}) %collective-permute-start.19) | collective-permute-done | bytes 786464 | tf_op jit(solution)/shard_map/ppermute | solution.py:62
  144.9 14.7 %collective-permute-done.6 = bf16[256,3072]{1,0:T(8,128)(2,1)S(1)} collective-permute-done((bf16[256,3072]{1,0:T(8,128)(2,1)S(1)}, bf16[256,3072]{1,0:T(8,128)(2,1)S(1)}, u32[]{:S(2)}, u32[]{:S(2)}) %collective-permute-start.6) | collective-permute-done | bytes 1572896 | tf_op jit(solution)/shard_map/ppermute | solution.py:62
  159.7 10.2 collective-permute-done.9
  202.2 28.8 %collective-permute-done.12 = bf16[256,1536]{1,0:T(8,128)(2,1)S(1)} collective-permute-done((bf16[256,1536]{1,0:T(8,128)(2,1)S(1)}, bf16[256,1536]{1,0:T(8,128)(2,1)S(1)}, u32[]{:S(2)}, u32[]{:S(2)}) %collective-permute-start.12) | collective-permute-done | bytes 786464 | tf_op jit(solution)/shard_map/ppermute | solution.py:62
  250.2 16.3 %collective-permute-done.14 = bf16[256,1536]{1,0:T(8,128)(2,1)S(1)} collective-permute-done((bf16[256,1536]{1,0:T(8,128)(2,1)S(1)}, bf16[256,1536]{1,0:T(8,128)(2,1)S(1)}, u32[]{:S(2)}, u32[]{:S(2)}) %collective-permute-start.14) | collective-permute-done | bytes 786464 | tf_op jit(solution)/shard_map/ppermute | solution.py:62
  336.1 18.2 %collective-permute-done.35 = bf16[256,1536]{1,0:T(8,128)(2,1)} collective-permute-done((bf16[256,1536]{1,0:T(8,128)(2,1)S(1)}, bf16[256,1536]{1,0:T(8,128)(2,1)}, u32[]{:S(2)}, u32[]{:S(2)}) %collective-permute-start.35) | collective-permute-done | bytes 786464 | tf_op jit(solution)/shard_map/ppermute | solution.py:62
  425.3 13.6 %fusion.4 = f32[2048,1024]{0,1:T(8,128)} fusion(bf16[2048,2048]{1,0:T(8,128)(2,1)} %fusion.89, bf16[2048,1536]{1,0:T(8,128)(2,1)S(1)} %bitcast.270), kind=kOutput, calls=%fused_computation.55 | convolution fusion | flops 8589934592 | bytes 20971520 | tf_op jit(solution)/shard_map/dot_general | solution.py:22
  442.7 14.6 %fusion.7 = f32[2048,1024]{0,1:T(8,128)} fusion(bf16[2048,2048]{1,0:T(8,128)(2,1)} %fusion.89, bf16[2048,1536]{1,0:T(8,128)(2,1)} %constant_dynamic-update-slice_fusion.93), kind=kOutput, calls=%fused_computation.58 | convolution fusion | flops 8589934592 | bytes 20971520 | tf_op jit(solution)/shard_map/dot_general | solution.py:22
  461.4 13.7 %multiply_convert_fusion.1 = (bf16[2048,512]{0,1:T(8,128)(2,1)}, bf16[2048,512]{0,1:T(8,128)(2,1)}, bf16[2048,512]{0,1:T(8,128)(2,1)}) fusion(f32[2048,1024]{0,1:T(8,128)} %fusion.4, bf16[2048,1536]{1,0:T(8,128)(2,1)S(1)} %bitcast.270, bf16[2048,2048]{1,0:T(8,128)(2,1)S(1)} %fusion.90, f32[2048]{0:T(1024)S(1)} %bitcast.290), kind=kOutput, calls=%fused_computation.45 | convolution fusion | flops 4324327424 | bytes 25174016 | tf_op jit(solution)/shard_map/dot_general | solution.py:22
  475.1 12.6 %convolution_convert_fusion = bf16[2048,1024]{0,1:T(8,128)(2,1)S(1)} fusion(bf16[2048,2048]{1,0:T(8,128)(2,1)} %fusion.89, bf16[2048,512]{0,1:T(8,128)(2,1)} %get-tuple-element.269, bf16[2048,512]{0,1:T(8,128)(2,1)} %get-tuple-element.268), kind=kOutput, calls=%fused_computation.52 | convolution fusion | flops 8600420352 | bytes 16777216 | tf_op jit(solution)/shard_map/dot_general | solution.py:26
  487.8 16.8 %fusion.2 = f32[2048,2048]{1,0:T(8,128)} fusion(bf16[2048,1536]{1,0:T(8,128)(2,1)} %constant_dynamic-update-slice_fusion.85, bf16[2048,512]{0,1:T(8,128)(2,1)} %get-tuple-element.269, bf16[2048,512]{0,1:T(8,128)(2,1)S(1)} %copy-done.108), kind=kOutput, calls=%fused_computation.53 | convolution fusion | flops 8598323200 | bytes 25165824 | tf_op jit(solution)/shard_map/dot_general | solution.py:30
  509.5 9.8 fusion.33
  523.2 11.7 %multiply_convert_fusion.3 = (bf16[2048,512]{0,1:T(8,128)(2,1)}, bf16[2048,512]{0,1:T(8,128)(2,1)}, bf16[2048,512]{0,1:T(8,128)(2,1)}) fusion(f32[2048,1024]{0,1:T(8,128)} %fusion.7, bf16[2048,1536]{1,0:T(8,128)(2,1)} %constant_dynamic-update-slice_fusion.93, bf16[2048,2048]{1,0:T(8,128)(2,1)S(1)} %fusion.90, f32[2048]{0:T(1024)S(1)} %bitcast.292), kind=kOutput, calls=%fused_computation.47 | convolution fusion | flops 4324327424 | bytes 25174016 | tf_op jit(solution)/shard_map/dot_general | solution.py:22
  534.9 19.0 %fusion.198 = (bf16[2048,2048]{1,0:T(8,128)(2,1)}, f32[2048,2048]{1,0:T(8,128)}) fusion(f32[2048,2048]{1,0:T(8,128)} %fusion.2, bf16[2048,1536]{1,0:T(8,128)(2,1)} %constant_dynamic-update-slice_fusion.93, bf16[2048,512]{0,1:T(8,128)(2,1)} %get-tuple-element.267, bf16[2048,512]{0,1:T(8,128)(2,1)} %get-tuple-element.266), kind=kOutput, calls=%fused_computation.561 | convolution fusion | flops 8606711808 | bytes 50331648 | tf_op jit(solution)/shard_map/dot_general | solution.py:30
  562.4 19.4 %fusion.183 = (bf16[2048,2048]{1,0:T(8,128)(2,1)}, f32[2048,2048]{1,0:T(8,128)}, f32[2048]{0:T(1024)S(1)}) fusion(f32[2048]{0:T(1024)S(1)} %bitcast.293, bf16[2048,2048]{1,0:T(8,128)(2,1)} %copy-done.6, f32[2048,2048]{1,0:T(8,128)} %fusion.33, bf16[2048,512]{0,1:T(8,128)(2,1)} %get-tuple-element.276, ...), kind=kOutput, calls=%fused_computation.546 | convolution fusion | flops 4320131072 | bytes 54542336 | tf_op jit(solution)/shard_map/dot_general | solution.py:30
  623.6 12.2 %fusion.15 = f32[2048,1024]{0,1:T(8,128)} fusion(bf16[2048,2048]{1,0:T(8,128)(2,1)S(1)} %bitcast.296, bf16[2048,512]{0,1:T(8,128)(2,1)S(1)} %copy-done.107, bf16[2048,512]{0,1:T(8,128)(2,1)S(1)} %copy-done.106), kind=kOutput, calls=%fused_computation.72 | convolution fusion | flops 8598323200 | bytes 20971520 | tf_op jit(solution)/shard_map/dot_general | solution.py:26
  669.7 9.8 collective-permute-done.73
  679.8 16.6 %collective-permute-done.81 = bf16[256,1536]{0,1:T(8,128)(2,1)S(1)} collective-permute-done((bf16[256,1536]{0,1:T(8,128)(2,1)}, bf16[256,1536]{0,1:T(8,128)(2,1)S(1)}, u32[]{:S(2)}, u32[]{:S(2)}) %collective-permute-start.81) | collective-permute-done | bytes 786464 | tf_op jit(solution)/shard_map/ppermute | solution.py:62
  714.1 16.1 %collective-permute-done.82 = bf16[256,1536]{0,1:T(8,128)(2,1)} collective-permute-done((bf16[256,1536]{0,1:T(8,128)(2,1)S(1)}, bf16[256,1536]{0,1:T(8,128)(2,1)}, u32[]{:S(2)}, u32[]{:S(2)}) %collective-permute-start.82) | collective-permute-done | bytes 786464 | tf_op jit(solution)/shard_map/ppermute | solution.py:62
  735.6 12.4 %all-to-all-start.3 = ((bf16[16,8,2048]{2,1,0:T(8,128)(2,1)}), bf16[16,8,2048]{2,1,0:T(8,128)(2,1)}, u32[]{:S(2)}, u32[]{:S(2)}) async-start(bf16[16,8,2048]{2,1,0:T(8,128)(2,1)} %get-tuple-element.301), calls=%async_computation.3 | async-start | bytes 1048576 | tf_op jit(solution)/shard_map/all_to_all | solution.py:621
  806.2 14.2 %fusion.199 = (bf16[2048,3072]{1,0:T(8,128)(2,1)}, f32[2048,3072]{1,0:T(8,128)}) fusion(bf16[256,2048]{1,0:T(8,128)(2,1)S(1)} %copy-done.35, bf16[256,1024]{1,0:T(8,128)(2,1)S(1)} %copy-done.33, bf16[256,1024]{1,0:T(8,128)(2,1)S(1)} %get-tuple-element.298, bf16[256,1024]{1,0:T(8,128)(2,1)S(1)} %get-tuple-element.297), kind=kOutput, calls=%fused_computation.562 | convolution fusion | flops 3232235520 | bytes 40370176 | tf_op jit(solution)/shard_map/dot_general | solution.py:26
  835.3 50.5 %collective-permute-done.95 = bf16[256,1536]{0,1:T(8,128)(2,1)S(1)} collective-permute-done((bf16[256,1536]{0,1:T(8,128)(2,1)S(1)}, bf16[256,1536]{0,1:T(8,128)(2,1)S(1)}, u32[]{:S(2)}, u32[]{:S(2)}) %collective-permute-start.95) | collective-permute-done | bytes 786464 | tf_op jit(solution)/shard_map/ppermute | solution.py:62
  885.9 13.6 %collective-permute-done.98 = bf16[256,1536]{0,1:T(8,128)(2,1)S(1)} collective-permute-done((bf16[256,1536]{0,1:T(8,128)(2,1)S(1)}, bf16[256,1536]{0,1:T(8,128)(2,1)S(1)}, u32[]{:S(2)}, u32[]{:S(2)}) %collective-permute-start.98) | collective-permute-done | bytes 786464 | tf_op jit(solution)/shard_map/ppermute | solution.py:62
  904.6 10.3 collective-permute-done.99
  922.3 13.6 %collective-permute-done.100 = bf16[256,1536]{0,1:T(8,128)(2,1)S(1)} collective-permute-done((bf16[256,1536]{0,1:T(8,128)(2,1)S(1)}, bf16[256,1536]{0,1:T(8,128)(2,1)S(1)}, u32[]{:S(2)}, u32[]{:S(2)}) %collective-permute-start.100) | collective-permute-done | bytes 786464 | tf_op jit(solution)/shard_map/ppermute | solution.py:62
  945.0 16.3 %collective-permute-done.104 = bf16[256,1024]{1,0:T(8,128)(2,1)} collective-permute-done((bf16[256,1024]{1,0:T(8,128)(2,1)S(1)}, bf16[256,1024]{1,0:T(8,128)(2,1)}, u32[]{:S(2)}, u32[]{:S(2)}) %collective-permute-start.104) | collective-permute-done | bytes 524320 | tf_op jit(solution)/shard_map/ppermute | solution.py:62
  974.7 23.6 %collective-permute-done.105 = bf16[256,1536]{0,1:T(8,128)(2,1)} collective-permute-done((bf16[256,1536]{0,1:T(8,128)(2,1)}, bf16[256,1536]{0,1:T(8,128)(2,1)}, u32[]{:S(2)}, u32[]{:S(2)}) %collective-permute-start.105) | collective-permute-done | bytes 786464 | tf_op jit(solution)/shard_map/ppermute | solution.py:62
  1027.1 11.3 %all-to-all-done.5 = bf16[16,8,2048]{2,1,0:T(8,128)(2,1)} async-done(((bf16[16,8,2048]{2,1,0:T(8,128)(2,1)}), bf16[16,8,2048]{2,1,0:T(8,128)(2,1)}, u32[]{:S(2)}, u32[]{:S(2)}) %all-to-all-start.5) | async-done | bytes 524320 | tf_op jit(solution)/shard_map/all_to_all | solution.py:621
  1058.5 21.2 %collective-permute-done.111 = bf16[256,1536]{0,1:T(8,128)(2,1)S(1)} collective-permute-done((bf16[256,1536]{0,1:T(8,128)(2,1)}, bf16[256,1536]{0,1:T(8,128)(2,1)S(1)}, u32[]{:S(2)}, u32[]{:S(2)}) %collective-permute-start.111) | collective-permute-done | bytes 786464 | tf_op jit(solution)/shard_map/ppermute | solution.py:62
  (789 shorter events, 598.9 us)
Async XLA Ops:
  22.5 50.5 %collective-permute-start.16 = (bf16[128,1024]{1,0:T(8,128)(2,1)}, bf16[128,1024]{1,0:T(8,128)(2,1)}, u32[]{:S(2)}, u32[]{:S(2)}) collective-permute-start(bf16[128,1024]{1,0:T(8,128)(2,1)} %bitcast.215), channel_id=1, source_target_pairs={{0,2},{2,0},{4,6},{6,4},{8,10},{10,8},{12,14},{14,12},{16,18},{18,... | collective-permute-start | bytes 786440 | tf_op jit(solution)/shard_map/ppermute | solution.py:122
  37.8 81.0 %collective-permute-start.8 = (bf16[8,128,1536]{2,1,0:T(8,128)(2,1)}, bf16[8,128,1536]{2,1,0:T(8,128)(2,1)}, u32[]{:S(2)}, u32[]{:S(2)}) collective-permute-start(bf16[8,128,1536]{2,1,0:T(8,128)(2,1)} %get-tuple-element.88), channel_id=1, source_target_pairs={{0,2},{2,0},{4,6},{6,4},{8,10},{10,8},{12,14},{14,12},{16,18},{18,... | collective-permute-start | bytes 9437192 | tf_op jit(solution)/shard_map/ppermute | solution.py:122
  100.7 74.4 %collective-permute-start.3 = (bf16[256,3072]{1,0:T(8,128)(2,1)}, bf16[256,3072]{1,0:T(8,128)(2,1)S(1)}, u32[]{:S(2)}, u32[]{:S(2)}) collective-permute-start(bf16[256,3072]{1,0:T(8,128)(2,1)} %collective-permute-done.2), channel_id=1, source_target_pairs={{0,2},{2,0},{4,6},{6,4},{8,10},{10,8},{12,14},{14,12},{16,18},{18,... | collective-permute-start | bytes 4718600 | tf_op jit(solution)/shard_map/ppermute | solution.py:122
  116.9 42.7 %collective-permute-start.6 = (bf16[256,3072]{1,0:T(8,128)(2,1)S(1)}, bf16[256,3072]{1,0:T(8,128)(2,1)S(1)}, u32[]{:S(2)}, u32[]{:S(2)}) collective-permute-start(bf16[256,3072]{1,0:T(8,128)(2,1)S(1)} %collective-permute-done.4), channel_id=1, source_target_pairs={{0,8},{2,6},{8,16},{10,2},{16,24},{18,10},{24,28},{26,18},{28,20},... | collective-permute-start | bytes 4718600 | tf_op jit(solution)/shard_map/ppermute | solution.py:62
  125.4 44.4 %collective-permute-start.9 = (bf16[256,1536]{1,0:T(8,128)(2,1)S(1)}, bf16[256,1536]{1,0:T(8,128)(2,1)S(1)}, u32[]{:S(2)}, u32[]{:S(2)}) collective-permute-start(bf16[256,1536]{1,0:T(8,128)(2,1)S(1)} %get-tuple-element.293), channel_id=1, source_target_pairs={{0,16},{2,18},{4,20},{6,22},{8,24},{10,26},{12,28},{14,30},{16,0},... | collective-permute-start | bytes 2359304 | tf_op jit(solution)/shard_map/ppermute | solution.py:62
  127.9 46.0 %collective-permute-start.40 = (bf16[256,1536]{1,0:T(8,128)(2,1)S(1)}, bf16[256,1536]{1,0:T(8,128)(2,1)S(1)}, u32[]{:S(2)}, u32[]{:S(2)}) collective-permute-start(bf16[256,1536]{1,0:T(8,128)(2,1)S(1)} %get-tuple-element.286), channel_id=1, source_target_pairs={{0,1},{1,0},{2,3},{3,2},{4,5},{5,4},{6,7},{7,6},{8,9},{9,8},{10,11... | collective-permute-start | bytes 2359304 | tf_op jit(solution)/shard_map/ppermute | solution.py:62
  142.4 54.4 %collective-permute-start.5 = (bf16[256,3072]{1,0:T(8,128)(2,1)S(1)}, bf16[256,3072]{1,0:T(8,128)(2,1)S(1)}, u32[]{:S(2)}, u32[]{:S(2)}) collective-permute-start(bf16[256,3072]{1,0:T(8,128)(2,1)S(1)} %collective-permute-done.4), channel_id=1, source_target_pairs={{0,2},{2,0},{4,6},{6,4},{8,10},{10,8},{12,14},{14,12},{16,18},{18,... | collective-permute-start | bytes 4718600 | tf_op jit(solution)/shard_map/ppermute | solution.py:122
  175.1 59.6 %collective-permute-start.7 = (bf16[256,3072]{1,0:T(8,128)(2,1)S(1)}, bf16[256,3072]{1,0:T(8,128)(2,1)S(1)}, u32[]{:S(2)}, u32[]{:S(2)}) collective-permute-start(bf16[256,3072]{1,0:T(8,128)(2,1)S(1)} %collective-permute-done.6), channel_id=1, source_target_pairs={{0,2},{2,0},{4,6},{6,4},{8,10},{10,8},{12,14},{14,12},{16,18},{18,... | collective-permute-start | bytes 4718600 | tf_op jit(solution)/shard_map/ppermute | solution.py:122
  183.1 49.1 %collective-permute-start.13 = (bf16[256,1536]{1,0:T(8,128)(2,1)S(1)}, bf16[256,1536]{1,0:T(8,128)(2,1)S(1)}, u32[]{:S(2)}, u32[]{:S(2)}) collective-permute-start(bf16[256,1536]{1,0:T(8,128)(2,1)S(1)} %collective-permute-done.9), channel_id=1, source_target_pairs={{0,1},{1,0},{2,3},{3,2},{4,5},{5,4},{6,7},{7,6},{8,9},{9,8},{10,11... | collective-permute-start | bytes 2359304 | tf_op jit(solution)/shard_map/ppermute | solution.py:62
  187.6 43.4 %collective-permute-start.12 = (bf16[256,1536]{1,0:T(8,128)(2,1)S(1)}, bf16[256,1536]{1,0:T(8,128)(2,1)S(1)}, u32[]{:S(2)}, u32[]{:S(2)}) collective-permute-start(bf16[256,1536]{1,0:T(8,128)(2,1)S(1)} %get-tuple-element.90), channel_id=1, source_target_pairs={{0,24},{2,26},{4,28},{6,30},{8,16},{10,18},{12,20},{14,22},{16,8},... | collective-permute-start | bytes 2359304 | tf_op jit(solution)/shard_map/ppermute | solution.py:62
  196.9 41.4 %collective-permute-start.11 = (bf16[128,3072]{1,0:T(8,128)(2,1)S(1)}, bf16[128,3072]{1,0:T(8,128)(2,1)S(1)}, u32[]{:S(2)}, u32[]{:S(2)}) collective-permute-start(bf16[128,3072]{1,0:T(8,128)(2,1)S(1)} %collective-permute-done.10), channel_id=1, source_target_pairs={{0,2},{2,0},{4,6},{6,4},{8,10},{10,8},{12,14},{14,12},{16,18},{18,... | collective-permute-start | bytes 2359304 | tf_op jit(solution)/shard_map/ppermute | solution.py:122
  231.0 71.3 %collective-permute-start.42 = (bf16[256,1536]{1,0:T(8,128)(2,1)}, bf16[256,1536]{1,0:T(8,128)(2,1)}, u32[]{:S(2)}, u32[]{:S(2)}) collective-permute-start(bf16[256,1536]{1,0:T(8,128)(2,1)} %collective-permute-done.20), channel_id=1, source_target_pairs={{0,1},{1,0},{2,3},{3,2},{4,5},{5,4},{6,7},{7,6},{8,9},{9,8},{10,11... | collective-permute-start | bytes 2359304 | tf_op jit(solution)/shard_map/ppermute | solution.py:62
  234.6 48.7 %collective-permute-start.25 = (bf16[256,1536]{1,0:T(8,128)(2,1)}, bf16[256,1536]{1,0:T(8,128)(2,1)}, u32[]{:S(2)}, u32[]{:S(2)}) collective-permute-start(bf16[256,1536]{1,0:T(8,128)(2,1)} %get-tuple-element.99), channel_id=1, source_target_pairs={{0,20},{2,22},{4,16},{6,18},{8,28},{10,30},{12,24},{14,26},{16,4},... | collective-permute-start | bytes 2359304 | tf_op jit(solution)/shard_map/ppermute | solution.py:62
  238.2 51.5 %collective-permute-start.18 = (bf16[256,1024]{1,0:T(8,128)(2,1)}, bf16[256,1024]{1,0:T(8,128)(2,1)}, u32[]{:S(2)}, u32[]{:S(2)}) collective-permute-start(bf16[256,1024]{1,0:T(8,128)(2,1)} %collective-permute-done.17), channel_id=1, source_target_pairs={{0,2},{2,0},{4,6},{6,4},{8,10},{10,8},{12,14},{14,12},{16,18},{18,... | collective-permute-start | bytes 1572872 | tf_op jit(solution)/shard_map/ppermute | solution.py:122
  327.1 45.1 %collective-permute-start.44 = (bf16[256,1536]{1,0:T(8,128)(2,1)}, bf16[256,1536]{1,0:T(8,128)(2,1)}, u32[]{:S(2)}, u32[]{:S(2)}) collective-permute-start(bf16[256,1536]{1,0:T(8,128)(2,1)} %collective-permute-done.32), channel_id=1, source_target_pairs={{0,1},{1,0},{2,3},{3,2},{4,5},{5,4},{6,7},{7,6},{8,9},{9,8},{10,11... | collective-permute-start | bytes 2359304 | tf_op jit(solution)/shard_map/ppermute | solution.py:62
  412.1 45.2 %collective-permute-start.52 = (bf16[256,2048]{1,0:T(8,128)(2,1)}, bf16[256,2048]{1,0:T(8,128)(2,1)S(1)}, u32[]{:S(2)}, u32[]{:S(2)}) collective-permute-start(bf16[256,2048]{1,0:T(8,128)(2,1)} %collective-permute-done.51), channel_id=1, source_target_pairs={{0,2},{2,0},{4,6},{6,4},{8,10},{10,8},{12,14},{14,12},{16,18},{18,... | collective-permute-start | bytes 3145736 | tf_op jit(solution)/shard_map/ppermute | solution.py:122
  521.9 82.8 %collective-permute-start.78 = (bf16[256,1536]{0,1:T(8,128)(2,1)}, bf16[256,1536]{0,1:T(8,128)(2,1)}, u32[]{:S(2)}, u32[]{:S(2)}) collective-permute-start(bf16[256,1536]{0,1:T(8,128)(2,1)} %get-tuple-element.130), channel_id=1, source_target_pairs={{0,1},{1,0},{2,3},{3,2},{4,5},{5,4},{6,7},{7,6},{8,9},{9,8},{10,11... | collective-permute-start | bytes 2359304 | tf_op jit(solution)/shard_map/ppermute | solution.py:62
  560.1 51.9 %collective-permute-start.67 = (bf16[256,2048]{1,0:T(8,128)(2,1)}, bf16[256,2048]{1,0:T(8,128)(2,1)S(1)}, u32[]{:S(2)}, u32[]{:S(2)}) collective-permute-start(bf16[256,2048]{1,0:T(8,128)(2,1)} %get-tuple-element.273), channel_id=1, source_target_pairs={{0,2},{2,0},{4,6},{6,4},{8,10},{10,8},{12,14},{14,12},{16,18},{18,... | collective-permute-start | bytes 3145736 | tf_op jit(solution)/shard_map/ppermute | solution.py:122
  604.8 41.4 %collective-permute-start.47 = (bf16[256,2048]{1,0:T(8,128)(2,1)}, bf16[256,2048]{1,0:T(8,128)(2,1)}, u32[]{:S(2)}, u32[]{:S(2)}) collective-permute-start(bf16[256,2048]{1,0:T(8,128)(2,1)} %get-tuple-element.272), channel_id=1, source_target_pairs={{0,2},{2,0},{4,6},{6,4},{8,10},{10,8},{12,14},{14,12},{16,18},{18,... | collective-permute-start | bytes 3145736 | tf_op jit(solution)/shard_map/ppermute | solution.py:122
  735.6 226.9 %all-to-all-start.3 = ((bf16[16,8,2048]{2,1,0:T(8,128)(2,1)}), bf16[16,8,2048]{2,1,0:T(8,128)(2,1)}, u32[]{:S(2)}, u32[]{:S(2)}) async-start(bf16[16,8,2048]{2,1,0:T(8,128)(2,1)} %get-tuple-element.301), calls=%async_computation.3 | async-start | bytes 1048576 | tf_op jit(solution)/shard_map/all_to_all | solution.py:621
  782.0 158.2 %collective-permute-start.102 = (bf16[256,1024]{1,0:T(8,128)(2,1)}, bf16[256,1024]{1,0:T(8,128)(2,1)}, u32[]{:S(2)}, u32[]{:S(2)}) collective-permute-start(bf16[256,1024]{1,0:T(8,128)(2,1)} %get-tuple-element.294), channel_id=1, source_target_pairs={{0,2},{2,0},{4,6},{6,4},{8,10},{10,8},{12,14},{14,12},{16,18},{18,... | collective-permute-start | bytes 1572872 | tf_op jit(solution)/shard_map/ppermute | solution.py:122
  783.7 45.2 %collective-permute-start.97 = (bf16[256,1024]{1,0:T(8,128)(2,1)}, bf16[256,1024]{1,0:T(8,128)(2,1)S(1)}, u32[]{:S(2)}, u32[]{:S(2)}) collective-permute-start(bf16[256,1024]{1,0:T(8,128)(2,1)} %get-tuple-element.295), channel_id=1, source_target_pairs={{0,2},{2,0},{4,6},{6,4},{8,10},{10,8},{12,14},{14,12},{16,18},{18,... | collective-permute-start | bytes 1572872 | tf_op jit(solution)/shard_map/ppermute | solution.py:122
  789.6 152.4 %collective-permute-start.103 = (bf16[256,1536]{0,1:T(8,128)(2,1)}, bf16[256,1536]{0,1:T(8,128)(2,1)}, u32[]{:S(2)}, u32[]{:S(2)}) collective-permute-start(bf16[256,1536]{0,1:T(8,128)(2,1)} %get-tuple-element.147), channel_id=1, source_target_pairs={{0,4},{2,6},{4,0},{6,2},{8,12},{10,14},{12,8},{14,10},{16,20},{18,... | collective-permute-start | bytes 2359304 | tf_op jit(solution)/shard_map/ppermute | solution.py:62
  827.4 89.9 %collective-permute-start.89 = (bf16[256,3072]{1,0:T(8,128)(2,1)S(1)}, bf16[256,3072]{1,0:T(8,128)(2,1)S(1)}, u32[]{:S(2)}, u32[]{:S(2)}) collective-permute-start(bf16[256,3072]{1,0:T(8,128)(2,1)S(1)} %get-tuple-element.264), channel_id=1, source_target_pairs={{0,2},{2,0},{4,6},{6,4},{8,10},{10,8},{12,14},{14,12},{16,18},{18,... | collective-permute-start | bytes 4718600 | tf_op jit(solution)/shard_map/ppermute | solution.py:122
  832.7 53.1 %collective-permute-start.95 = (bf16[256,1536]{0,1:T(8,128)(2,1)S(1)}, bf16[256,1536]{0,1:T(8,128)(2,1)S(1)}, u32[]{:S(2)}, u32[]{:S(2)}) collective-permute-start(bf16[256,1536]{0,1:T(8,128)(2,1)S(1)} %get-tuple-element.141), channel_id=1, source_target_pairs={{0,24},{2,26},{4,28},{6,30},{8,16},{10,18},{12,20},{14,22},{16,8},... | collective-permute-start | bytes 2359304 | tf_op jit(solution)/shard_map/ppermute | solution.py:62
  833.9 65.6 %collective-permute-start.98 = (bf16[256,1536]{0,1:T(8,128)(2,1)S(1)}, bf16[256,1536]{0,1:T(8,128)(2,1)S(1)}, u32[]{:S(2)}, u32[]{:S(2)}) collective-permute-start(bf16[256,1536]{0,1:T(8,128)(2,1)S(1)} %get-tuple-element.143), channel_id=1, source_target_pairs={{0,16},{2,18},{4,20},{6,22},{8,24},{10,26},{12,28},{14,30},{16,0},... | collective-permute-start | bytes 2359304 | tf_op jit(solution)/shard_map/ppermute | solution.py:62
  915.0 130.6 %collective-permute-start.87 = (bf16[256,3072]{1,0:T(8,128)(2,1)}, bf16[256,3072]{1,0:T(8,128)(2,1)}, u32[]{:S(2)}, u32[]{:S(2)}) collective-permute-start(bf16[256,3072]{1,0:T(8,128)(2,1)} %get-tuple-element.263), channel_id=1, source_target_pairs={{0,2},{2,0},{4,6},{6,4},{8,10},{10,8},{12,14},{14,12},{16,18},{18,... | collective-permute-start | bytes 4718600 | tf_op jit(solution)/shard_map/ppermute | solution.py:122
  917.2 52.7 %collective-permute-start.88 = (bf16[256,3072]{1,0:T(8,128)(2,1)}, bf16[256,3072]{1,0:T(8,128)(2,1)}, u32[]{:S(2)}, u32[]{:S(2)}) collective-permute-start(bf16[256,3072]{1,0:T(8,128)(2,1)} %get-tuple-element.265), channel_id=1, source_target_pairs={{0,2},{2,0},{4,6},{6,4},{8,10},{10,8},{12,14},{14,12},{16,18},{18,... | collective-permute-start | bytes 4718600 | tf_op jit(solution)/shard_map/ppermute | solution.py:122
  998.3 47.3 %collective-permute-start.106 = (bf16[256,3072]{1,0:T(8,128)(2,1)}, bf16[256,3072]{1,0:T(8,128)(2,1)}, u32[]{:S(2)}, u32[]{:S(2)}) collective-permute-start(bf16[256,3072]{1,0:T(8,128)(2,1)} %fusion.12), channel_id=1, source_target_pairs={{0,8},{2,6},{8,16},{10,2},{16,24},{18,10},{24,28},{26,18},{28,20},... | collective-permute-start | bytes 4718600 | tf_op jit(solution)/shard_map/ppermute | solution.py:62
  1011.8 93.2 %collective-permute-start.84 = (bf16[128,2048]{1,0:T(8,128)(2,1)}, bf16[128,2048]{1,0:T(8,128)(2,1)}, u32[]{:S(2)}, u32[]{:S(2)}) collective-permute-start(bf16[128,2048]{1,0:T(8,128)(2,1)} %bitcast.60), channel_id=1, source_target_pairs={{0,1},{1,0},{2,3},{3,2},{4,5},{5,4},{6,7},{7,6},{8,9},{9,8},{10,11... | collective-permute-start | bytes 1572872 | tf_op jit(solution)/shard_map/ppermute | solution.py:62
  1038.4 69.2 %collective-permute-start.86 = (bf16[128,2048]{1,0:T(8,128)(2,1)}, bf16[128,2048]{1,0:T(8,128)(2,1)}, u32[]{:S(2)}, u32[]{:S(2)}) collective-permute-start(bf16[128,2048]{1,0:T(8,128)(2,1)} %bitcast.84), channel_id=1, source_target_pairs={{0,1},{1,0},{2,3},{3,2},{4,5},{5,4},{6,7},{7,6},{8,9},{9,8},{10,11... | collective-permute-start | bytes 1572872 | tf_op jit(solution)/shard_map/ppermute | solution.py:62
  1050.2 46.7 %collective-permute-start.108 = (bf16[256,3072]{1,0:T(8,128)(2,1)}, bf16[256,3072]{1,0:T(8,128)(2,1)}, u32[]{:S(2)}, u32[]{:S(2)}) collective-permute-start(bf16[256,3072]{1,0:T(8,128)(2,1)} %fusion.14), channel_id=1, source_target_pairs={{0,8},{2,6},{8,16},{10,2},{16,24},{18,10},{24,28},{26,18},{28,20},... | collective-permute-start | bytes 4718600 | tf_op jit(solution)/shard_map/ppermute | solution.py:62
  (206 other events, 4898.4 us)
Sparse Core Ops, SparseCore 0:
  10.9 2.8 sort.12.cloned.1.call-done
  (1 shorter events, 0.0 us)

commit v3 on v2

v3 whole, which is shorter than its diff:
```python
import jax
import jax.numpy as jnp
from jax import lax
from jax.experimental import pallas as pl
from jax.experimental.pallas import tpu as pltpu
from jax.sharding import PartitionSpec as P

HEAD_DIM = 128
EXPERTS = 16
EPS = 1e-05
ROPE_BASE = 10000.0
MASKED = -1e30
F32 = jnp.float32
BF16 = jnp.bfloat16


def row_scale(values):
    return lax.rsqrt(jnp.mean(values * values, -1, keepdims=True) + EPS)


def mm(left, right):
    return lax.dot_general(left, right, (((1,), (0,)), ((), ())), preferred_element_type=F32)


def inner_rows(left, right):
    return lax.dot_general(left, right, (((0,), (0,)), ((), ())), preferred_element_type=F32)


def outer_cols(left, right):
    return lax.dot_general(left, right, (((1,), (1,)), ((), ())), preferred_element_type=F32)


def rope_tables(positions, head_size):
    half_size = head_size // 2
    freq_table = ROPE_BASE ** (-2.0 * jnp.arange(half_size, dtype=F32) / head_size)
    angles = positions[:, None] * freq_table[None, :]
    cosines, sines = jnp.cos(angles), jnp.sin(angles)
    return jnp.stack(
        [jnp.concatenate([cosines, cosines], -1), jnp.concatenate([-sines, sines], -1)]
    )


def after(value, *others):
    return lax.optimization_barrier((value, others))[0]


def ring_chip(place, chips):
    return 2 * place if place < chips // 2 else 2 * (chips - 1 - place) + 1


def core_index():
    return lax.axis_index("dp") % 2


def flow_pairs(chips):
    pairs = []
    for first in range(0, lax.axis_size("dp"), 2 * chips):
        for place in range(chips):
            here = ring_chip(place, chips)
            for core, step in ((0, 1), (1, -1)):
                there = ring_chip((place + step) % chips, chips)
                pairs.append((first + 2 * here + core, first + 2 * there + core))
    return pairs


def ring_order(chips):
    chip = (lax.axis_index("dp") // 2) % chips
    place = jnp.where(chip % 2 == 0, chip // 2, chips - 1 - chip // 2)
    toward = jnp.where(core_index() == 0, -1, 1)
    offsets = [0]
    for step in range(1, chips // 2):
        offsets += [toward * step, -toward * step]
    offsets.append(chips // 2)
    places = [lax.rem(place + offset + chips, chips) for offset in offsets]
    return jnp.stack(
        [jnp.where(at < chips // 2, 2 * at, 2 * (chips - 1 - at) + 1) for at in places]
    )


def to_sibling(values):
    pairs = [(index, index ^ 1) for index in range(lax.axis_size("dp"))]
    return lax.ppermute(values, "dp", pairs)


def to_peer(values):
    return lax.ppermute(values, "tensor", [(0, 1), (1, 0)])


def by_core(mine, sibling, axis=0):
    return jnp.where(
        core_index() == 0,
        jnp.concatenate([mine, sibling], axis),
        jnp.concatenate([sibling, mine], axis),
    )


def core_part(values, core):
    size = values.shape[0] // 2
    return lax.dynamic_slice_in_dim(values, core * size, size, 0)


def ring_scatter(parts, chips, kind, waits=()):
    core, pairs = core_index(), flow_pairs(chips)
    parts = [part.astype(F32) for part in parts]
    theirs = to_sibling(core_part(parts[-1], 1 - core).astype(kind)).astype(F32)
    flow = lax.ppermute((core_part(parts[-1], core) + theirs).astype(kind), "dp", pairs)
    none = jnp.zeros_like(flow)
    flow = by_core(flow, none).astype(F32)
    for step in range(chips // 2 - 1, 0, -1):
        theirs = to_sibling(parts[2 * step - 1].astype(kind)).astype(F32)
        flow = after((parts[2 * step] + theirs + flow).astype(kind), *waits[-step:][:1])
        flow = lax.ppermute(flow, "dp", pairs).astype(F32)
    total = parts[0] + flow
    theirs = to_sibling(core_part(total, 1 - core).astype(kind)).astype(F32)
    return core_part(total, core) + theirs


def pieces_of(values, count, axis=0):
    size = values.shape[axis] // count
    return [lax.slice_in_dim(values, at * size, (at + 1) * size, axis=axis) for at in range(count)]


def columns_in(values, order, count):
    size = values.shape[1] // count
    blocks = [lax.dynamic_slice_in_dim(values, order[at] * size, size, 1) for at in range(count)]
    return jnp.concatenate(blocks, 1)


def pack_kernel(place_ref, gate_ref, up_ref, down_ref, own_ref, sibling_ref):
    width = gate_ref.shape[2]
    for out_ref, core in ((own_ref, place_ref[1]), (sibling_ref, 1 - place_ref[1])):
        out_ref[0, :, :width] = gate_ref[core].astype(BF16)
        out_ref[0, :, width : 2 * width] = up_ref[core].astype(BF16)
        out_ref[0, :, 2 * width :] = down_ref[core].T.astype(BF16)


def pack_experts(place, gate_weight, up_weight, down_weight):
    count, shard, width = gate_weight.shape
    side_in = pl.BlockSpec((2, shard, width), lambda k, p: (p[0] ^ k, 0, 0))
    down_in = pl.BlockSpec((2, width, shard), lambda k, p: (p[0] ^ k, 0, 0))
    out = pl.BlockSpec((1, shard, 3 * width), lambda k, p: (k, 0, 0))
    return pl.pallas_call(
        pack_kernel,
        grid_spec=pltpu.PrefetchScalarGridSpec(
            num_scalar_prefetch=1,
            grid=(count // 2,),
            in_specs=[side_in, side_in, down_in],
            out_specs=[out, out],
        ),
        out_shape=[jax.ShapeDtypeStruct((count // 2, shard, 3 * width), BF16)] * 2,
    )(place, gate_weight, up_weight, down_weight)


def merge_kernel(place_ref, own_ref, sibling_ref, out_ref):
    size = own_ref.shape[1]
    for part_ref, core in ((own_ref, place_ref[1]), (sibling_ref, 1 - place_ref[1])):
        out_ref[0, pl.ds(pl.multiple_of(core * size, size), size)] = part_ref[0]


def merge_cores(place, own, sibling):
    chips, size, width = own.shape
    part = pl.BlockSpec((1, size, width), lambda k, p: (k, 0, 0))
    return pl.pallas_call(
        merge_kernel,
        grid_spec=pltpu.PrefetchScalarGridSpec(
            num_scalar_prefetch=1,
            grid=(chips,),
            in_specs=[part, part],
            out_specs=pl.BlockSpec((1, 2 * size, width), lambda k, p: (k, 0, 0)),
        ),
        out_shape=jax.ShapeDtypeStruct((chips, 2 * size, width), own.dtype),
    )(place, own, sibling)


def unpack_kernel(place_ref, own_ref, sibling_ref, gate_ref, up_ref, down_ref):
    width = gate_ref.shape[2]
    own_core = place_ref[pl.num_programs(0)]
    for chunk, core in ((own_ref[0, 0], own_core), (sibling_ref[0], 1 - own_core)):
        chunk = chunk.astype(F32)
        gate_ref[core] = chunk[:, :width]
        up_ref[core] = chunk[:, width : 2 * width]
        down_ref[core] = chunk[:, 2 * width :].T


def unpack_experts(place, own, sibling):
    chips, _, shard, width = own.shape
    width = width // 3
    side_out = pl.BlockSpec((2, shard, width), lambda k, p: (p[k], 0, 0))
    down_out = pl.BlockSpec((2, width, shard), lambda k, p: (p[k], 0, 0))
    sides = jax.ShapeDtypeStruct((2 * chips, shard, width), F32)
    return pl.pallas_call(
        unpack_kernel,
        grid_spec=pltpu.PrefetchScalarGridSpec(
            num_scalar_prefetch=1,
            grid=(chips,),
            in_specs=[
                pl.BlockSpec((1, 1, shard, 3 * width), lambda k, p: (k, p[chips], 0, 0)),
                pl.BlockSpec((1, shard, 3 * width), lambda k, p: (k, 0, 0)),
            ],
            out_specs=[side_out, side_out, down_out],
        ),
        out_shape=[sides, sides, jax.ShapeDtypeStruct((2 * chips, width, shard), F32)],
    )(place, own, sibling)


ROW_VMEM = 48 * 1024 * 1024
LIGHT = pl.CostEstimate(flops=1024, bytes_accessed=1024, transcendentals=0)


def mix_grads(front, active_grad, width):
    gate_pre, up_pre = front[:, :width], front[:, width:]
    sigmoid_gate = 1.0 / (1.0 + jnp.exp(-gate_pre))
    active = (gate_pre * sigmoid_gate * up_pre).astype(BF16)
    gate_grad = active_grad * up_pre * sigmoid_gate * (1.0 + gate_pre * (1.0 - sigmoid_gate))
    up_grad = active_grad * gate_pre * sigmoid_gate
    return active, jnp.concatenate([gate_grad.astype(BF16), up_grad.astype(BF16)], 1)


def rows_kernel(
    expert_ref, rows_ref, cot_ref, use_ref, router_ref, own_ref, peer_ref, *out_refs
):
    grad_ref, active_ref, front_grad_ref, cells_ref, gate_ref = out_refs
    width = own_ref.shape[1] // 3
    logits = mm(rows_ref[...], router_ref[...])
    powered = jnp.exp(logits - jnp.max(logits, -1, keepdims=True))
    router_probs = powered / jnp.sum(powered, -1, keepdims=True)
    numbers = lax.broadcasted_iota(jnp.int32, router_probs.shape, 1)
    gate = jnp.sum(jnp.where(numbers == expert_ref[0], router_probs, 0.0), -1, keepdims=True)
    gate = gate * use_ref[...]
    gate_ref[...] = gate
    cells = (cot_ref[...].astype(F32) * gate).astype(BF16)
    cells_ref[...] = cells
    total = None
    for half, weights_ref in enumerate((own_ref, peer_ref)):
        front = mm(rows_ref[...], weights_ref[:, : 2 * width])
        active_grad = mm(cells, weights_ref[:, 2 * width :])
        active, front_grad = mix_grads(front, active_grad, width)
        active_ref[:, half * width : (half + 1) * width] = active
        front_grad_ref[:, 2 * half * width : 2 * (half + 1) * width] = front_grad
        part = outer_cols(front_grad, weights_ref[:, : 2 * width])
        total = part if total is None else total + part
    grad_ref[...] = total.astype(BF16)


def expert_rows(expert, rows, cot_rows, uses, router, own, peer, tile):
    count, model_width = rows.shape
    width = own.shape[1] // 3
    part = lambda columns: pl.BlockSpec((tile, columns), lambda i, e: (i, 0))
    whole = lambda values: pl.BlockSpec(
        values.shape, lambda i, e: (0, 0), pipeline_mode=pl.Buffered(1)
    )
    outs = (model_width, 2 * width, 4 * width, model_width)
    return pl.pallas_call(
        rows_kernel,
        grid_spec=pltpu.PrefetchScalarGridSpec(
            num_scalar_prefetch=1,
            grid=(count // tile,),
            in_specs=[part(model_width), part(model_width), part(1)]
            + [whole(values) for values in (router, own, peer)],
            out_specs=[part(columns) for columns in outs + (1,)],
        ),
        out_shape=[jax.ShapeDtypeStruct((count, columns), BF16) for columns in outs]
        + [jax.ShapeDtypeStruct((count, 1), F32)],
        compiler_params=pltpu.CompilerParams(vmem_limit_bytes=ROW_VMEM),
        cost_estimate=LIGHT,
    )(expert, rows, cot_rows, uses, router, own, peer)


def mixture_kernel(active_ref, cot_ref, gate_ref, own_ref, peer_ref, mixed_ref, mixing_ref):
    width = own_ref.shape[1]
    produced = outer_cols(active_ref[:, :width], own_ref[...])
    produced = produced + outer_cols(active_ref[:, width:], peer_ref[...])
    mixing_ref[...] = jnp.sum(produced * cot_ref[...].astype(F32), -1, keepdims=True)
    mixed_ref[...] = (produced * gate_ref[...]).astype(BF16)


def expert_mixture(active, cot_rows, gates, own, peer, tile):
    count, model_width = cot_rows.shape
    width = own.shape[1] // 3
    wide = pl.BlockSpec((tile, model_width), lambda i: (i, 0))
    single = pl.BlockSpec((tile, 1), lambda i: (i, 0))
    down = pl.BlockSpec((model_width, width), lambda i: (0, 2), pipeline_mode=pl.Buffered(1))
    return pl.pallas_call(
        mixture_kernel,
        grid=(count // tile,),
        in_specs=[pl.BlockSpec((tile, 2 * width), lambda i: (i, 0)), wide, single, down, down],
        out_specs=[wide, single],
        out_shape=[
            jax.ShapeDtypeStruct((count, model_width), BF16),
            jax.ShapeDtypeStruct((count, 1), F32),
        ],
        compiler_params=pltpu.CompilerParams(vmem_limit_bytes=ROW_VMEM),
        cost_estimate=LIGHT,
    )(active, cot_rows, gates, own, peer)


def wgrad_kernel(
    order_ref, rows_ref, cells_ref, front_grad_ref, active_ref, first_ref, last_ref, own_ref
):
    number, early = pl.program_id(0), 3 * pl.num_programs(0) // 4
    width = active_ref.shape[1] // 2
    front = mm(rows_ref[...].T, front_grad_ref[...]).astype(BF16)
    down = mm(cells_ref[...].T, active_ref[...]).astype(BF16)
    own_ref[0, :, : 2 * width] = front[:, : 2 * width]
    own_ref[0, :, 2 * width :] = down[:, :width]
    for wanted, out_ref in ((number < early, first_ref), (number >= early, last_ref)):

        @pl.when(wanted)
        def _():
            out_ref[0, :, : 2 * width] = front[:, 2 * width :]
            out_ref[0, :, 2 * width :] = down[:, width:]


def expert_wgrads(order, rows, cells, front_grad, active):
    count, model_width = rows.shape
    blocks = order.shape[0]
    early = 3 * blocks // 4
    size, width = model_width // blocks, active.shape[1] // 2
    columns = pl.BlockSpec((count, size), lambda i, o: (0, o[i]))
    whole = lambda values: pl.BlockSpec(
        values.shape, lambda i, o: (0, 0), pipeline_mode=pl.Buffered(1)
    )
    part = (1, size, 3 * width)
    return pl.pallas_call(
        wgrad_kernel,
        grid_spec=pltpu.PrefetchScalarGridSpec(
            num_scalar_prefetch=1,
            grid=(blocks,),
            in_specs=[columns, columns, whole(front_grad), whole(active)],
            out_specs=[
                pl.BlockSpec(part, lambda i, o: (jnp.minimum(i, early - 1), 0, 0)),
                pl.BlockSpec(part, lambda i, o: (jnp.maximum(i - early, 0), 0, 0)),
                pl.BlockSpec(part, lambda i, o: (i, 0, 0)),
            ],
        ),
        out_shape=[
            jax.ShapeDtypeStruct((many, size, 3 * width), BF16) for many in (early, blocks - early, blocks)
        ],
        compiler_params=pltpu.CompilerParams(vmem_limit_bytes=ROW_VMEM),
        cost_estimate=LIGHT,
    )(order, rows, cells, front_grad, active)


def attention_kernel(
    query_ref, key_ref, value_ref, scale_ref, gain_ref, turn_ref, mask_ref, *out_refs
):
    rotated_query_ref, rotated_key_ref, context_ref, log_ref = out_refs
    cosine, sine = turn_ref[0], turn_ref[1]
    rotated = []
    for number, (raw_ref, out_ref) in enumerate(
        ((query_ref, rotated_query_ref), (key_ref, rotated_key_ref))
    ):
        normed = raw_ref[...] * scale_ref[number] * gain_ref[number : number + 1]
        turned = normed * cosine + pltpu.roll(normed, HEAD_DIM // 2, 1) * sine
        rotated.append(turned.astype(BF16))
        out_ref[...] = rotated[number]
    scores = outer_cols(rotated[0], rotated[1]) * HEAD_DIM ** (-0.5)
    scores = jnp.where(mask_ref[...] > 0, scores, MASKED)
    peak_value = jnp.max(scores, -1, keepdims=True)
    powered = jnp.exp(scores - peak_value)
    total_weight = jnp.sum(powered, -1, keepdims=True)
    probs = (powered / total_weight).astype(BF16)
    log_ref[0] = peak_value + jnp.log(total_weight)
    context_ref[...] = mm(probs, value_ref[...].astype(BF16)).astype(BF16)


def attention_grad_kernel(
    query_ref,
    key_ref,
    value_ref,
    scale_ref,
    gain_ref,
    turn_ref,
    mask_ref,
    rotated_query_ref,
    rotated_key_ref,
    log_ref,
    context_grad_ref,
    query_grad_ref,
    key_grad_ref,
    value_grad_ref,
    gain_grad_ref,
    inner_ref,
):
    head_scale = HEAD_DIM ** (-0.5)
    cosine, sine = turn_ref[0], turn_ref[1]
    query, key = rotated_query_ref[...], rotated_key_ref[...]
    scores = outer_cols(query, key) * head_scale
    scores = jnp.where(mask_ref[...] > 0, scores, MASKED)
    probs = jnp.exp(scores - log_ref[0])
    context_grad = context_grad_ref[...]
    probs_grad = outer_cols(context_grad, value_ref[...].astype(BF16))
    value_grad_ref[...] = mm(probs.astype(BF16).T, context_grad).astype(BF16)
    scores_grad = probs * (probs_grad - jnp.sum(probs * probs_grad, -1, keepdims=True))
    scores_grad = scores_grad.astype(BF16)

    @pl.when(pl.program_id(0) == 0)
    def _():
        inner_ref[...] = jnp.zeros_like(inner_ref)

    for number, (raw_ref, grad, out_ref) in enumerate(
        (
            (query_ref, mm(scores_grad, key), query_grad_ref),
            (key_ref, mm(scores_grad.T, query), key_grad_ref),
        )
    ):
        grad = grad * head_scale
        grad = grad * cosine - pltpu.roll(grad, HEAD_DIM // 2, 1) * sine
        out_ref[...] = grad
        raw = raw_ref[...]
        gain_grad_ref[number : number + 1] = jnp.sum(
            grad * raw * scale_ref[number], 0, keepdims=True
        )
        inner_ref[number] += jnp.sum(
            grad * gain_ref[number : number + 1] * raw, -1, keepdims=True
        )


def by_heads(kernel, rows, heads, inputs, extra, outs, log_out):
    column = pl.BlockSpec((rows, HEAD_DIM), lambda h: (0, h))
    at = lambda part: pl.BlockSpec((rows, HEAD_DIM), lambda h: (0, part * heads + h))
    logs = pl.BlockSpec((1, rows, 1), lambda h: (h, 0, 0))
    pair = pl.BlockSpec((2, HEAD_DIM), lambda h: (0, h))
    whole = lambda *shape: pl.BlockSpec(shape, lambda h: (0,) * len(shape))
    in_specs = [at(0), at(1), at(2), whole(2, rows, 1), pair]
    in_specs += [whole(2, rows, HEAD_DIM), whole(rows, rows)]
    in_specs += [logs if values.ndim == 3 else column for values in extra]
    out_shape = [jax.ShapeDtypeStruct((rows, heads * HEAD_DIM), kind) for kind in outs]
    out_specs = [column] * len(outs)
    if log_out:
        out_shape += [jax.ShapeDtypeStruct((heads, rows, 1), F32)]
        out_specs += [logs]
    else:
        out_shape += [
            jax.ShapeDtypeStruct((2, heads * HEAD_DIM), F32),
            jax.ShapeDtypeStruct((2, rows, 1), F32),
        ]
        out_specs += [pair, whole(2, rows, 1)]
    return pl.pallas_call(
        kernel,
        grid=(heads,),
        in_specs=in_specs,
        out_specs=out_specs,
        out_shape=out_shape,
        cost_estimate=LIGHT,
    )(*inputs, *extra)


def body(
    tokens,
    cotangent,
    dealing,
    lengths,
    routes,
    attention_gain,
    query_weight,
    key_weight,
    value_weight,
    output_weight,
    query_gain,
    key_gain,
    ffn_gain,
    router_weight,
    gate_weight,
    up_weight,
    down_weight,
):
    groups = lax.axis_size("dp")
    me = lax.axis_index("dp")
    side = lax.axis_index("tensor")
    rows_here, model_width = tokens.shape
    per_peer = rows_here // groups
    half_peer = per_peer // 2
    half_rows = rows_here // 2
    chips = groups // 2
    moe_chips = EXPERTS // 2
    replicas = groups // EXPERTS
    expert = lax.rem(me, EXPERTS)
    expert_chip, core = expert // 2, core_index()
    expert_place = jnp.stack([expert_chip, core]).astype(jnp.int32)

    dealt = dealing.reshape(groups, rows_here)
    places = jnp.arange(rows_here, dtype=jnp.int32)
    source_block = dealt // rows_here
    own_sources = lax.dynamic_slice_in_dim(source_block, me, 1, 0)
    numbers = jnp.arange(groups, dtype=jnp.int32)[:, None]
    chosen = jnp.concatenate([source_block == me, own_sources == numbers], 0).astype(BF16)
    earlier = (places[:, None] < places[None, :]).astype(BF16)
    rank = mm(chosen, earlier).astype(jnp.int32)
    turns = jnp.arange(per_peer, dtype=jnp.int32)[None, :, None]
    listed = (rank[:, None, :] == turns) & (chosen[:, None, :] > 0)
    leaving = jnp.sum(jnp.where(listed[:groups], lax.rem(dealt, rows_here)[:, None, :], 0), -1)
    own_order = jnp.sum(jnp.where(listed[groups:], places[None, None, :], 0), -1)
    leaving = leaving.reshape(groups, 2, half_peer)
    own_order = own_order.reshape(groups, 2, half_peer)

    def by_side(table):
        first, second = table[:, 0].reshape(-1), table[:, 1].reshape(-1)
        return jnp.concatenate(
            [jnp.where(side == 0, first, second), jnp.where(side == 0, second, first)]
        )

    leaving = by_side(leaving)
    own_order = by_side(own_order)
    expert_ids = jnp.arange(EXPERTS, dtype=jnp.int32)
    uses = jnp.sum((routes[:, :, None] == expert_ids[None, None, :]).astype(F32), 1)
    reorder = (own_order[:half_rows, None] == places[None, :]).astype(BF16)
    used = mm(reorder, uses.astype(BF16))

    told = jnp.tile(used.T.astype(BF16), (groups // EXPERTS, 1)).reshape(groups, per_peer, -1)

    small = jnp.concatenate(
        [
            attention_gain,
            ffn_gain,
            query_gain.reshape(-1),
            key_gain.reshape(-1),
            router_weight.reshape(-1),
        ]
    ).astype(BF16)
    small = jnp.broadcast_to(small.reshape(1, per_peer, -1), (groups, per_peer, small.size // per_peer))
    pick = (leaving[:half_rows, None] == places[None, :]).astype(BF16)
    sent = jnp.concatenate(
        [
            mm(pick, tokens).astype(BF16).reshape(groups, half_peer, model_width),
            mm(pick, cotangent).astype(BF16).reshape(groups, half_peer, model_width),
        ],
        1,
    )
    sent = jnp.concatenate([sent, small, told], 2)
    got = lax.all_to_all(sent, "dp", split_axis=0, concat_axis=0, tiled=True)

    packed_own, packed_sibling = pack_experts(expert_place, gate_weight, up_weight, down_weight)
    packed_experts = merge_cores(expert_place, packed_own, to_sibling(packed_sibling))
    got = after(got, packed_experts)
    rows = got[:, :half_peer, :model_width].reshape(half_rows, model_width).astype(F32)
    cot_rows = got[:, half_peer:, :model_width].reshape(half_rows, model_width)
    small = got[:, :, model_width : model_width + small.shape[2]].reshape(groups, -1)
    told = got[:, :, got.shape[2] - told.shape[2] :].reshape(groups, -1)
    told = lax.dynamic_slice_in_dim(told, me // EXPERTS * EXPERTS, EXPERTS, 0)
    uses_all = told.reshape(-1, 1).astype(F32)

    shard = attention_gain.shape[0]
    gain_shard = query_gain.shape[1]
    first_gain = small[:, :shard].reshape(-1).astype(F32)
    second_gain = small[:, shard : 2 * shard].reshape(-1).astype(F32)
    at = 2 * shard
    query_scale_gain = small[:, at : at + gain_shard].reshape(-1).astype(F32)
    key_scale_gain = small[:, at + gain_shard : at + 2 * gain_shard].reshape(-1).astype(F32)
    router_full = small[:, at + 2 * gain_shard :].reshape(model_width, EXPERTS)

    norm_one = row_scale(rows)
    normed_own = (rows * norm_one * first_gain).astype(BF16)
    normed_peer = to_peer(normed_own)

    hidden_half = gate_weight.shape[2]
    across = [list(range(at, groups, EXPERTS)) for at in range(EXPERTS)]
    own_chunks = [packed_experts[0]] + [None] * (moe_chips - 1)
    peer_chunks = [None] * moe_chips

    def chip_pairs(step):
        return [(index, index ^ (2 * step)) for index in range(groups)]

    def fetch_experts(steps):
        for step in steps:
            if step > 0:
                own_chunks[step] = lax.ppermute(packed_experts[step], "dp", chip_pairs(step))

    def share_experts(steps):
        for step in steps:
            peer_chunks[step] = to_peer(own_chunks[step])

    qkv_block = jnp.concatenate([query_weight, key_weight, value_weight], 1).astype(BF16)
    qkv_full = lax.all_gather(qkv_block, "dp", axis=0, tiled=True)
    output_full = lax.all_gather(output_weight.T.astype(BF16), "dp", axis=0, tiled=True)
    within = [list(range(at, at + EXPERTS)) for at in range(0, groups, EXPERTS)]
    in_group = {} if replicas == 1 else {"axis_index_groups": within}
    fetch_experts([4, 6, 1, 2, 3, 5, 7])
    own_chunks[0] = after(own_chunks[0], normed_peer)
    share_experts([0, 1, 2, 3])
    heads_width = query_weight.shape[1]
    order = ring_order(chips)

    finish_at = jnp.cumsum(lengths[0])
    start_at = finish_at - lengths[0]
    segment_ids = jnp.sum((own_order[:, None] >= finish_at[None, :]).astype(jnp.int32), -1)
    numbers = jnp.arange(lengths.shape[1], dtype=jnp.int32)
    begins = jnp.sum(jnp.where(segment_ids[:, None] == numbers[None, :], start_at[None, :], 0), -1)
    turn_tables = rope_tables((own_order - begins).astype(F32), HEAD_DIM)
    allowed = (segment_ids[:, None] == segment_ids[None, :]) & (
        own_order[None, :] <= own_order[:, None]
    )

    normed_one = jnp.concatenate([normed_own, normed_peer], 0)
    normed_one = after(normed_one, *[own_chunks[step] for step in (1, 2, 3, 4, 6)])
    qkv = mm(normed_one, qkv_full)
    query_raw, key_raw = qkv[:, :heads_width], qkv[:, heads_width : 2 * heads_width]

    def over_sides(values):
        theirs = to_peer(values)
        return values + jnp.concatenate([theirs[:, half_rows:], theirs[:, :half_rows]], 1)

    squares = over_sides(
        jnp.stack([jnp.sum(query_raw * query_raw, -1), jnp.sum(key_raw * key_raw, -1)])
    )
    scales = lax.rsqrt(squares / model_width + EPS)[:, :, None]
    heads_here = heads_width // HEAD_DIM
    head_inputs = (
        qkv,
        qkv,
        qkv,
        scales,
        jnp.stack([query_scale_gain, key_scale_gain]),
        turn_tables,
        allowed.astype(F32),
    )
    query_heads, key_heads, context, log_total = by_heads(
        attention_kernel, rows_here, heads_here, head_inputs, (), (BF16,) * 3, True
    )
    attention = outer_cols(context, output_full)
    attention = after(attention, own_chunks[5])
    attention = attention[:half_rows] + to_peer(
        attention[half_rows:].astype(BF16)
    ).astype(F32)
    for step in (4, 6, 5, 7):
        own_chunks[step] = after(own_chunks[step], attention)
    share_experts([4, 6, 5, 7])
    hidden = rows + attention

    norm_two = row_scale(hidden)
    normed_two = (hidden * norm_two * second_gain).astype(BF16)
    logits = mm(normed_two, router_full)
    powered_two = jnp.exp(logits - jnp.max(logits, -1, keepdims=True))
    router_probs = powered_two / jnp.sum(powered_two, -1, keepdims=True)

    def to_experts(table):
        return lax.all_to_all(table, "dp", split_axis=0, concat_axis=0, tiled=True, **in_group)


    def placed(chunks):
        size, width = chunks[0].shape
        whole = jnp.zeros((moe_chips * size, width), chunks[0].dtype)
        for step, chunk in enumerate(chunks):
            at = (expert_chip ^ step) * size
            whole = lax.dynamic_update_slice_in_dim(whole, chunk, at, 0)
        return whole

    expert_own, expert_peer = placed(own_chunks), placed(peer_chunks)
    if replicas > 1:
        expert_own, expert_peer = (
            lax.all_gather(part, "dp", axis=0, tiled=True, axis_index_groups=across)
            for part in (expert_own, expert_peer)
        )
    inputs_all = lax.all_gather(after(normed_two, own_chunks[7]), "dp", axis=0, tiled=True, **in_group)
    cot_all = lax.all_gather(cot_rows, "dp", axis=0, tiled=True, **in_group)
    input_grad, active, front_grad, cells, gates = expert_rows(
        expert[None].astype(jnp.int32),
        inputs_all,
        cot_all,
        uses_all,
        router_full,
        expert_own,
        expert_peer,
        rows_here,
    )

    def sum_experts(values):
        return lax.psum_scatter(values, "dp", scatter_dimension=0, tiled=True, **in_group)

    steps_back = [4, 1, 6, 2, 5, 3, 7, 0]
    early = 3 * moe_chips // 4
    chips_back = jnp.stack([expert_chip ^ step for step in steps_back]).astype(jnp.int32)
    block_order = chips_back if replicas == 1 else jnp.arange(moe_chips, dtype=jnp.int32)
    wgrad_first, wgrad_last, wgrad_own = expert_wgrads(
        block_order, inputs_all, cells, front_grad, active
    )
    normed_two_grad = after(sum_experts(input_grad), wgrad_own)
    if replicas == 1:
        peer_first = to_peer(wgrad_first)
    mixed, mixing = expert_mixture(active, cot_all, gates, expert_own, expert_peer, rows_here)
    normed_two_grad = normed_two_grad.astype(F32)
    mixing_table = to_experts(mixing.reshape(EXPERTS, -1))
    mixture = sum_experts(after(mixed, normed_two_grad)).astype(F32)
    out_rows = (hidden + mixture).astype(BF16)

    if replicas > 1:

        def over_replicas(values):
            values = lax.psum_scatter(
                values.reshape(model_width, -1),
                "dp",
                scatter_dimension=0,
                tiled=True,
                axis_index_groups=across,
            )
            return jnp.take(values.reshape(moe_chips, -1, values.shape[1]), chips_back, axis=0)

        wgrad_own = over_replicas(wgrad_own)
        wgrad_peer = over_replicas(jnp.concatenate([wgrad_first, wgrad_last], 0))
        wgrad_first, wgrad_last = wgrad_peer[:early], wgrad_peer[early:]
        peer_first = to_peer(wgrad_first)

    def add_wgrads(own, theirs):
        return list((own.astype(F32) + theirs.astype(F32)).astype(BF16))

    summed = add_wgrads(wgrad_own[:early], peer_first)

    def return_wgrad(at):
        step = steps_back[at]
        return lax.ppermute(summed[at], "dp", chip_pairs(step)) if step > 0 else summed[at]

    wgrad_chunks = [return_wgrad(at) for at in range(early)]

    prob_grad = mixing_table.T * used
    logit_grad = (
        router_probs * (prob_grad - jnp.sum(router_probs * prob_grad, -1, keepdims=True))
    ).astype(BF16)
    router_wgrad = inner_rows(normed_two, logit_grad)
    normed_two_grad = normed_two_grad + outer_cols(logit_grad, router_full)
    ffn_gain_grad = jnp.sum(normed_two_grad * hidden * norm_two, 0)
    scaled_two = normed_two_grad * second_gain
    hidden_grad = cot_rows.astype(F32) + norm_two * (
        scaled_two - hidden * norm_two * norm_two * jnp.mean(scaled_two * hidden, -1, keepdims=True)
    )

    attn_own = hidden_grad.astype(BF16)
    attn_peer = to_peer(attn_own)
    attn_grad = jnp.concatenate([attn_own, attn_peer], 0)
    attn_grad = after(attn_grad, summed[0])
    context_grad = mm(attn_grad, output_full).astype(BF16)
    query_norm_grad, key_norm_grad, value_grad, gain_grads, inner_parts = by_heads(
        attention_grad_kernel,
        rows_here,
        heads_here,
        head_inputs,
        (query_heads, key_heads, log_total, context_grad),
        (F32, F32, BF16),
        False,
    )
    output_wgrad = inner_rows(attn_grad, context).astype(BF16)
    query_gain_grad, key_gain_grad = gain_grads
    inners = over_sides(inner_parts[:, :, 0])
    query_scale, key_scale = scales
    output_wgrad = lax.psum_scatter(output_wgrad, "dp", scatter_dimension=0, tiled=True)
    peer_last = to_peer(after(wgrad_last, attn_peer))
    summed += add_wgrads(wgrad_own[early:], peer_last)
    wgrad_chunks += [return_wgrad(at) for at in range(early, moe_chips)]
    query_raw_grad = (
        query_scale * query_scale_gain * query_norm_grad
        - query_raw * query_scale**3 * inners[0][:, None] / model_width
    ).astype(BF16)
    key_raw_grad = (
        key_scale * key_scale_gain * key_norm_grad
        - key_raw * key_scale**3 * inners[1][:, None] / model_width
    ).astype(BF16)
    qkv_grad = jnp.concatenate([query_raw_grad, key_raw_grad, value_grad], 1)
    qkv_grad = after(qkv_grad, wgrad_chunks[0])
    ring_rows = columns_in(normed_one, order, chips)
    qkv_wgrad = inner_rows(ring_rows, qkv_grad).astype(BF16)
    normed_one_grad = outer_cols(qkv_grad, qkv_full)
    normed_one_grad = normed_one_grad[:half_rows] + to_peer(
        normed_one_grad[half_rows:].astype(BF16)
    ).astype(F32)
    attention_gain_grad = jnp.sum(normed_one_grad * rows * norm_one, 0)
    scaled_one = normed_one_grad * first_gain
    rows_grad = hidden_grad + norm_one * (
        scaled_one - rows * norm_one * norm_one * jnp.mean(scaled_one * rows, -1, keepdims=True)
    )

    small_grad = jnp.concatenate(
        [
            query_gain_grad.reshape(groups, -1),
            key_gain_grad.reshape(groups, -1),
            attention_gain_grad.reshape(groups, -1),
            ffn_gain_grad.reshape(groups, -1),
            router_wgrad.reshape(groups, -1),
        ],
        1,
    )
    small_grad = jnp.sum(
        lax.all_to_all(small_grad, "dp", split_axis=0, concat_axis=0, tiled=True), 0
    )
    at = 2 * gain_shard
    by_rows = small_grad[at:]
    by_rows = by_rows + to_peer(by_rows)

    place_back = (places[:, None] == leaving[None, :]).astype(BF16)

    def send_back(values):
        back = values.reshape(groups, half_peer, model_width)
        back = lax.all_to_all(back, "dp", split_axis=0, concat_axis=0, tiled=True)
        back = back.reshape(half_rows, model_width)
        return mm(place_back, jnp.concatenate([back, to_peer(back)], 0)).astype(BF16)

    block_out = send_back(after(out_rows, qkv_grad))
    token_grad = send_back(rows_grad.astype(BF16))
    qkv_wgrad = after(qkv_wgrad, wgrad_chunks[2], summed[early])
    qkv_wgrad = ring_scatter(pieces_of(qkv_wgrad, chips), chips, BF16, ((by_rows, wgrad_chunks[4]), token_grad, block_out))
    returned = jnp.stack(wgrad_chunks).reshape(moe_chips, 2, -1, 3 * hidden_half)
    of_sibling = to_sibling(lax.dynamic_index_in_dim(returned, 1 - core, 1, keepdims=False))
    gate_weight_grad, up_weight_grad, down_weight_grad = unpack_experts(
        jnp.append(chips_back, core).astype(jnp.int32), returned, of_sibling
    )
    return (
        block_out,
        token_grad,
        by_rows[:shard],
        qkv_wgrad[:, :heads_width],
        qkv_wgrad[:, heads_width : 2 * heads_width],
        qkv_wgrad[:, 2 * heads_width :],
        output_wgrad.T.astype(F32),
        small_grad[:gain_shard][None],
        small_grad[gain_shard:at][None],
        by_rows[shard : 2 * shard],
        by_rows[2 * shard :].reshape(router_weight.shape),
        gate_weight_grad,
        up_weight_grad,
        down_weight_grad,
    )


def solution(mesh):
    rows = P("dp", None)
    columns = P("tensor", "dp")
    inputs = (rows, rows, P(), rows, rows, P("dp"))
    inputs += (P("dp", "tensor"),) * 3 + (columns,) * 3 + (P("dp"), rows)
    inputs += (P(None, "dp", "tensor"),) * 2 + (P(None, "tensor", "dp"),)
    outputs = (rows, rows, P("dp")) + (P("dp", "tensor"),) * 3 + (columns,) * 3
    outputs += (P("dp"), rows) + (P(None, "dp", "tensor"),) * 2 + (P(None, "tensor", "dp"),)
    return jax.shard_map(body, mesh=mesh, in_specs=inputs, out_specs=outputs, check_vma=False)
```

time: 1140 us -> 1040 us (0.912)
  matrix products: 211 us -> 35.8 us
  Pallas kernels: 19.5 us -> 155 us
  waiting for transfers between devices: 440 us -> 565 us
  starting transfers between devices: 181 us -> 110 us
  other arithmetic: 119 us -> 60 us
  local copies, waits for them, and re-layouts: 137 us -> 91.1 us
    pallas_call x0 -> x6, Pallas kernels: none -> 135 us  [the longest x1 55.8 us: expert_rows(): pl.pallas_call(rows_kernel, grid_spec=pltpu.PrefetchScalarGridSpec(num_sc...]
    dot_general x7 -> x3, matrix products: 73.3 us -> 12 us  [outer_cols(): lax.dot_general(left, right, (((1,), (1,)), ((), ())), preferred_element_...]
    dot_general x12 -> x9, matrix products: 69.2 us -> 15 us  [mm(): lax.dot_general(left, right, (((1,), (0,)), ((), ())), preferred_element_...]
    dot_general x7 -> x3, matrix products: 60 us -> 8.79 us  [inner_rows(): lax.dot_general(left, right, (((0,), (0,)), ((), ())), preferred_element_...]
    ppermute x42 -> x7, starting transfers between devices: 53.8 us -> 5.21 us  [to_sibling(): return lax.ppermute(values, 'dp', pairs)]
    all_gather x0 -> x4, waiting for transfers between devices: none -> 42.8 us  [the longest x1 42.8 us: body(): lax.all_gather(output_weight.T.astype(BF16), 'dp', axis=0, tiled=True)]
    ppermute x71 -> x37, waiting for transfers between devices: 416 us -> 453 us  [the longest x19 183 us: to_peer(): return lax.ppermute(values, 'tensor', [(0, 1), (1, 0)])]
    convert_element_type x12 -> x3, other arithmetic: 36.6 us -> 11.9 us  [ring_scatter(): (parts[2 * step] + theirs + flow).astype(kind)]
  transfers between devices with their start and end apart: 120 -> 56, of which waited for: 47 -> 25; matrix products, arithmetic and copies ran while one was open for 35% -> 16% of each run, Pallas kernels for 1% -> 10%
where the time goes in v3:
time: 1040 us; the launch traced here: 1030 us
  waiting for transfers between devices  565 us (54%)
  Pallas kernels  155 us (15%)
  starting transfers between devices  110 us (11%)
  local copies, waits for them, and re-layouts  91.1 us (9%)
  other arithmetic  60 us (6%)
  matrix products  35.8 us (3%)
  between operations  15.7 us (2%)
    ppermute x19, waiting for transfers between devices, to_peer(): return lax.ppermute(values, 'tensor', [(0, 1), (1, 0)])  183 us
    ppermute x7, waiting for transfers between devices, fetch_experts(): lax.ppermute(packed_experts[step], 'dp', chip_pairs(step))  137 us
    ppermute x7, waiting for transfers between devices, return_wgrad(): lax.ppermute(summed[at], 'dp', chip_pairs(step))  89.9 us
    pallas_call x1, Pallas kernels, expert_rows(): pl.pallas_call(rows_kernel, grid_spec=pltpu.PrefetchScalarGridSpec(num_sc...  55.8 us
    all_gather x1, waiting for transfers between devices, body(): lax.all_gather(output_weight.T.astype(BF16), 'dp', axis=0, tiled=True)  42.8 us
    pallas_call x1, Pallas kernels, expert_wgrads(): pl.pallas_call(wgrad_kernel, grid_spec=pltpu.PrefetchScalarGridSpec(num_s...  34.3 us
    all_to_all x2, waiting for transfers between devices, send_back(): back = lax.all_to_all(back, 'dp', split_axis=0, concat_axis=0, tiled=True)  31.5 us
    unnamed x153, local copies, waits for them, and re-layouts  30.8 us
  transfers between devices with their start and end apart: 56, of which 25 were waited for; matrix products, arithmetic and copies ran while one was open for 16% of the time, Pallas kernels for 10%

profile of v3, /device:TPU:17, one launch (start us, length us, event | category | flops | bytes accessed | tf_op | source)
XLA Modules:
  0.0 1032.9 jit_solution(8596865473345523881)
XLA Ops:
  13.1 10.3 shard_map.272
  36.2 8.6 shard_map.273
  44.8 30.0 %all-to-all-done = bf16[16,16,2208]{2,1,0:T(8,128)(2,1)S(1)} async-done(((bf16[16,16,2208]{2,1,0:T(8,128)(2,1)}), bf16[16,16,2208]{2,1,0:T(8,128)(2,1)S(1)}, u32[]{:S(2)}, u32[]{:S(2)}) %all-to-all-start) | async-done | bytes 1130528 | tf_op jit(solution)/shard_map/all_to_all | solution.py:531
  96.8 76.8 %collective-permute-done.6 = bf16[256,1536]{1,0:T(8,128)(2,1)} collective-permute-done((bf16[256,1536]{1,0:T(8,128)(2,1)}, bf16[256,1536]{1,0:T(8,128)(2,1)}, u32[]{:S(2)}, u32[]{:S(2)}) %collective-permute-start.6) | collective-permute-done | bytes 786464 | tf_op jit(solution)/shard_map/ppermute | solution.py:567
  173.6 18.0 %collective-permute-done.5 = bf16[256,1536]{1,0:T(8,128)(2,1)} collective-permute-done((bf16[256,1536]{1,0:T(8,128)(2,1)}, bf16[256,1536]{1,0:T(8,128)(2,1)}, u32[]{:S(2)}, u32[]{:S(2)}) %collective-permute-start.5) | collective-permute-done | bytes 786464 | tf_op jit(solution)/shard_map/ppermute | solution.py:567
  193.4 6.4 fusion.59.query_ref.key_ref.value_ref
  206.1 8.8 shard_map.274
  215.0 42.8 %all-gather.7.cloned.1.call-done = bf16[2048,1024]{0,1:T(8,128)(2,1)} async-done(((bf16[128,1024]{0,1:T(8,128)(2,1)}), bf16[2048,1024]{0,1:T(8,128)(2,1)}) %all-gather.7.cloned.1.call-update) | async-done | bytes 4194320 | tf_op jit(solution)/shard_map/all_gather | solution.py:575
  264.1 10.8 %collective-permute-done.9 = bf16[128,2048]{1,0:T(8,128)(2,1)S(1)} collective-permute-done((bf16[128,2048]{1,0:T(8,128)(2,1)S(1)}, bf16[128,2048]{1,0:T(8,128)(2,1)S(1)}, u32[]{:S(2)}, u32[]{:S(2)}) %collective-permute-start.9) | collective-permute-done | bytes 524320 | tf_op jit(solution)/shard_map/ppermute | solution.py:86
  275.2 40.8 %collective-permute-done.10 = bf16[256,1536]{1,0:T(8,128)(2,1)S(1)} collective-permute-done((bf16[256,1536]{1,0:T(8,128)(2,1)S(1)}, bf16[256,1536]{1,0:T(8,128)(2,1)S(1)}, u32[]{:S(2)}, u32[]{:S(2)}) %collective-permute-start.10) | collective-permute-done | bytes 786464 | tf_op jit(solution)/shard_map/ppermute | solution.py:567
  340.5 46.5 %collective-permute-done.12 = bf16[256,1536]{1,0:T(8,128)(2,1)S(1)} collective-permute-done((bf16[256,1536]{1,0:T(8,128)(2,1)}, bf16[256,1536]{1,0:T(8,128)(2,1)S(1)}, u32[]{:S(2)}, u32[]{:S(2)}) %collective-permute-start.12) | collective-permute-done | bytes 786464 | tf_op jit(solution)/shard_map/ppermute | solution.py:86
  400.0 38.7 %collective-permute-done.15 = bf16[256,1536]{1,0:T(8,128)(2,1)S(1)} collective-permute-done((bf16[256,1536]{1,0:T(8,128)(2,1)}, bf16[256,1536]{1,0:T(8,128)(2,1)S(1)}, u32[]{:S(2)}, u32[]{:S(2)}) %collective-permute-start.15) | collective-permute-done | bytes 786464 | tf_op jit(solution)/shard_map/ppermute | solution.py:86
  439.7 15.9 %collective-permute-done.16 = bf16[256,1536]{1,0:T(8,128)(2,1)S(1)} collective-permute-done((bf16[256,1536]{1,0:T(8,128)(2,1)}, bf16[256,1536]{1,0:T(8,128)(2,1)S(1)}, u32[]{:S(2)}, u32[]{:S(2)}) %collective-permute-start.16) | collective-permute-done | bytes 786464 | tf_op jit(solution)/shard_map/ppermute | solution.py:86
  458.4 55.8 %shard_map.275 = (bf16[2048,2048]{1,0:T(8,128)(2,1)}, bf16[2048,1024]{1,0:T(8,128)(2,1)}, bf16[2048,2048]{1,0:T(8,128)(2,1)}, bf16[2048,2048]{1,0:T(8,128)(2,1)}, f32[2048,1]{1,0:T(8,128)S(1)}) custom-call(s32[1]{0:T(128)} %bitcast.34.expert_ref, bf16[2048,2048]{1,0:T(8,128)(2,1)} %all-gather.9.cloned.1.call-done.rows_ref, ...), custom_call_target="tpu_custom_call" | custom-call | flops 1024 | bytes 1024 | tf_op jit(solution)/shard_map/pallas_call | solution.py:253
  516.6 34.3 %shard_map.277 = (bf16[6,256,1536]{2,1,0:T(8,128)(2,1)}, bf16[2,256,1536]{2,1,0:T(8,128)(2,1)S(1)}, bf16[8,256,1536]{2,1,0:T(8,128)(2,1)}) custom-call(s32[8]{0:T(128)S(1)} %stack.112.order_ref, bf16[2048,2048]{1,0:T(8,128)(2,1)} %all-gather.9.cloned.1.call-done.rows_ref, bf16[2048,2048]{1,0:T(8,128)(2,1)} %get-tuple-element.73.cells_ref, ...), custom_call_target="tpu_custom_call" | custom-call | flops 1024 | bytes 1024 | tf_op jit(solution)/shard_map/pallas_call | solution.py:324
  554.4 16.3 %shard_map.276 = (bf16[2048,2048]{1,0:T(8,128)(2,1)}, f32[2048,1]{1,0:T(8,128)S(1)}) custom-call(bf16[2048,1024]{1,0:T(8,128)(2,1)} %get-tuple-element.69.active_ref, bf16[2048,2048]{1,0:T(8,128)(2,1)} %all-gather.11.cloned.1.call-done.cot_ref, f32[2048,1]{1,0:T(8,128)S(1)} %get-tuple-element.70.gate_ref, ...), custom_call_target="tpu_custom_call" | custom-call | flops 1024 | bytes 1024 | tf_op jit(solution)/shard_map/pallas_call | solution.py:283
  576.9 12.8 %all-to-all-start.1 = ((f32[16,1,128]{2,1,0:T(1,128)}), f32[16,1,128]{2,1,0:T(1,128)S(1)}, u32[]{:S(2)}, u32[]{:S(2)}) async-start(f32[16,1,128]{2,1,0:T(1,128)} %bitcast.47), calls=%async_computation.3 | async-start | bytes 16384 | tf_op jit(solution)/shard_map/all_to_all | solution.py:637
  593.4 57.5 %collective-permute-done.20 = bf16[6,256,1536]{2,1,0:T(8,128)(2,1)} collective-permute-done((bf16[6,256,1536]{2,1,0:T(8,128)(2,1)}, bf16[6,256,1536]{2,1,0:T(8,128)(2,1)}, u32[]{:S(2)}, u32[]{:S(2)}) %collective-permute-start.20) | collective-permute-done | bytes 4718624 | tf_op jit(solution)/shard_map/ppermute | solution.py:86
  650.9 7.6 add_convert_fusion
  673.0 11.3 %shard_map.278 = (f32[256,1024]{1,0:T(8,128)}, f32[256,1024]{1,0:T(8,128)}, bf16[256,1024]{1,0:T(8,128)(2,1)}, f32[2,1024]{1,0:T(2,128)}, f32[2,256,1]{2,1,0:T(8,128)}) custom-call(f32[256,3072]{1,0:T(8,128)} %copy-done.5, f32[256,3072]{1,0:T(8,128)} %copy-done.5, f32[256,3072]{1,0:T(8,128)} %copy-done.5, f32[2,256,1]{2,1,0:T(8,128)} %rsqrt.33.scale_ref, ...), custom_call_target="tpu_custom_call" | custom-call | flops 1024 | bytes 1024 | tf_op jit(solution)/shard_map/pallas_call | solution.py:439
  687.1 10.2 collective-permute-start.27
  701.2 42.8 %collective-permute-done.22 = bf16[256,1536]{1,0:T(8,128)(2,1)} collective-permute-done((bf16[256,1536]{1,0:T(8,128)(2,1)}, bf16[256,1536]{1,0:T(8,128)(2,1)}, u32[]{:S(2)}, u32[]{:S(2)}) %collective-permute-start.22) | collective-permute-done | bytes 786464 | tf_op jit(solution)/shard_map/ppermute | solution.py:710
  744.0 6.7 fusion.61
  764.6 15.0 %collective-permute-done.27 = bf16[256,1536]{1,0:T(8,128)(2,1)} collective-permute-done((bf16[256,1536]{1,0:T(8,128)(2,1)S(1)}, bf16[256,1536]{1,0:T(8,128)(2,1)}, u32[]{:S(2)}, u32[]{:S(2)}) %collective-permute-start.27) | collective-permute-done | bytes 786464 | tf_op jit(solution)/shard_map/ppermute | solution.py:710
  805.6 18.2 %collective-permute-start.33 = (bf16[128,3072]{1,0:T(8,128)(2,1)}, bf16[128,3072]{1,0:T(8,128)(2,1)}, u32[]{:S(2)}, u32[]{:S(2)}) collective-permute-start(bf16[128,3072]{1,0:T(8,128)(2,1)} %add_convert_fusion.5), channel_id=1, source_target_pairs={{0,8},{2,6},{8,16},{10,2},{16,24},{18,10},{24,28},{26,18},{28,20},... | collective-permute-start | bytes 2359304 | tf_op jit(solution)/shard_map/ppermute | solution.py:106
  831.5 18.9 %collective-permute-done.33 = bf16[128,3072]{1,0:T(8,128)(2,1)} collective-permute-done((bf16[128,3072]{1,0:T(8,128)(2,1)}, bf16[128,3072]{1,0:T(8,128)(2,1)}, u32[]{:S(2)}, u32[]{:S(2)}) %collective-permute-start.33) | collective-permute-done | bytes 786464 | tf_op jit(solution)/shard_map/ppermute | solution.py:106
  866.5 7.5 all-to-all-start.2
  877.4 9.6 collective-permute-done.35
  898.6 31.5 %all-to-all-done.2 = bf16[16,8,2048]{2,1,0:T(8,128)(2,1)} async-done(((bf16[16,8,2048]{2,1,0:T(8,128)(2,1)}), bf16[16,8,2048]{2,1,0:T(8,128)(2,1)}, u32[]{:S(2)}, u32[]{:S(2)}) %all-to-all-start.2) | async-done | bytes 524320 | tf_op jit(solution)/shard_map/all_to_all | solution.py:791
  943.1 32.1 %collective-permute-done.42 = bf16[256,1536]{1,0:T(8,128)(2,1)S(1)} collective-permute-done((bf16[256,1536]{1,0:T(8,128)(2,1)}, bf16[256,1536]{1,0:T(8,128)(2,1)S(1)}, u32[]{:S(2)}, u32[]{:S(2)}) %collective-permute-start.42) | collective-permute-done | bytes 786464 | tf_op jit(solution)/shard_map/ppermute | solution.py:710
  989.2 13.6 %collective-permute-done.37 = bf16[256,3072]{1,0:T(8,128)(2,1)S(1)} collective-permute-done((bf16[256,3072]{1,0:T(8,128)(2,1)S(1)}, bf16[256,3072]{1,0:T(8,128)(2,1)S(1)}, u32[]{:S(2)}, u32[]{:S(2)}) %collective-permute-start.37) | collective-permute-done | bytes 1572896 | tf_op jit(solution)/shard_map/ppermute | solution.py:112
  1011.5 9.5 shard_map.279
  (419 shorter events, 251.7 us)
Async XLA Ops:
  7.2 186.2 %all-gather.5.cloned.1.call-start = ((), (), s32[]{:S(2)}) async-start(), calls=%async_computation.8 | async-start | bytes 13369344 | tf_op jit(solution)/shard_map/all_gather | solution.py:574
  11.6 246.2 %all-gather.7.cloned.1.call-start = ((), (), s32[]{:S(2)}) async-start(), calls=%async_computation.9 | async-start | bytes 4456448 | tf_op jit(solution)/shard_map/all_gather | solution.py:575
  36.2 422.3 %all-gather.11.cloned.1.call-start = ((), (), s32[]{:S(2)}) async-start(), calls=%async_computation.11 | async-start | bytes 8912896 | tf_op jit(solution)/shard_map/all_gather | solution.py:655
  75.8 382.6 %all-gather.9.cloned.1.call-start = ((), (), s32[]{:S(2)}) async-start(), calls=%async_computation.10 | async-start | bytes 8912896 | tf_op jit(solution)/shard_map/all_gather | solution.py:654
  85.2 88.3 %collective-permute-start.6 = (bf16[256,1536]{1,0:T(8,128)(2,1)}, bf16[256,1536]{1,0:T(8,128)(2,1)}, u32[]{:S(2)}, u32[]{:S(2)}) collective-permute-start(bf16[256,1536]{1,0:T(8,128)(2,1)} %get-tuple-element.208), channel_id=1, source_target_pairs={{0,24},{2,26},{4,28},{6,30},{8,16},{10,18},{12,20},{14,22},{16,8},... | collective-permute-start | bytes 2359304 | tf_op jit(solution)/shard_map/ppermute | solution.py:567
  85.2 106.3 %collective-permute-start.5 = (bf16[256,1536]{1,0:T(8,128)(2,1)}, bf16[256,1536]{1,0:T(8,128)(2,1)}, u32[]{:S(2)}, u32[]{:S(2)}) collective-permute-start(bf16[256,1536]{1,0:T(8,128)(2,1)} %get-tuple-element.209), channel_id=1, source_target_pairs={{0,16},{2,18},{4,20},{6,22},{8,24},{10,26},{12,28},{14,30},{16,0},... | collective-permute-start | bytes 2359304 | tf_op jit(solution)/shard_map/ppermute | solution.py:567
  86.0 105.6 %collective-permute-start.4 = (bf16[256,1536]{1,0:T(8,128)(2,1)}, bf16[256,1536]{1,0:T(8,128)(2,1)}, u32[]{:S(2)}, u32[]{:S(2)}) collective-permute-start(bf16[256,1536]{1,0:T(8,128)(2,1)} %get-tuple-element.210), channel_id=1, source_target_pairs={{0,12},{2,14},{4,8},{6,10},{8,4},{10,6},{12,0},{14,2},{16,28},{18,... | collective-permute-start | bytes 2359304 | tf_op jit(solution)/shard_map/ppermute | solution.py:567
  88.1 105.3 %collective-permute-start.3 = (bf16[256,1536]{1,0:T(8,128)(2,1)}, bf16[256,1536]{1,0:T(8,128)(2,1)}, u32[]{:S(2)}, u32[]{:S(2)}) collective-permute-start(bf16[256,1536]{1,0:T(8,128)(2,1)} %get-tuple-element.211), channel_id=1, source_target_pairs={{0,8},{2,10},{4,12},{6,14},{8,0},{10,2},{12,4},{14,6},{16,24},{18,... | collective-permute-start | bytes 2359304 | tf_op jit(solution)/shard_map/ppermute | solution.py:567
  92.0 101.4 %collective-permute-start.2 = (bf16[256,1536]{1,0:T(8,128)(2,1)}, bf16[256,1536]{1,0:T(8,128)(2,1)}, u32[]{:S(2)}, u32[]{:S(2)}) collective-permute-start(bf16[256,1536]{1,0:T(8,128)(2,1)} %get-tuple-element.212), channel_id=1, source_target_pairs={{0,4},{2,6},{4,0},{6,2},{8,12},{10,14},{12,8},{14,10},{16,20},{18,... | collective-permute-start | bytes 2359304 | tf_op jit(solution)/shard_map/ppermute | solution.py:567
  173.6 87.8 %collective-permute-start.8 = (bf16[256,1536]{1,0:T(8,128)(2,1)}, bf16[256,1536]{1,0:T(8,128)(2,1)}, u32[]{:S(2)}, u32[]{:S(2)}) collective-permute-start(bf16[256,1536]{1,0:T(8,128)(2,1)} %get-tuple-element.207), channel_id=1, source_target_pairs={{0,20},{2,22},{4,16},{6,18},{8,28},{10,30},{12,24},{14,26},{16,4},... | collective-permute-start | bytes 2359304 | tf_op jit(solution)/shard_map/ppermute | solution.py:567
  262.7 53.3 %collective-permute-start.10 = (bf16[256,1536]{1,0:T(8,128)(2,1)S(1)}, bf16[256,1536]{1,0:T(8,128)(2,1)S(1)}, u32[]{:S(2)}, u32[]{:S(2)}) collective-permute-start(bf16[256,1536]{1,0:T(8,128)(2,1)S(1)} %get-tuple-element.206), channel_id=1, source_target_pairs={{0,28},{2,30},{4,24},{6,26},{8,20},{10,22},{12,16},{14,18},{16,12}... | collective-permute-start | bytes 2359304 | tf_op jit(solution)/shard_map/ppermute | solution.py:567
  317.9 340.6 %reduce-scatter.4.cloned.1.call-start = ((), (), s32[]{:S(2)}) async-start(), calls=%async_computation.12 | async-start | bytes 8912896 | tf_op jit(solution)/shard_map/reduce_scatter | solution.py:668
  324.3 64.6 %collective-permute-start.14 = (bf16[256,1536]{1,0:T(8,128)(2,1)}, bf16[256,1536]{1,0:T(8,128)(2,1)S(1)}, u32[]{:S(2)}, u32[]{:S(2)}) collective-permute-start(bf16[256,1536]{1,0:T(8,128)(2,1)} %collective-permute-done.4), channel_id=1, source_target_pairs={{0,1},{1,0},{2,3},{3,2},{4,5},{5,4},{6,7},{7,6},{8,9},{9,8},{10,11... | collective-permute-start | bytes 2359304 | tf_op jit(solution)/shard_map/ppermute | solution.py:86
  325.6 62.4 %collective-permute-start.13 = (bf16[256,1536]{1,0:T(8,128)(2,1)}, bf16[256,1536]{1,0:T(8,128)(2,1)S(1)}, u32[]{:S(2)}, u32[]{:S(2)}) collective-permute-start(bf16[256,1536]{1,0:T(8,128)(2,1)} %collective-permute-done.3), channel_id=1, source_target_pairs={{0,1},{1,0},{2,3},{3,2},{4,5},{5,4},{6,7},{7,6},{8,9},{9,8},{10,11... | collective-permute-start | bytes 2359304 | tf_op jit(solution)/shard_map/ppermute | solution.py:86
  325.8 61.2 %collective-permute-start.12 = (bf16[256,1536]{1,0:T(8,128)(2,1)}, bf16[256,1536]{1,0:T(8,128)(2,1)S(1)}, u32[]{:S(2)}, u32[]{:S(2)}) collective-permute-start(bf16[256,1536]{1,0:T(8,128)(2,1)} %collective-permute-done.2), channel_id=1, source_target_pairs={{0,1},{1,0},{2,3},{3,2},{4,5},{5,4},{6,7},{7,6},{8,9},{9,8},{10,11... | collective-permute-start | bytes 2359304 | tf_op jit(solution)/shard_map/ppermute | solution.py:86
  389.9 67.6 %collective-permute-start.18 = (bf16[256,1536]{1,0:T(8,128)(2,1)S(1)}, bf16[256,1536]{1,0:T(8,128)(2,1)S(1)}, u32[]{:S(2)}, u32[]{:S(2)}) collective-permute-start(bf16[256,1536]{1,0:T(8,128)(2,1)S(1)} %copy-done.31), channel_id=1, source_target_pairs={{0,1},{1,0},{2,3},{3,2},{4,5},{5,4},{6,7},{7,6},{8,9},{9,8},{10,11... | collective-permute-start | bytes 2359304 | tf_op jit(solution)/shard_map/ppermute | solution.py:86
  390.5 66.1 %collective-permute-start.17 = (bf16[256,1536]{1,0:T(8,128)(2,1)}, bf16[256,1536]{1,0:T(8,128)(2,1)S(1)}, u32[]{:S(2)}, u32[]{:S(2)}) collective-permute-start(bf16[256,1536]{1,0:T(8,128)(2,1)} %collective-permute-done.6), channel_id=1, source_target_pairs={{0,1},{1,0},{2,3},{3,2},{4,5},{5,4},{6,7},{7,6},{8,9},{9,8},{10,11... | collective-permute-start | bytes 2359304 | tf_op jit(solution)/shard_map/ppermute | solution.py:86
  392.0 63.6 %collective-permute-start.16 = (bf16[256,1536]{1,0:T(8,128)(2,1)}, bf16[256,1536]{1,0:T(8,128)(2,1)S(1)}, u32[]{:S(2)}, u32[]{:S(2)}) collective-permute-start(bf16[256,1536]{1,0:T(8,128)(2,1)} %collective-permute-done.8), channel_id=1, source_target_pairs={{0,1},{1,0},{2,3},{3,2},{4,5},{5,4},{6,7},{7,6},{8,9},{9,8},{10,11... | collective-permute-start | bytes 2359304 | tf_op jit(solution)/shard_map/ppermute | solution.py:86
  514.3 309.5 %reduce-scatter.6.cloned.1.call-start = ((), (), s32[]{:S(2)}) async-start(), calls=%async_computation.13 | async-start | bytes 8912896 | tf_op jit(solution)/shard_map/reduce_scatter | solution.py:668
  552.1 98.8 %collective-permute-start.20 = (bf16[6,256,1536]{2,1,0:T(8,128)(2,1)}, bf16[6,256,1536]{2,1,0:T(8,128)(2,1)}, u32[]{:S(2)}, u32[]{:S(2)}) collective-permute-start(bf16[6,256,1536]{2,1,0:T(8,128)(2,1)} %get-tuple-element.82), channel_id=1, source_target_pairs={{0,1},{1,0},{2,3},{3,2},{4,5},{5,4},{6,7},{7,6},{8,9},{9,8},{10,11... | collective-permute-start | bytes 14155784 | tf_op jit(solution)/shard_map/ppermute | solution.py:86
  687.1 56.9 %collective-permute-start.22 = (bf16[256,1536]{1,0:T(8,128)(2,1)}, bf16[256,1536]{1,0:T(8,128)(2,1)}, u32[]{:S(2)}, u32[]{:S(2)}) collective-permute-start(bf16[256,1536]{1,0:T(8,128)(2,1)} %get-tuple-element.218), channel_id=1, source_target_pairs={{0,16},{2,18},{4,20},{6,22},{8,24},{10,26},{12,28},{14,30},{16,0},... | collective-permute-start | bytes 2359304 | tf_op jit(solution)/shard_map/ppermute | solution.py:710
  687.1 92.5 %collective-permute-start.27 = (bf16[256,1536]{1,0:T(8,128)(2,1)S(1)}, bf16[256,1536]{1,0:T(8,128)(2,1)}, u32[]{:S(2)}, u32[]{:S(2)}) collective-permute-start(bf16[256,1536]{1,0:T(8,128)(2,1)S(1)} %get-tuple-element.217), channel_id=1, source_target_pairs={{0,24},{2,26},{4,28},{6,30},{8,16},{10,18},{12,20},{14,22},{16,8},... | collective-permute-start | bytes 2359304 | tf_op jit(solution)/shard_map/ppermute | solution.py:710
  697.3 61.4 %collective-permute-start.28 = (bf16[2,256,1536]{2,1,0:T(8,128)(2,1)S(1)}, bf16[2,256,1536]{2,1,0:T(8,128)(2,1)}, u32[]{:S(2)}, u32[]{:S(2)}) collective-permute-start(bf16[2,256,1536]{2,1,0:T(8,128)(2,1)S(1)} %copy-done.4), channel_id=1, source_target_pairs={{0,1},{1,0},{2,3},{3,2},{4,5},{5,4},{6,7},{7,6},{8,9},{9,8},{10,11... | collective-permute-start | bytes 4718600 | tf_op jit(solution)/shard_map/ppermute | solution.py:86
  795.6 64.5 %collective-permute-start.39 = (bf16[256,1536]{1,0:T(8,128)(2,1)}, bf16[256,1536]{1,0:T(8,128)(2,1)}, u32[]{:S(2)}, u32[]{:S(2)}) collective-permute-start(bf16[256,1536]{1,0:T(8,128)(2,1)} %get-tuple-element.215), channel_id=1, source_target_pairs={{0,4},{2,6},{4,0},{6,2},{8,12},{10,14},{12,8},{14,10},{16,20},{18,... | collective-permute-start | bytes 2359304 | tf_op jit(solution)/shard_map/ppermute | solution.py:710
  796.8 57.9 %collective-permute-start.34 = (bf16[256,1536]{1,0:T(8,128)(2,1)}, bf16[256,1536]{1,0:T(8,128)(2,1)}, u32[]{:S(2)}, u32[]{:S(2)}) collective-permute-start(bf16[256,1536]{1,0:T(8,128)(2,1)} %get-tuple-element.216), channel_id=1, source_target_pairs={{0,20},{2,22},{4,16},{6,18},{8,28},{10,30},{12,24},{14,26},{16,4},... | collective-permute-start | bytes 2359304 | tf_op jit(solution)/shard_map/ppermute | solution.py:710
  796.8 53.5 %collective-permute-start.31 = (bf16[256,3072]{1,0:T(8,128)(2,1)}, bf16[256,3072]{1,0:T(8,128)(2,1)}, u32[]{:S(2)}, u32[]{:S(2)}) collective-permute-start(bf16[256,3072]{1,0:T(8,128)(2,1)} %get-tuple-element.203), channel_id=1, source_target_pairs={{0,2},{2,0},{4,6},{6,4},{8,10},{10,8},{12,14},{14,12},{16,18},{18,... | collective-permute-start | bytes 4718600 | tf_op jit(solution)/shard_map/ppermute | solution.py:82
  831.2 189.9 %reduce-scatter.8.cloned.1.call-start = ((), (), s32[]{:S(2)}) async-start(), calls=%async_computation.14 | async-start | bytes 4456448 | tf_op jit(solution)/shard_map/reduce_scatter | solution.py:744
  856.8 79.1 %collective-permute-start.41 = (bf16[256,1536]{1,0:T(8,128)(2,1)S(1)}, bf16[256,1536]{1,0:T(8,128)(2,1)}, u32[]{:S(2)}, u32[]{:S(2)}) collective-permute-start(bf16[256,1536]{1,0:T(8,128)(2,1)S(1)} %copy-done.29), channel_id=1, source_target_pairs={{0,12},{2,14},{4,8},{6,10},{8,4},{10,6},{12,0},{14,2},{16,28},{18,... | collective-permute-start | bytes 2359304 | tf_op jit(solution)/shard_map/ppermute | solution.py:710
  856.8 74.4 %collective-permute-start.40 = (bf16[256,1536]{1,0:T(8,128)(2,1)}, bf16[256,1536]{1,0:T(8,128)(2,1)}, u32[]{:S(2)}, u32[]{:S(2)}) collective-permute-start(bf16[256,1536]{1,0:T(8,128)(2,1)} %get-tuple-element.214), channel_id=1, source_target_pairs={{0,8},{2,10},{4,12},{6,14},{8,0},{10,2},{12,4},{14,6},{16,24},{18,... | collective-permute-start | bytes 2359304 | tf_op jit(solution)/shard_map/ppermute | solution.py:710
  866.5 63.7 %all-to-all-start.2 = ((bf16[16,8,2048]{2,1,0:T(8,128)(2,1)}), bf16[16,8,2048]{2,1,0:T(8,128)(2,1)}, u32[]{:S(2)}, u32[]{:S(2)}) async-start(bf16[16,8,2048]{2,1,0:T(8,128)(2,1)} %bitcast.54), calls=%async_computation.4 | async-start | bytes 1048576 | tf_op jit(solution)/shard_map/all_to_all | solution.py:791
  874.1 103.1 %collective-permute-start.29 = (bf16[256,3072]{1,0:T(8,128)(2,1)S(1)}, bf16[256,3072]{1,0:T(8,128)(2,1)}, u32[]{:S(2)}, u32[]{:S(2)}) collective-permute-start(bf16[256,3072]{1,0:T(8,128)(2,1)S(1)} %copy-done.27), channel_id=1, source_target_pairs={{0,2},{2,0},{4,6},{6,4},{8,10},{10,8},{12,14},{14,12},{16,18},{18,... | collective-permute-start | bytes 4718600 | tf_op jit(solution)/shard_map/ppermute | solution.py:82
  891.5 85.7 %collective-permute-start.36 = (bf16[256,3072]{1,0:T(8,128)(2,1)}, bf16[256,3072]{1,0:T(8,128)(2,1)}, u32[]{:S(2)}, u32[]{:S(2)}) collective-permute-start(bf16[256,3072]{1,0:T(8,128)(2,1)} %add_convert_fusion.2), channel_id=1, source_target_pairs={{0,8},{2,6},{8,16},{10,2},{16,24},{18,10},{24,28},{26,18},{28,20},... | collective-permute-start | bytes 4718600 | tf_op jit(solution)/shard_map/ppermute | solution.py:112
  (92 other events, 1902.5 us)
Sparse Core Ops, SparseCore 0:
  11.7 165.5 all-gather.4
  180.0 77.7 all-gather.6
  259.9 95.1 all-gather.10
  357.8 73.1 all-gather.8
  514.4 110.1 reduce-scatter.3
  628.5 146.9 reduce-scatter.5
  866.7 95.5 reduce-scatter.7

commit v4 on v3

--- a/solution.py
+++ b/solution.py
@@ -575,7 +575,11 @@
     output_full = lax.all_gather(output_weight.T.astype(BF16), "dp", axis=0, tiled=True)
     within = [list(range(at, at + EXPERTS)) for at in range(0, groups, EXPERTS)]
     in_group = {} if replicas == 1 else {"axis_index_groups": within}
-    fetch_experts([4, 6, 1, 2, 3, 5, 7])
+    fetch_experts([4, 6, 1, 2, 3])
+    packed_experts = list(packed_experts)
+    for step in (5, 7):
+        packed_experts[step] = after(packed_experts[step], output_full)
+    fetch_experts([5, 7])
     own_chunks[0] = after(own_chunks[0], normed_peer)
     share_experts([0, 1, 2, 3])
     heads_width = query_weight.shape[1]
@@ -604,6 +608,9 @@
         jnp.stack([jnp.sum(query_raw * query_raw, -1), jnp.sum(key_raw * key_raw, -1)])
     )
     scales = lax.rsqrt(squares / model_width + EPS)[:, :, None]
+    for step in (4, 6):
+        own_chunks[step] = after(own_chunks[step], squares)
+    share_experts([4, 6])
     heads_here = heads_width // HEAD_DIM
     head_inputs = (
         qkv,
@@ -618,13 +625,13 @@
         attention_kernel, rows_here, heads_here, head_inputs, (), (BF16,) * 3, True
     )
     attention = outer_cols(context, output_full)
-    attention = after(attention, own_chunks[5])
+    attention = after(attention, peer_chunks[4], peer_chunks[6])
     attention = attention[:half_rows] + to_peer(
         attention[half_rows:].astype(BF16)
     ).astype(F32)
-    for step in (4, 6, 5, 7):
+    for step in (5, 7):
         own_chunks[step] = after(own_chunks[step], attention)
-    share_experts([4, 6, 5, 7])
+    share_experts([5, 7])
     hidden = rows + attention
 
     norm_two = row_scale(hidden)
@@ -754,7 +761,6 @@
         - key_raw * key_scale**3 * inners[1][:, None] / model_width
     ).astype(BF16)
     qkv_grad = jnp.concatenate([query_raw_grad, key_raw_grad, value_grad], 1)
-    qkv_grad = after(qkv_grad, wgrad_chunks[0])
     ring_rows = columns_in(normed_one, order, chips)
     qkv_wgrad = inner_rows(ring_rows, qkv_grad).astype(BF16)
     normed_one_grad = outer_cols(qkv_grad, qkv_full)
@@ -794,7 +800,7 @@
 
     block_out = send_back(after(out_rows, qkv_grad))
     token_grad = send_back(rows_grad.astype(BF16))
-    qkv_wgrad = after(qkv_wgrad, wgrad_chunks[2], summed[early])
+    qkv_wgrad = after(qkv_wgrad, wgrad_chunks[0], wgrad_chunks[2], summed[early])
     qkv_wgrad = ring_scatter(pieces_of(qkv_wgrad, chips), chips, BF16, ((by_rows, wgrad_chunks[4]), token_grad, block_out))
     returned = jnp.stack(wgrad_chunks).reshape(moe_chips, 2, -1, 3 * hidden_half)
     of_sibling = to_sibling(lax.dynamic_index_in_dim(returned, 1 - core, 1, keepdims=False))

time: 1040 us -> 1020 us (0.981)
  starting transfers between devices: 110 us -> 96.3 us
  local copies, waits for them, and re-layouts: 91.1 us -> 78.5 us
    all_gather x1, waiting for transfers between devices: 42.8 us -> 21.1 us  [body(): lax.all_gather(output_weight.T.astype(BF16), 'dp', axis=0, tiled=True)]
    all_gather x1, waiting for transfers between devices: 0.01 us -> 20 us  [body(): lax.all_gather(after(normed_two, own_chunks[7]), 'dp', axis=0, tiled=True...]
    ppermute x7, waiting for transfers between devices: 89.9 us -> 78.1 us  [return_wgrad(): lax.ppermute(summed[at], 'dp', chip_pairs(step))]
    unnamed x153 -> x127, local copies, waits for them, and re-layouts: 30.8 us -> 25.5 us
  transfers between devices with their start and end apart: 56 -> 56, of which waited for: 25 -> 26; matrix products, arithmetic and copies ran while one was open for 16% -> 15% of each run, Pallas kernels for 10% -> 10%
where the time goes in v4:
time: 1020 us; the launch traced here: 1010 us
  waiting for transfers between devices  568 us (56%)
  Pallas kernels  156 us (15%)
  starting transfers between devices  96.3 us (9%)
  local copies, waits for them, and re-layouts  78.5 us (8%)
  other arithmetic  58 us (6%)
  matrix products  37.4 us (4%)
  between operations  15.5 us (2%)
    ppermute x19, waiting for transfers between devices, to_peer(): return lax.ppermute(values, 'tensor', [(0, 1), (1, 0)])  189 us
    ppermute x7, waiting for transfers between devices, fetch_experts(): lax.ppermute(packed_experts[step], 'dp', chip_pairs(step))  143 us
    ppermute x7, waiting for transfers between devices, return_wgrad(): lax.ppermute(summed[at], 'dp', chip_pairs(step))  78.1 us
    pallas_call x1, Pallas kernels, expert_rows(): pl.pallas_call(rows_kernel, grid_spec=pltpu.PrefetchScalarGridSpec(num_sc...  55.8 us
    all_to_all x2, waiting for transfers between devices, send_back(): back = lax.all_to_all(back, 'dp', split_axis=0, concat_axis=0, tiled=True)  35 us
    pallas_call x1, Pallas kernels, expert_wgrads(): pl.pallas_call(wgrad_kernel, grid_spec=pltpu.PrefetchScalarGridSpec(num_s...  34.8 us
    all_to_all x1, waiting for transfers between devices, body(): got = lax.all_to_all(sent, 'dp', split_axis=0, concat_axis=0, tiled=True)  31 us
    unnamed x127, local copies, waits for them, and re-layouts  25.5 us
  transfers between devices with their start and end apart: 56, of which 26 were waited for; matrix products, arithmetic and copies ran while one was open for 15% of the time, Pallas kernels for 10%

profile of v4, /device:TPU:17, one launch (start us, length us, event | category | flops | bytes accessed | tf_op | source)
XLA Modules:
  0.0 1010.1 jit_solution(6555838393717464574)
XLA Ops:
  13.1 10.3 %shard_map.272 = (bf16[8,128,1536]{2,1,0:T(8,128)(2,1)}, bf16[8,128,1536]{2,1,0:T(8,128)(2,1)}) custom-call(s32[2]{0:T(128)} %pad_add_fusion.3.place_ref, f32[16,128,512]{2,1,0:T(8,128)} %gate_ref.1, f32[16,128,512]{2,1,0:T(8,128)} %up_ref.1, f32[16,512,128]{2,1,0:T(8,128)} %down_ref.1), custom_call_target="tpu_custom_call" | custom-call | tf_op jit(solution)/shard_map/pallas_call | solution.py:142
  35.2 8.7 shard_map.273
  43.8 31.0 %all-to-all-done = bf16[16,16,2208]{2,1,0:T(8,128)(2,1)S(1)} async-done(((bf16[16,16,2208]{2,1,0:T(8,128)(2,1)}), bf16[16,16,2208]{2,1,0:T(8,128)(2,1)S(1)}, u32[]{:S(2)}, u32[]{:S(2)}) %all-to-all-start) | async-done | bytes 1130528 | tf_op jit(solution)/shard_map/all_to_all | solution.py:531
  92.1 78.6 %collective-permute-done.6 = bf16[256,1536]{1,0:T(8,128)(2,1)} collective-permute-done((bf16[256,1536]{1,0:T(8,128)(2,1)S(1)}, bf16[256,1536]{1,0:T(8,128)(2,1)}, u32[]{:S(2)}, u32[]{:S(2)}) %collective-permute-start.6) | collective-permute-done | bytes 786464 | tf_op jit(solution)/shard_map/ppermute | solution.py:567
  170.7 21.4 %collective-permute-done.5 = bf16[256,1536]{1,0:T(8,128)(2,1)} collective-permute-done((bf16[256,1536]{1,0:T(8,128)(2,1)S(1)}, bf16[256,1536]{1,0:T(8,128)(2,1)}, u32[]{:S(2)}, u32[]{:S(2)}) %collective-permute-start.5) | collective-permute-done | bytes 786464 | tf_op jit(solution)/shard_map/ppermute | solution.py:567
  209.1 8.9 shard_map.274
  218.0 21.1 %all-gather.7.cloned.1.call-done = bf16[2048,1024]{0,1:T(8,128)(2,1)} async-done(((bf16[128,1024]{0,1:T(8,128)(2,1)}), bf16[2048,1024]{0,1:T(8,128)(2,1)}) %all-gather.7.cloned.1.call-update) | async-done | bytes 4194320 | tf_op jit(solution)/shard_map/all_gather | solution.py:575
  244.1 12.1 %collective-permute-done.10 = bf16[128,2048]{1,0:T(8,128)(2,1)S(1)} collective-permute-done((bf16[128,2048]{1,0:T(8,128)(2,1)S(1)}, bf16[128,2048]{1,0:T(8,128)(2,1)S(1)}, u32[]{:S(2)}, u32[]{:S(2)}) %collective-permute-start.10) | collective-permute-done | bytes 524320 | tf_op jit(solution)/shard_map/ppermute | solution.py:86
  256.6 40.9 %collective-permute-done.11 = bf16[256,1536]{1,0:T(8,128)(2,1)S(1)} collective-permute-done((bf16[256,1536]{1,0:T(8,128)(2,1)S(1)}, bf16[256,1536]{1,0:T(8,128)(2,1)S(1)}, u32[]{:S(2)}, u32[]{:S(2)}) %collective-permute-start.11) | collective-permute-done | bytes 786464 | tf_op jit(solution)/shard_map/ppermute | solution.py:567
  299.3 9.6 reduce-scatter.4.cloned.1.call-start
  328.0 46.7 %collective-permute-done.14 = bf16[256,1536]{1,0:T(8,128)(2,1)S(1)} collective-permute-done((bf16[256,1536]{1,0:T(8,128)(2,1)}, bf16[256,1536]{1,0:T(8,128)(2,1)S(1)}, u32[]{:S(2)}, u32[]{:S(2)}) %collective-permute-start.14) | collective-permute-done | bytes 786464 | tf_op jit(solution)/shard_map/ppermute | solution.py:86
  394.7 15.0 %collective-permute-done.18 = bf16[256,1536]{1,0:T(8,128)(2,1)S(1)} collective-permute-done((bf16[256,1536]{1,0:T(8,128)(2,1)S(1)}, bf16[256,1536]{1,0:T(8,128)(2,1)S(1)}, u32[]{:S(2)}, u32[]{:S(2)}) %collective-permute-start.18) | collective-permute-done | bytes 786464 | tf_op jit(solution)/shard_map/ppermute | solution.py:86
  410.6 20.0 %all-gather.9.cloned.1.call-done.rows_ref = bf16[2048,2048]{1,0:T(8,128)(2,1)} async-done(((bf16[128,2048]{1,0:T(8,128)(2,1)}), bf16[2048,2048]{1,0:T(8,128)(2,1)}) %all-gather.9.cloned.1.call-update) | async-done | bytes 8388624 | tf_op jit(solution)/shard_map/all_gather | solution.py:661
  430.6 55.8 %shard_map.275 = (bf16[2048,2048]{1,0:T(8,128)(2,1)}, bf16[2048,1024]{1,0:T(8,128)(2,1)}, bf16[2048,2048]{1,0:T(8,128)(2,1)}, bf16[2048,2048]{1,0:T(8,128)(2,1)}, f32[2048,1]{1,0:T(8,128)S(1)}) custom-call(s32[1]{0:T(128)} %bitcast.33.expert_ref, bf16[2048,2048]{1,0:T(8,128)(2,1)} %all-gather.9.cloned.1.call-done.rows_ref, ...), custom_call_target="tpu_custom_call" | custom-call | flops 1024 | bytes 1024 | tf_op jit(solution)/shard_map/pallas_call | solution.py:253
  488.7 34.8 %shard_map.277 = (bf16[6,256,1536]{2,1,0:T(8,128)(2,1)}, bf16[2,256,1536]{2,1,0:T(8,128)(2,1)S(1)}, bf16[8,256,1536]{2,1,0:T(8,128)(2,1)}) custom-call(s32[8]{0:T(128)S(1)} %stack.112.order_ref, bf16[2048,2048]{1,0:T(8,128)(2,1)} %all-gather.9.cloned.1.call-done.rows_ref, bf16[2048,2048]{1,0:T(8,128)(2,1)} %get-tuple-element.76.cells_ref, ...), custom_call_target="tpu_custom_call" | custom-call | flops 1024 | bytes 1024 | tf_op jit(solution)/shard_map/pallas_call | solution.py:324
  526.0 16.4 %shard_map.276 = (bf16[2048,2048]{1,0:T(8,128)(2,1)}, f32[2048,1]{1,0:T(8,128)S(1)}) custom-call(bf16[2048,1024]{1,0:T(8,128)(2,1)} %get-tuple-element.72.active_ref, bf16[2048,2048]{1,0:T(8,128)(2,1)} %all-gather.11.cloned.1.call-done.cot_ref, f32[2048,1]{1,0:T(8,128)S(1)} %get-tuple-element.73.gate_ref, ...), custom_call_target="tpu_custom_call" | custom-call | flops 1024 | bytes 1024 | tf_op jit(solution)/shard_map/pallas_call | solution.py:283
  555.6 72.6 %collective-permute-done.20 = bf16[6,256,1536]{2,1,0:T(8,128)(2,1)} collective-permute-done((bf16[6,256,1536]{2,1,0:T(8,128)(2,1)}, bf16[6,256,1536]{2,1,0:T(8,128)(2,1)}, u32[]{:S(2)}, u32[]{:S(2)}) %collective-permute-start.20) | collective-permute-done | bytes 4718624 | tf_op jit(solution)/shard_map/ppermute | solution.py:86
  628.2 7.4 add_convert_fusion
  642.5 9.3 collective-permute-done.19
  654.0 11.4 %shard_map.278 = (f32[256,1024]{1,0:T(8,128)}, f32[256,1024]{1,0:T(8,128)}, bf16[256,1024]{1,0:T(8,128)(2,1)}, f32[2,1024]{1,0:T(2,128)}, f32[2,256,1]{2,1,0:T(8,128)}) custom-call(f32[256,3072]{1,0:T(8,128)} %copy-done.5, f32[256,3072]{1,0:T(8,128)} %copy-done.5, f32[256,3072]{1,0:T(8,128)} %copy-done.5, f32[2,256,1]{2,1,0:T(8,128)} %rsqrt.33.scale_ref, ...), custom_call_target="tpu_custom_call" | custom-call | flops 1024 | bytes 1024 | tf_op jit(solution)/shard_map/pallas_call | solution.py:439
  672.3 6.6 fusion.46
  681.0 6.8 convolution_convert_fusion
  687.9 14.7 %collective-permute-done.28 = bf16[2,256,1536]{2,1,0:T(8,128)(2,1)S(1)} collective-permute-done((bf16[2,256,1536]{2,1,0:T(8,128)(2,1)S(1)}, bf16[2,256,1536]{2,1,0:T(8,128)(2,1)S(1)}, u32[]{:S(2)}, u32[]{:S(2)}) %collective-permute-start.28) | collective-permute-done | bytes 1572896 | tf_op jit(solution)/shard_map/ppermute | solution.py:86
  705.7 48.3 %collective-permute-done.27 = bf16[256,1536]{1,0:T(8,128)(2,1)S(1)} collective-permute-done((bf16[256,1536]{1,0:T(8,128)(2,1)}, bf16[256,1536]{1,0:T(8,128)(2,1)S(1)}, u32[]{:S(2)}, u32[]{:S(2)}) %collective-permute-start.27) | collective-permute-done | bytes 786464 | tf_op jit(solution)/shard_map/ppermute | solution.py:717
  782.5 18.2 %collective-permute-start.33 = (bf16[128,3072]{1,0:T(8,128)(2,1)}, bf16[128,3072]{1,0:T(8,128)(2,1)}, u32[]{:S(2)}, u32[]{:S(2)}) collective-permute-start(bf16[128,3072]{1,0:T(8,128)(2,1)} %add_convert_fusion.5), channel_id=1, source_target_pairs={{0,8},{2,6},{8,16},{10,2},{16,24},{18,10},{24,28},{26,18},{28,20},... | collective-permute-start | bytes 2359304 | tf_op jit(solution)/shard_map/ppermute | solution.py:106
  808.5 19.8 %collective-permute-done.33 = bf16[128,3072]{1,0:T(8,128)(2,1)} collective-permute-done((bf16[128,3072]{1,0:T(8,128)(2,1)}, bf16[128,3072]{1,0:T(8,128)(2,1)}, u32[]{:S(2)}, u32[]{:S(2)}) %collective-permute-start.33) | collective-permute-done | bytes 786464 | tf_op jit(solution)/shard_map/ppermute | solution.py:106
  842.3 7.1 all-to-all-start.2
  854.1 10.8 %collective-permute-done.35 = bf16[256,3072]{1,0:T(8,128)(2,1)} collective-permute-done((bf16[256,3072]{1,0:T(8,128)(2,1)}, bf16[256,3072]{1,0:T(8,128)(2,1)}, u32[]{:S(2)}, u32[]{:S(2)}) %collective-permute-start.35) | collective-permute-done | bytes 1572896 | tf_op jit(solution)/shard_map/ppermute | solution.py:112
  875.2 35.0 %all-to-all-done.2 = bf16[16,8,2048]{2,1,0:T(8,128)(2,1)} async-done(((bf16[16,8,2048]{2,1,0:T(8,128)(2,1)}), bf16[16,8,2048]{2,1,0:T(8,128)(2,1)}, u32[]{:S(2)}, u32[]{:S(2)}) %all-to-all-start.2) | async-done | bytes 524320 | tf_op jit(solution)/shard_map/all_to_all | solution.py:797
  925.2 29.8 %collective-permute-done.42 = bf16[256,1536]{1,0:T(8,128)(2,1)S(1)} collective-permute-done((bf16[256,1536]{1,0:T(8,128)(2,1)}, bf16[256,1536]{1,0:T(8,128)(2,1)S(1)}, u32[]{:S(2)}, u32[]{:S(2)}) %collective-permute-start.42) | collective-permute-done | bytes 786464 | tf_op jit(solution)/shard_map/ppermute | solution.py:717
  966.2 13.6 %collective-permute-done.37 = bf16[256,3072]{1,0:T(8,128)(2,1)S(1)} collective-permute-done((bf16[256,3072]{1,0:T(8,128)(2,1)S(1)}, bf16[256,3072]{1,0:T(8,128)(2,1)S(1)}, u32[]{:S(2)}, u32[]{:S(2)}) %collective-permute-start.37) | collective-permute-done | bytes 1572896 | tf_op jit(solution)/shard_map/ppermute | solution.py:112
  988.7 9.5 shard_map.279
  (392 shorter events, 242.4 us)
Async XLA Ops:
  7.2 187.6 %all-gather.5.cloned.1.call-start = ((), (), s32[]{:S(2)}) async-start(), calls=%async_computation.8 | async-start | bytes 13369344 | tf_op jit(solution)/shard_map/all_gather | solution.py:574
  11.6 227.5 %all-gather.7.cloned.1.call-start = ((), (), s32[]{:S(2)}) async-start(), calls=%async_computation.9 | async-start | bytes 4456448 | tf_op jit(solution)/shard_map/all_gather | solution.py:575
  29.2 45.6 %all-to-all-start = ((bf16[16,16,2208]{2,1,0:T(8,128)(2,1)}), bf16[16,16,2208]{2,1,0:T(8,128)(2,1)S(1)}, u32[]{:S(2)}, u32[]{:S(2)}) async-start(bf16[16,16,2208]{2,1,0:T(8,128)(2,1)} %concatenate.100), calls=%async_computation | async-start | bytes 2359296 | tf_op jit(solution)/shard_map/all_to_all | solution.py:531
  35.1 375.5 %all-gather.11.cloned.1.call-start = ((), (), s32[]{:S(2)}) async-start(), calls=%async_computation.11 | async-start | bytes 8912896 | tf_op jit(solution)/shard_map/all_gather | solution.py:662
  75.8 354.8 %all-gather.9.cloned.1.call-start = ((), (), s32[]{:S(2)}) async-start(), calls=%async_computation.10 | async-start | bytes 8912896 | tf_op jit(solution)/shard_map/all_gather | solution.py:661
  82.7 88.0 %collective-permute-start.6 = (bf16[256,1536]{1,0:T(8,128)(2,1)S(1)}, bf16[256,1536]{1,0:T(8,128)(2,1)}, u32[]{:S(2)}, u32[]{:S(2)}) collective-permute-start(bf16[256,1536]{1,0:T(8,128)(2,1)S(1)} %get-tuple-element.212), channel_id=1, source_target_pairs={{0,24},{2,26},{4,28},{6,30},{8,16},{10,18},{12,20},{14,22},{16,8},... | collective-permute-start | bytes 2359304 | tf_op jit(solution)/shard_map/ppermute | solution.py:567
  82.7 109.4 %collective-permute-start.5 = (bf16[256,1536]{1,0:T(8,128)(2,1)S(1)}, bf16[256,1536]{1,0:T(8,128)(2,1)}, u32[]{:S(2)}, u32[]{:S(2)}) collective-permute-start(bf16[256,1536]{1,0:T(8,128)(2,1)S(1)} %get-tuple-element.213), channel_id=1, source_target_pairs={{0,16},{2,18},{4,20},{6,22},{8,24},{10,26},{12,28},{14,30},{16,0},... | collective-permute-start | bytes 2359304 | tf_op jit(solution)/shard_map/ppermute | solution.py:567
  83.6 108.6 %collective-permute-start.4 = (bf16[256,1536]{1,0:T(8,128)(2,1)S(1)}, bf16[256,1536]{1,0:T(8,128)(2,1)S(1)}, u32[]{:S(2)}, u32[]{:S(2)}) collective-permute-start(bf16[256,1536]{1,0:T(8,128)(2,1)S(1)} %get-tuple-element.214), channel_id=1, source_target_pairs={{0,12},{2,14},{4,8},{6,10},{8,4},{10,6},{12,0},{14,2},{16,28},{18,... | collective-permute-start | bytes 2359304 | tf_op jit(solution)/shard_map/ppermute | solution.py:567
  85.5 108.5 %collective-permute-start.3 = (bf16[256,1536]{1,0:T(8,128)(2,1)S(1)}, bf16[256,1536]{1,0:T(8,128)(2,1)S(1)}, u32[]{:S(2)}, u32[]{:S(2)}) collective-permute-start(bf16[256,1536]{1,0:T(8,128)(2,1)S(1)} %get-tuple-element.215), channel_id=1, source_target_pairs={{0,8},{2,10},{4,12},{6,14},{8,0},{10,2},{12,4},{14,6},{16,24},{18,... | collective-permute-start | bytes 2359304 | tf_op jit(solution)/shard_map/ppermute | solution.py:567
  90.3 104.5 %collective-permute-start.2 = (bf16[256,1536]{1,0:T(8,128)(2,1)S(1)}, bf16[256,1536]{1,0:T(8,128)(2,1)}, u32[]{:S(2)}, u32[]{:S(2)}) collective-permute-start(bf16[256,1536]{1,0:T(8,128)(2,1)S(1)} %get-tuple-element.216), channel_id=1, source_target_pairs={{0,4},{2,6},{4,0},{6,2},{8,12},{10,14},{12,8},{14,10},{16,20},{18,... | collective-permute-start | bytes 2359304 | tf_op jit(solution)/shard_map/ppermute | solution.py:567
  244.1 53.4 %collective-permute-start.11 = (bf16[256,1536]{1,0:T(8,128)(2,1)S(1)}, bf16[256,1536]{1,0:T(8,128)(2,1)S(1)}, u32[]{:S(2)}, u32[]{:S(2)}) collective-permute-start(bf16[256,1536]{1,0:T(8,128)(2,1)S(1)} %get-tuple-element.66), channel_id=1, source_target_pairs={{0,28},{2,30},{4,24},{6,26},{8,20},{10,22},{12,16},{14,18},{16,12}... | collective-permute-start | bytes 2359304 | tf_op jit(solution)/shard_map/ppermute | solution.py:567
  299.3 336.3 %reduce-scatter.4.cloned.1.call-start = ((), (), s32[]{:S(2)}) async-start(), calls=%async_computation.12 | async-start | bytes 8912896 | tf_op jit(solution)/shard_map/reduce_scatter | solution.py:675
  314.1 62.6 %collective-permute-start.16 = (bf16[256,1536]{1,0:T(8,128)(2,1)S(1)}, bf16[256,1536]{1,0:T(8,128)(2,1)S(1)}, u32[]{:S(2)}, u32[]{:S(2)}) collective-permute-start(bf16[256,1536]{1,0:T(8,128)(2,1)S(1)} %copy-done.33), channel_id=1, source_target_pairs={{0,1},{1,0},{2,3},{3,2},{4,5},{5,4},{6,7},{7,6},{8,9},{9,8},{10,11... | collective-permute-start | bytes 2359304 | tf_op jit(solution)/shard_map/ppermute | solution.py:86
  315.4 60.3 %collective-permute-start.15 = (bf16[256,1536]{1,0:T(8,128)(2,1)S(1)}, bf16[256,1536]{1,0:T(8,128)(2,1)S(1)}, u32[]{:S(2)}, u32[]{:S(2)}) collective-permute-start(bf16[256,1536]{1,0:T(8,128)(2,1)S(1)} %copy-done.35), channel_id=1, source_target_pairs={{0,1},{1,0},{2,3},{3,2},{4,5},{5,4},{6,7},{7,6},{8,9},{9,8},{10,11... | collective-permute-start | bytes 2359304 | tf_op jit(solution)/shard_map/ppermute | solution.py:86
  315.5 59.2 %collective-permute-start.14 = (bf16[256,1536]{1,0:T(8,128)(2,1)}, bf16[256,1536]{1,0:T(8,128)(2,1)S(1)}, u32[]{:S(2)}, u32[]{:S(2)}) collective-permute-start(bf16[256,1536]{1,0:T(8,128)(2,1)} %collective-permute-done.2), channel_id=1, source_target_pairs={{0,1},{1,0},{2,3},{3,2},{4,5},{5,4},{6,7},{7,6},{8,9},{9,8},{10,11... | collective-permute-start | bytes 2359304 | tf_op jit(solution)/shard_map/ppermute | solution.py:86
  328.0 51.7 %collective-permute-start.12 = (bf16[256,1536]{1,0:T(8,128)(2,1)S(1)}, bf16[256,1536]{1,0:T(8,128)(2,1)S(1)}, u32[]{:S(2)}, u32[]{:S(2)}) collective-permute-start(bf16[256,1536]{1,0:T(8,128)(2,1)S(1)} %copy-done.29), channel_id=1, source_target_pairs={{0,20},{2,22},{4,16},{6,18},{8,28},{10,30},{12,24},{14,26},{16,4},... | collective-permute-start | bytes 2359304 | tf_op jit(solution)/shard_map/ppermute | solution.py:567
  486.4 314.3 %reduce-scatter.6.cloned.1.call-start = ((), (), s32[]{:S(2)}) async-start(), calls=%async_computation.13 | async-start | bytes 8912896 | tf_op jit(solution)/shard_map/reduce_scatter | solution.py:675
  524.7 103.5 %collective-permute-start.20 = (bf16[6,256,1536]{2,1,0:T(8,128)(2,1)}, bf16[6,256,1536]{2,1,0:T(8,128)(2,1)}, u32[]{:S(2)}, u32[]{:S(2)}) collective-permute-start(bf16[6,256,1536]{2,1,0:T(8,128)(2,1)} %get-tuple-element.85), channel_id=1, source_target_pairs={{0,1},{1,0},{2,3},{3,2},{4,5},{5,4},{6,7},{7,6},{8,9},{9,8},{10,11... | collective-permute-start | bytes 14155784 | tf_op jit(solution)/shard_map/ppermute | solution.py:86
  667.8 86.2 %collective-permute-start.26 = (bf16[256,1536]{1,0:T(8,128)(2,1)S(1)}, bf16[256,1536]{1,0:T(8,128)(2,1)S(1)}, u32[]{:S(2)}, u32[]{:S(2)}) collective-permute-start(bf16[256,1536]{1,0:T(8,128)(2,1)S(1)} %get-tuple-element.222), channel_id=1, source_target_pairs={{0,16},{2,18},{4,20},{6,22},{8,24},{10,26},{12,28},{14,30},{16,0},... | collective-permute-start | bytes 2359304 | tf_op jit(solution)/shard_map/ppermute | solution.py:717
  669.2 84.7 %collective-permute-start.27 = (bf16[256,1536]{1,0:T(8,128)(2,1)}, bf16[256,1536]{1,0:T(8,128)(2,1)S(1)}, u32[]{:S(2)}, u32[]{:S(2)}) collective-permute-start(bf16[256,1536]{1,0:T(8,128)(2,1)} %get-tuple-element.221), channel_id=1, source_target_pairs={{0,24},{2,26},{4,28},{6,30},{8,16},{10,18},{12,20},{14,22},{16,8},... | collective-permute-start | bytes 2359304 | tf_op jit(solution)/shard_map/ppermute | solution.py:717
  679.8 85.4 %collective-permute-start.23 = (bf16[128,2048]{1,0:T(8,128)(2,1)}, bf16[128,2048]{1,0:T(8,128)(2,1)}, u32[]{:S(2)}, u32[]{:S(2)}) collective-permute-start(bf16[128,2048]{1,0:T(8,128)(2,1)} %slice.324), channel_id=1, source_target_pairs={{0,1},{1,0},{2,3},{3,2},{4,5},{5,4},{6,7},{7,6},{8,9},{9,8},{10,11... | collective-permute-start | bytes 1572872 | tf_op jit(solution)/shard_map/ppermute | solution.py:86
  773.4 63.3 %collective-permute-start.39 = (bf16[256,1536]{1,0:T(8,128)(2,1)}, bf16[256,1536]{1,0:T(8,128)(2,1)}, u32[]{:S(2)}, u32[]{:S(2)}) collective-permute-start(bf16[256,1536]{1,0:T(8,128)(2,1)} %get-tuple-element.219), channel_id=1, source_target_pairs={{0,4},{2,6},{4,0},{6,2},{8,12},{10,14},{12,8},{14,10},{16,20},{18,... | collective-permute-start | bytes 2359304 | tf_op jit(solution)/shard_map/ppermute | solution.py:717
  774.6 57.9 %collective-permute-start.34 = (bf16[256,1536]{1,0:T(8,128)(2,1)}, bf16[256,1536]{1,0:T(8,128)(2,1)}, u32[]{:S(2)}, u32[]{:S(2)}) collective-permute-start(bf16[256,1536]{1,0:T(8,128)(2,1)} %get-tuple-element.220), channel_id=1, source_target_pairs={{0,20},{2,22},{4,16},{6,18},{8,28},{10,30},{12,24},{14,26},{16,4},... | collective-permute-start | bytes 2359304 | tf_op jit(solution)/shard_map/ppermute | solution.py:717
  774.6 53.6 %collective-permute-start.31 = (bf16[256,3072]{1,0:T(8,128)(2,1)}, bf16[256,3072]{1,0:T(8,128)(2,1)}, u32[]{:S(2)}, u32[]{:S(2)}) collective-permute-start(bf16[256,3072]{1,0:T(8,128)(2,1)} %get-tuple-element.207), channel_id=1, source_target_pairs={{0,2},{2,0},{4,6},{6,4},{8,10},{10,8},{12,14},{14,12},{16,18},{18,... | collective-permute-start | bytes 4718600 | tf_op jit(solution)/shard_map/ppermute | solution.py:82
  782.5 45.7 %collective-permute-start.33 = (bf16[128,3072]{1,0:T(8,128)(2,1)}, bf16[128,3072]{1,0:T(8,128)(2,1)}, u32[]{:S(2)}, u32[]{:S(2)}) collective-permute-start(bf16[128,3072]{1,0:T(8,128)(2,1)} %add_convert_fusion.5), channel_id=1, source_target_pairs={{0,8},{2,6},{8,16},{10,2},{16,24},{18,10},{24,28},{26,18},{28,20},... | collective-permute-start | bytes 2359304 | tf_op jit(solution)/shard_map/ppermute | solution.py:106
  808.1 190.2 %reduce-scatter.8.cloned.1.call-start = ((), (), s32[]{:S(2)}) async-start(), calls=%async_computation.14 | async-start | bytes 4456448 | tf_op jit(solution)/shard_map/reduce_scatter | solution.py:751
  808.2 45.9 %collective-permute-start.30 = (bf16[256,3072]{1,0:T(8,128)(2,1)}, bf16[256,3072]{1,0:T(8,128)(2,1)}, u32[]{:S(2)}, u32[]{:S(2)}) collective-permute-start(bf16[256,3072]{1,0:T(8,128)(2,1)} %get-tuple-element.208), channel_id=1, source_target_pairs={{0,2},{2,0},{4,6},{6,4},{8,10},{10,8},{12,14},{14,12},{16,18},{18,... | collective-permute-start | bytes 4718600 | tf_op jit(solution)/shard_map/ppermute | solution.py:82
  834.6 79.8 %collective-permute-start.41 = (bf16[256,1536]{1,0:T(8,128)(2,1)S(1)}, bf16[256,1536]{1,0:T(8,128)(2,1)}, u32[]{:S(2)}, u32[]{:S(2)}) collective-permute-start(bf16[256,1536]{1,0:T(8,128)(2,1)S(1)} %copy-done.28), channel_id=1, source_target_pairs={{0,12},{2,14},{4,8},{6,10},{8,4},{10,6},{12,0},{14,2},{16,28},{18,... | collective-permute-start | bytes 2359304 | tf_op jit(solution)/shard_map/ppermute | solution.py:717
  834.7 75.5 %collective-permute-start.40 = (bf16[256,1536]{1,0:T(8,128)(2,1)}, bf16[256,1536]{1,0:T(8,128)(2,1)}, u32[]{:S(2)}, u32[]{:S(2)}) collective-permute-start(bf16[256,1536]{1,0:T(8,128)(2,1)} %get-tuple-element.218), channel_id=1, source_target_pairs={{0,8},{2,10},{4,12},{6,14},{8,0},{10,2},{12,4},{14,6},{16,24},{18,... | collective-permute-start | bytes 2359304 | tf_op jit(solution)/shard_map/ppermute | solution.py:717
  842.3 67.8 %all-to-all-start.2 = ((bf16[16,8,2048]{2,1,0:T(8,128)(2,1)}), bf16[16,8,2048]{2,1,0:T(8,128)(2,1)}, u32[]{:S(2)}, u32[]{:S(2)}) async-start(bf16[16,8,2048]{2,1,0:T(8,128)(2,1)} %bitcast.54), calls=%async_computation.4 | async-start | bytes 1048576 | tf_op jit(solution)/shard_map/all_to_all | solution.py:797
  849.4 107.4 %collective-permute-start.29 = (bf16[256,3072]{1,0:T(8,128)(2,1)S(1)}, bf16[256,3072]{1,0:T(8,128)(2,1)}, u32[]{:S(2)}, u32[]{:S(2)}) collective-permute-start(bf16[256,3072]{1,0:T(8,128)(2,1)S(1)} %copy-done.24), channel_id=1, source_target_pairs={{0,2},{2,0},{4,6},{6,4},{8,10},{10,8},{12,14},{14,12},{16,18},{18,... | collective-permute-start | bytes 4718600 | tf_op jit(solution)/shard_map/ppermute | solution.py:82
  869.3 87.5 %collective-permute-start.36 = (bf16[256,3072]{1,0:T(8,128)(2,1)}, bf16[256,3072]{1,0:T(8,128)(2,1)}, u32[]{:S(2)}, u32[]{:S(2)}) collective-permute-start(bf16[256,3072]{1,0:T(8,128)(2,1)} %add_convert_fusion.2), channel_id=1, source_target_pairs={{0,8},{2,6},{8,16},{10,2},{16,24},{18,10},{24,28},{26,18},{28,20},... | collective-permute-start | bytes 4718600 | tf_op jit(solution)/shard_map/ppermute | solution.py:112
  (79 other events, 1437.3 us)
Sparse Core Ops, SparseCore 0:
  11.7 170.2 all-gather.4
  184.7 54.3 all-gather.6
  241.3 109.1 all-gather.10
  353.0 77.5 all-gather.8
  486.5 103.0 reduce-scatter.3
  593.6 136.4 reduce-scatter.5
  842.5 96.0 reduce-scatter.7

commit v5 on v4

--- a/solution.py
+++ b/solution.py
@@ -294,51 +294,52 @@
     )(active, cot_rows, gates, own, peer)
 
 
-def wgrad_kernel(
-    order_ref, rows_ref, cells_ref, front_grad_ref, active_ref, first_ref, last_ref, own_ref
-):
-    number, early = pl.program_id(0), 3 * pl.num_programs(0) // 4
+PARTS = 4
+
+
+def wgrad_kernel(order_ref, rows_ref, cells_ref, front_grad_ref, active_ref, *out_refs):
+    number, many = pl.program_id(0), pl.num_programs(0) // PARTS
     width = active_ref.shape[1] // 2
     front = mm(rows_ref[...].T, front_grad_ref[...]).astype(BF16)
     down = mm(cells_ref[...].T, active_ref[...]).astype(BF16)
-    own_ref[0, :, : 2 * width] = front[:, : 2 * width]
-    own_ref[0, :, 2 * width :] = down[:, :width]
-    for wanted, out_ref in ((number < early, first_ref), (number >= early, last_ref)):
-
-        @pl.when(wanted)
+    for part in range(PARTS):
+
+        @pl.when((number >= part * many) & (number < (part + 1) * many))
         def _():
-            out_ref[0, :, : 2 * width] = front[:, 2 * width :]
-            out_ref[0, :, 2 * width :] = down[:, width:]
+            own_ref, peer_ref = out_refs[part], out_refs[PARTS + part]
+            own_ref[0, :, : 2 * width] = front[:, : 2 * width]
+            own_ref[0, :, 2 * width :] = down[:, :width]
+            peer_ref[0, :, : 2 * width] = front[:, 2 * width :]
+            peer_ref[0, :, 2 * width :] = down[:, width:]
 
 
 def expert_wgrads(order, rows, cells, front_grad, active):
     count, model_width = rows.shape
     blocks = order.shape[0]
-    early = 3 * blocks // 4
+    many = blocks // PARTS
     size, width = model_width // blocks, active.shape[1] // 2
     columns = pl.BlockSpec((count, size), lambda i, o: (0, o[i]))
     whole = lambda values: pl.BlockSpec(
         values.shape, lambda i, o: (0, 0), pipeline_mode=pl.Buffered(1)
     )
-    part = (1, size, 3 * width)
-    return pl.pallas_call(
+    block = (1, size, 3 * width)
+
+    def of_part(part):
+        return pl.BlockSpec(block, lambda i, o: (jnp.clip(i - part * many, 0, many - 1), 0, 0))
+
+    found = pl.pallas_call(
         wgrad_kernel,
         grid_spec=pltpu.PrefetchScalarGridSpec(
             num_scalar_prefetch=1,
             grid=(blocks,),
             in_specs=[columns, columns, whole(front_grad), whole(active)],
-            out_specs=[
-                pl.BlockSpec(part, lambda i, o: (jnp.minimum(i, early - 1), 0, 0)),
-                pl.BlockSpec(part, lambda i, o: (jnp.maximum(i - early, 0), 0, 0)),
-                pl.BlockSpec(part, lambda i, o: (i, 0, 0)),
-            ],
+            out_specs=[of_part(part) for part in range(PARTS)] * 2,
         ),
-        out_shape=[
-            jax.ShapeDtypeStruct((many, size, 3 * width), BF16) for many in (early, blocks - early, blocks)
-        ],
+        out_shape=[jax.ShapeDtypeStruct((many,) + block[1:], BF16)] * (2 * PARTS),
         compiler_params=pltpu.CompilerParams(vmem_limit_bytes=ROW_VMEM),
         cost_estimate=LIGHT,
     )(order, rows, cells, front_grad, active)
+    return found[:PARTS], found[PARTS:]
 
 
 def attention_kernel(
@@ -675,15 +676,10 @@
         return lax.psum_scatter(values, "dp", scatter_dimension=0, tiled=True, **in_group)
 
     steps_back = [4, 1, 6, 2, 5, 3, 7, 0]
-    early = 3 * moe_chips // 4
     chips_back = jnp.stack([expert_chip ^ step for step in steps_back]).astype(jnp.int32)
     block_order = chips_back if replicas == 1 else jnp.arange(moe_chips, dtype=jnp.int32)
-    wgrad_first, wgrad_last, wgrad_own = expert_wgrads(
-        block_order, inputs_all, cells, front_grad, active
-    )
-    normed_two_grad = after(sum_experts(input_grad), wgrad_own)
-    if replicas == 1:
-        peer_first = to_peer(wgrad_first)
+    wgrad_own, wgrad_peer = expert_wgrads(block_order, inputs_all, cells, front_grad, active)
+    normed_two_grad = after(sum_experts(input_grad), wgrad_own[0])
     mixed, mixing = expert_mixture(active, cot_all, gates, expert_own, expert_peer, rows_here)
     normed_two_grad = normed_two_grad.astype(F32)
     mixing_table = to_experts(mixing.reshape(EXPERTS, -1))
@@ -702,21 +698,24 @@
             )
             return jnp.take(values.reshape(moe_chips, -1, values.shape[1]), chips_back, axis=0)
 
-        wgrad_own = over_replicas(wgrad_own)
-        wgrad_peer = over_replicas(jnp.concatenate([wgrad_first, wgrad_last], 0))
-        wgrad_first, wgrad_last = wgrad_peer[:early], wgrad_peer[early:]
-        peer_first = to_peer(wgrad_first)
-
-    def add_wgrads(own, theirs):
-        return list((own.astype(F32) + theirs.astype(F32)).astype(BF16))
-
-    summed = add_wgrads(wgrad_own[:early], peer_first)
-
-    def return_wgrad(at):
-        step = steps_back[at]
-        return lax.ppermute(summed[at], "dp", chip_pairs(step)) if step > 0 else summed[at]
-
-    wgrad_chunks = [return_wgrad(at) for at in range(early)]
+        wgrad_own, wgrad_peer = (
+            pieces_of(over_replicas(jnp.concatenate(parts, 0)), PARTS)
+            for parts in (wgrad_own, wgrad_peer)
+        )
+    summed, wgrad_chunks, exchanged = [], [], []
+
+    def return_wgrads(part, *others):
+        exchanged.append(to_peer(after(wgrad_peer[part], *others)))
+        chunks = wgrad_own[part].astype(F32) + exchanged[part].astype(F32)
+        for chunk in chunks.astype(BF16):
+            step = steps_back[len(summed)]
+            summed.append(chunk)
+            wgrad_chunks.append(
+                lax.ppermute(chunk, "dp", chip_pairs(step)) if step > 0 else chunk
+            )
+
+    for part in range(PARTS - 1):
+        return_wgrads(part)
 
     prob_grad = mixing_table.T * used
     logit_grad = (
@@ -733,7 +732,7 @@
     attn_own = hidden_grad.astype(BF16)
     attn_peer = to_peer(attn_own)
     attn_grad = jnp.concatenate([attn_own, attn_peer], 0)
-    attn_grad = after(attn_grad, summed[0])
+    attn_grad = after(attn_grad, wgrad_chunks[0], summed[2], summed[4])
     context_grad = mm(attn_grad, output_full).astype(BF16)
     query_norm_grad, key_norm_grad, value_grad, gain_grads, inner_parts = by_heads(
         attention_grad_kernel,
@@ -749,9 +748,7 @@
     inners = over_sides(inner_parts[:, :, 0])
     query_scale, key_scale = scales
     output_wgrad = lax.psum_scatter(output_wgrad, "dp", scatter_dimension=0, tiled=True)
-    peer_last = to_peer(after(wgrad_last, attn_peer))
-    summed += add_wgrads(wgrad_own[early:], peer_last)
-    wgrad_chunks += [return_wgrad(at) for at in range(early, moe_chips)]
+    return_wgrads(PARTS - 1, attn_peer)
     query_raw_grad = (
         query_scale * query_scale_gain * query_norm_grad
         - query_raw * query_scale**3 * inners[0][:, None] / model_width
@@ -800,7 +797,7 @@
 
     block_out = send_back(after(out_rows, qkv_grad))
     token_grad = send_back(rows_grad.astype(BF16))
-    qkv_wgrad = after(qkv_wgrad, wgrad_chunks[0], wgrad_chunks[2], summed[early])
+    qkv_wgrad = after(qkv_wgrad, wgrad_chunks[0], wgrad_chunks[2], summed[6])
     qkv_wgrad = ring_scatter(pieces_of(qkv_wgrad, chips), chips, BF16, ((by_rows, wgrad_chunks[4]), token_grad, block_out))
     returned = jnp.stack(wgrad_chunks).reshape(moe_chips, 2, -1, 3 * hidden_half)
     of_sibling = to_sibling(lax.dynamic_index_in_dim(returned, 1 - core, 1, keepdims=False))

time: 1020 us -> 995 us (0.975)
  starting transfers between devices: 96.3 us -> 70.9 us
    ppermute x7, waiting for transfers between devices: 78.1 us -> 48 us  [return_wgrads(): lax.ppermute(chunk, 'dp', chip_pairs(step))]
    all_to_all x1, waiting for transfers between devices: 3.98 us -> 24.3 us  [body(): lax.all_to_all(small_grad, 'dp', split_axis=0, concat_axis=0, tiled=True)]
    ppermute x1, starting transfers between devices: 18.2 us -> 0.01 us  [ring_scatter(): lax.ppermute((core_part(parts[-1], core) + theirs).astype(kind), 'dp', pa...]
    ppermute x19 -> x21, waiting for transfers between devices: 189 us -> 182 us  [to_peer(): return lax.ppermute(values, 'tensor', [(0, 1), (1, 0)])]
    unnamed x127 -> x149, local copies, waits for them, and re-layouts: 25.5 us -> 27.4 us
  transfers between devices with their start and end apart: 56 -> 58, of which waited for: 26 -> 29; matrix products, arithmetic and copies ran while one was open for 15% -> 16% of each run, Pallas kernels for 10% -> 10%
where the time goes in v5:
time: 995 us; the launch traced here: 986 us
  waiting for transfers between devices  561 us (56%)
  Pallas kernels  158 us (16%)
  local copies, waits for them, and re-layouts  84.4 us (8%)
  starting transfers between devices  70.9 us (7%)
  other arithmetic  56.4 us (6%)
  matrix products  38.9 us (4%)
  between operations  15.8 us (2%)
    ppermute x21, waiting for transfers between devices, to_peer(): return lax.ppermute(values, 'tensor', [(0, 1), (1, 0)])  182 us
    ppermute x7, waiting for transfers between devices, fetch_experts(): lax.ppermute(packed_experts[step], 'dp', chip_pairs(step))  141 us
    pallas_call x1, Pallas kernels, expert_rows(): pl.pallas_call(rows_kernel, grid_spec=pltpu.PrefetchScalarGridSpec(num_sc...  55.8 us
    ppermute x7, waiting for transfers between devices, return_wgrads(): lax.ppermute(chunk, 'dp', chip_pairs(step))  48 us
    pallas_call x1, Pallas kernels, expert_wgrads(): pl.pallas_call(wgrad_kernel, grid_spec=pltpu.PrefetchScalarGridSpec(num_s...  37.6 us
    all_to_all x2, waiting for transfers between devices, send_back(): back = lax.all_to_all(back, 'dp', split_axis=0, concat_axis=0, tiled=True)  36.6 us
    all_to_all x1, waiting for transfers between devices, body(): got = lax.all_to_all(sent, 'dp', split_axis=0, concat_axis=0, tiled=True)  30 us
    all_gather x1, waiting for transfers between devices, body(): lax.all_gather(after(normed_two, own_chunks[7]), 'dp', axis=0, tiled=True...  29.8 us
  transfers between devices with their start and end apart: 58, of which 29 were waited for; matrix products, arithmetic and copies ran while one was open for 16% of the time, Pallas kernels for 10%

profile of v5, /device:TPU:17, one launch (start us, length us, event | category | flops | bytes accessed | tf_op | source)
XLA Modules:
  0.0 985.7 jit_solution(12853735054139152553)
XLA Ops:
  13.1 10.3 %shard_map.272 = (bf16[8,128,1536]{2,1,0:T(8,128)(2,1)}, bf16[8,128,1536]{2,1,0:T(8,128)(2,1)}) custom-call(s32[2]{0:T(128)} %pad_add_fusion.3.place_ref, f32[16,128,512]{2,1,0:T(8,128)} %gate_ref.1, f32[16,128,512]{2,1,0:T(8,128)} %up_ref.1, f32[16,512,128]{2,1,0:T(8,128)} %down_ref.1), custom_call_target="tpu_custom_call" | custom-call | tf_op jit(solution)/shard_map/pallas_call | solution.py:142
  36.2 8.6 shard_map.273
  44.9 30.0 %all-to-all-done = bf16[16,16,2208]{2,1,0:T(8,128)(2,1)S(1)} async-done(((bf16[16,16,2208]{2,1,0:T(8,128)(2,1)}), bf16[16,16,2208]{2,1,0:T(8,128)(2,1)S(1)}, u32[]{:S(2)}, u32[]{:S(2)}) %all-to-all-start) | async-done | bytes 1130528 | tf_op jit(solution)/shard_map/all_to_all | solution.py:532
  92.7 79.3 %collective-permute-done.6 = bf16[256,1536]{1,0:T(8,128)(2,1)S(1)} collective-permute-done((bf16[256,1536]{1,0:T(8,128)(2,1)S(1)}, bf16[256,1536]{1,0:T(8,128)(2,1)S(1)}, u32[]{:S(2)}, u32[]{:S(2)}) %collective-permute-start.6) | collective-permute-done | bytes 786464 | tf_op jit(solution)/shard_map/ppermute | solution.py:568
  172.0 19.6 %collective-permute-done.5 = bf16[256,1536]{1,0:T(8,128)(2,1)} collective-permute-done((bf16[256,1536]{1,0:T(8,128)(2,1)S(1)}, bf16[256,1536]{1,0:T(8,128)(2,1)}, u32[]{:S(2)}, u32[]{:S(2)}) %collective-permute-start.5) | collective-permute-done | bytes 786464 | tf_op jit(solution)/shard_map/ppermute | solution.py:568
  208.4 8.8 shard_map.274
  217.3 20.9 %all-gather.7.cloned.1.call-done = bf16[2048,1024]{0,1:T(8,128)(2,1)} async-done(((bf16[128,1024]{0,1:T(8,128)(2,1)}), bf16[2048,1024]{0,1:T(8,128)(2,1)}) %all-gather.7.cloned.1.call-update) | async-done | bytes 4194320 | tf_op jit(solution)/shard_map/all_gather | solution.py:576
  243.1 12.0 %collective-permute-done.10 = bf16[128,2048]{1,0:T(8,128)(2,1)S(1)} collective-permute-done((bf16[128,2048]{1,0:T(8,128)(2,1)S(1)}, bf16[128,2048]{1,0:T(8,128)(2,1)S(1)}, u32[]{:S(2)}, u32[]{:S(2)}) %collective-permute-start.10) | collective-permute-done | bytes 524320 | tf_op jit(solution)/shard_map/ppermute | solution.py:86
  255.5 40.9 %collective-permute-done.11 = bf16[256,1536]{1,0:T(8,128)(2,1)S(1)} collective-permute-done((bf16[256,1536]{1,0:T(8,128)(2,1)S(1)}, bf16[256,1536]{1,0:T(8,128)(2,1)S(1)}, u32[]{:S(2)}, u32[]{:S(2)}) %collective-permute-start.11) | collective-permute-done | bytes 786464 | tf_op jit(solution)/shard_map/ppermute | solution.py:568
  319.3 46.5 %collective-permute-done.14 = bf16[256,1536]{1,0:T(8,128)(2,1)S(1)} collective-permute-done((bf16[256,1536]{1,0:T(8,128)(2,1)}, bf16[256,1536]{1,0:T(8,128)(2,1)S(1)}, u32[]{:S(2)}, u32[]{:S(2)}) %collective-permute-start.14) | collective-permute-done | bytes 786464 | tf_op jit(solution)/shard_map/ppermute | solution.py:86
  377.1 8.0 collective-permute-done.17
  388.2 13.8 %collective-permute-done.18 = bf16[256,1536]{1,0:T(8,128)(2,1)S(1)} collective-permute-done((bf16[256,1536]{1,0:T(8,128)(2,1)S(1)}, bf16[256,1536]{1,0:T(8,128)(2,1)S(1)}, u32[]{:S(2)}, u32[]{:S(2)}) %collective-permute-start.18) | collective-permute-done | bytes 786464 | tf_op jit(solution)/shard_map/ppermute | solution.py:86
  402.9 29.8 %all-gather.9.cloned.1.call-done.rows_ref = bf16[2048,2048]{1,0:T(8,128)(2,1)} async-done(((bf16[128,2048]{1,0:T(8,128)(2,1)}), bf16[2048,2048]{1,0:T(8,128)(2,1)}) %all-gather.9.cloned.1.call-update) | async-done | bytes 8388624 | tf_op jit(solution)/shard_map/all_gather | solution.py:662
  432.7 55.8 %shard_map.275 = (bf16[2048,2048]{1,0:T(8,128)(2,1)}, bf16[2048,1024]{1,0:T(8,128)(2,1)}, bf16[2048,2048]{1,0:T(8,128)(2,1)}, bf16[2048,2048]{1,0:T(8,128)(2,1)}, f32[2048,1]{1,0:T(8,128)S(1)}) custom-call(s32[1]{0:T(128)} %bitcast.33.expert_ref, bf16[2048,2048]{1,0:T(8,128)(2,1)} %all-gather.9.cloned.1.call-done.rows_ref, ...), custom_call_target="tpu_custom_call" | custom-call | flops 1024 | bytes 1024 | tf_op jit(solution)/shard_map/pallas_call | solution.py:253
  490.2 37.6 %shard_map.277 = (bf16[2,256,1536]{2,1,0:T(8,128)(2,1)S(1)}, bf16[2,256,1536]{2,1,0:T(8,128)(2,1)S(1)}, bf16[2,256,1536]{2,1,0:T(8,128)(2,1)S(1)}, bf16[2,256,15...) custom-call(s32[8]{0:T(128)S(1)} %stack.112.order_ref, ...), custom_call_target="tpu_custom_call" | custom-call | flops 1024 | bytes 1024 | tf_op jit(solution)/shard_map/pallas_call | solution.py:330
  534.5 16.4 %shard_map.276 = (bf16[2048,2048]{1,0:T(8,128)(2,1)}, f32[2048,1]{1,0:T(8,128)S(1)}) custom-call(bf16[2048,1024]{1,0:T(8,128)(2,1)} %get-tuple-element.77.active_ref, bf16[2048,2048]{1,0:T(8,128)(2,1)} %all-gather.11.cloned.1.call-done.cot_ref, f32[2048,1]{1,0:T(8,128)S(1)} %copy-done.6, bf16[2048,1536]{1,0:T(8,128)(2,1)} %constant_dynamic-update-slice_fusion.17.own_ref, ...), custom_call_target="tpu_custom_call" | custom-call | flops 1024 | bytes 1024 | tf_op jit(solution)/shard_map/pallas_call | solution.py:283
  571.4 28.5 %collective-permute-done.22 = bf16[2,256,1536]{2,1,0:T(8,128)(2,1)} collective-permute-done((bf16[2,256,1536]{2,1,0:T(8,128)(2,1)}, bf16[2,256,1536]{2,1,0:T(8,128)(2,1)}, u32[]{:S(2)}, u32[]{:S(2)}) %collective-permute-start.22) | collective-permute-done | bytes 1572896 | tf_op jit(solution)/shard_map/ppermute | solution.py:86
  603.0 30.6 %collective-permute-done.23 = bf16[2,256,1536]{2,1,0:T(8,128)(2,1)} collective-permute-done((bf16[2,256,1536]{2,1,0:T(8,128)(2,1)}, bf16[2,256,1536]{2,1,0:T(8,128)(2,1)}, u32[]{:S(2)}, u32[]{:S(2)}) %collective-permute-start.23) | collective-permute-done | bytes 1572896 | tf_op jit(solution)/shard_map/ppermute | solution.py:86
  642.1 9.8 collective-permute-done.19
  654.1 11.3 %shard_map.278 = (f32[256,1024]{1,0:T(8,128)}, f32[256,1024]{1,0:T(8,128)}, bf16[256,1024]{1,0:T(8,128)(2,1)}, f32[2,1024]{1,0:T(2,128)}, f32[2,256,1]{2,1,0:T(8,128)}) custom-call(f32[256,3072]{1,0:T(8,128)} %copy-done.8, f32[256,3072]{1,0:T(8,128)} %copy-done.8, f32[256,3072]{1,0:T(8,128)} %copy-done.8, f32[2,256,1]{2,1,0:T(8,128)} %rsqrt.33.scale_ref, ...), custom_call_target="tpu_custom_call" | custom-call | flops 1024 | bytes 1024 | tf_op jit(solution)/shard_map/pallas_call | solution.py:440
  680.9 6.7 convolution_convert_fusion
  687.7 14.2 %collective-permute-done.30 = bf16[2,256,1536]{2,1,0:T(8,128)(2,1)S(1)} collective-permute-done((bf16[2,256,1536]{2,1,0:T(8,128)(2,1)}, bf16[2,256,1536]{2,1,0:T(8,128)(2,1)S(1)}, u32[]{:S(2)}, u32[]{:S(2)}) %collective-permute-start.30) | collective-permute-done | bytes 1572896 | tf_op jit(solution)/shard_map/ppermute | solution.py:86
  703.5 17.3 %collective-permute-done.29 = bf16[256,1536]{1,0:T(8,128)(2,1)S(1)} collective-permute-done((bf16[256,1536]{1,0:T(8,128)(2,1)}, bf16[256,1536]{1,0:T(8,128)(2,1)S(1)}, u32[]{:S(2)}, u32[]{:S(2)}) %collective-permute-start.29) | collective-permute-done | bytes 786464 | tf_op jit(solution)/shard_map/ppermute | solution.py:714
  744.3 24.3 %all-to-all-done.4 = f32[16,1,2432]{2,1,0:T(1,128)S(1)} async-done(((f32[16,1,2432]{2,1,0:T(1,128)}), f32[16,1,2432]{2,1,0:T(1,128)S(1)}, u32[]{:S(2)}, u32[]{:S(2)}) %all-to-all-start.4) | async-done | bytes 155680 | tf_op jit(solution)/shard_map/all_to_all | solution.py:784
  782.5 18.5 %collective-permute-done.35 = bf16[128,3072]{1,0:T(8,128)(2,1)} collective-permute-done((bf16[128,3072]{1,0:T(8,128)(2,1)}, bf16[128,3072]{1,0:T(8,128)(2,1)}, u32[]{:S(2)}, u32[]{:S(2)}) %collective-permute-start.35) | collective-permute-done | bytes 786464 | tf_op jit(solution)/shard_map/ppermute | solution.py:106
  817.4 7.1 all-to-all-start.2
  828.2 11.7 %collective-permute-done.37 = bf16[256,3072]{1,0:T(8,128)(2,1)} collective-permute-done((bf16[256,3072]{1,0:T(8,128)(2,1)}, bf16[256,3072]{1,0:T(8,128)(2,1)}, u32[]{:S(2)}, u32[]{:S(2)}) %collective-permute-start.37) | collective-permute-done | bytes 1572896 | tf_op jit(solution)/shard_map/ppermute | solution.py:112
  848.5 36.6 %all-to-all-done.2 = bf16[16,8,2048]{2,1,0:T(8,128)(2,1)} async-done(((bf16[16,8,2048]{2,1,0:T(8,128)(2,1)}), bf16[16,8,2048]{2,1,0:T(8,128)(2,1)}, u32[]{:S(2)}, u32[]{:S(2)}) %all-to-all-start.2) | async-done | bytes 524320 | tf_op jit(solution)/shard_map/all_to_all | solution.py:794
  892.4 6.6 collective-permute-done.25
  901.5 30.7 %collective-permute-done.44 = bf16[256,1536]{1,0:T(8,128)(2,1)S(1)} collective-permute-done((bf16[256,1536]{1,0:T(8,128)(2,1)}, bf16[256,1536]{1,0:T(8,128)(2,1)S(1)}, u32[]{:S(2)}, u32[]{:S(2)}) %collective-permute-start.44) | collective-permute-done | bytes 786464 | tf_op jit(solution)/shard_map/ppermute | solution.py:714
  941.5 15.4 %collective-permute-done.39 = bf16[256,3072]{1,0:T(8,128)(2,1)S(1)} collective-permute-done((bf16[256,3072]{1,0:T(8,128)(2,1)S(1)}, bf16[256,3072]{1,0:T(8,128)(2,1)S(1)}, u32[]{:S(2)}, u32[]{:S(2)}) %collective-permute-start.39) | collective-permute-done | bytes 1572896 | tf_op jit(solution)/shard_map/ppermute | solution.py:112
  964.3 9.5 shard_map.279
  (423 shorter events, 252.7 us)
Async XLA Ops:
  7.2 186.9 %all-gather.5.cloned.1.call-start = ((), (), s32[]{:S(2)}) async-start(), calls=%async_computation.8 | async-start | bytes 13369344 | tf_op jit(solution)/shard_map/all_gather | solution.py:575
  11.6 226.6 %all-gather.7.cloned.1.call-start = ((), (), s32[]{:S(2)}) async-start(), calls=%async_computation.9 | async-start | bytes 4456448 | tf_op jit(solution)/shard_map/all_gather | solution.py:576
  30.3 44.6 %all-to-all-start = ((bf16[16,16,2208]{2,1,0:T(8,128)(2,1)}), bf16[16,16,2208]{2,1,0:T(8,128)(2,1)S(1)}, u32[]{:S(2)}, u32[]{:S(2)}) async-start(bf16[16,16,2208]{2,1,0:T(8,128)(2,1)} %concatenate.100), calls=%async_computation | async-start | bytes 2359296 | tf_op jit(solution)/shard_map/all_to_all | solution.py:532
  36.2 366.8 %all-gather.11.cloned.1.call-start = ((), (), s32[]{:S(2)}) async-start(), calls=%async_computation.11 | async-start | bytes 8912896 | tf_op jit(solution)/shard_map/all_gather | solution.py:663
  75.8 356.9 %all-gather.9.cloned.1.call-start = ((), (), s32[]{:S(2)}) async-start(), calls=%async_computation.10 | async-start | bytes 8912896 | tf_op jit(solution)/shard_map/all_gather | solution.py:662
  83.4 88.7 %collective-permute-start.6 = (bf16[256,1536]{1,0:T(8,128)(2,1)S(1)}, bf16[256,1536]{1,0:T(8,128)(2,1)S(1)}, u32[]{:S(2)}, u32[]{:S(2)}) collective-permute-start(bf16[256,1536]{1,0:T(8,128)(2,1)S(1)} %get-tuple-element.222), channel_id=1, source_target_pairs={{0,24},{2,26},{4,28},{6,30},{8,16},{10,18},{12,20},{14,22},{16,8},... | collective-permute-start | bytes 2359304 | tf_op jit(solution)/shard_map/ppermute | solution.py:568
  83.4 108.3 %collective-permute-start.5 = (bf16[256,1536]{1,0:T(8,128)(2,1)S(1)}, bf16[256,1536]{1,0:T(8,128)(2,1)}, u32[]{:S(2)}, u32[]{:S(2)}) collective-permute-start(bf16[256,1536]{1,0:T(8,128)(2,1)S(1)} %get-tuple-element.223), channel_id=1, source_target_pairs={{0,16},{2,18},{4,20},{6,22},{8,24},{10,26},{12,28},{14,30},{16,0},... | collective-permute-start | bytes 2359304 | tf_op jit(solution)/shard_map/ppermute | solution.py:568
  84.1 107.5 %collective-permute-start.4 = (bf16[256,1536]{1,0:T(8,128)(2,1)S(1)}, bf16[256,1536]{1,0:T(8,128)(2,1)S(1)}, u32[]{:S(2)}, u32[]{:S(2)}) collective-permute-start(bf16[256,1536]{1,0:T(8,128)(2,1)S(1)} %get-tuple-element.224), channel_id=1, source_target_pairs={{0,12},{2,14},{4,8},{6,10},{8,4},{10,6},{12,0},{14,2},{16,28},{18,... | collective-permute-start | bytes 2359304 | tf_op jit(solution)/shard_map/ppermute | solution.py:568
  86.3 107.0 %collective-permute-start.3 = (bf16[256,1536]{1,0:T(8,128)(2,1)S(1)}, bf16[256,1536]{1,0:T(8,128)(2,1)S(1)}, u32[]{:S(2)}, u32[]{:S(2)}) collective-permute-start(bf16[256,1536]{1,0:T(8,128)(2,1)S(1)} %get-tuple-element.225), channel_id=1, source_target_pairs={{0,8},{2,10},{4,12},{6,14},{8,0},{10,2},{12,4},{14,6},{16,24},{18,... | collective-permute-start | bytes 2359304 | tf_op jit(solution)/shard_map/ppermute | solution.py:568
  91.0 103.1 %collective-permute-start.2 = (bf16[256,1536]{1,0:T(8,128)(2,1)S(1)}, bf16[256,1536]{1,0:T(8,128)(2,1)}, u32[]{:S(2)}, u32[]{:S(2)}) collective-permute-start(bf16[256,1536]{1,0:T(8,128)(2,1)S(1)} %get-tuple-element.226), channel_id=1, source_target_pairs={{0,4},{2,6},{4,0},{6,2},{8,12},{10,14},{12,8},{14,10},{16,20},{18,... | collective-permute-start | bytes 2359304 | tf_op jit(solution)/shard_map/ppermute | solution.py:568
  243.1 53.3 %collective-permute-start.11 = (bf16[256,1536]{1,0:T(8,128)(2,1)S(1)}, bf16[256,1536]{1,0:T(8,128)(2,1)S(1)}, u32[]{:S(2)}, u32[]{:S(2)}) collective-permute-start(bf16[256,1536]{1,0:T(8,128)(2,1)S(1)} %copy-done.32), channel_id=1, source_target_pairs={{0,28},{2,30},{4,24},{6,26},{8,20},{10,22},{12,16},{14,18},{16,12}... | collective-permute-start | bytes 2359304 | tf_op jit(solution)/shard_map/ppermute | solution.py:568
  298.3 338.3 %reduce-scatter.4.cloned.1.call-start = ((), (), s32[]{:S(2)}) async-start(), calls=%async_computation.12 | async-start | bytes 8912896 | tf_op jit(solution)/shard_map/reduce_scatter | solution.py:676
  304.1 63.7 %collective-permute-start.16 = (bf16[256,1536]{1,0:T(8,128)(2,1)S(1)}, bf16[256,1536]{1,0:T(8,128)(2,1)S(1)}, u32[]{:S(2)}, u32[]{:S(2)}) collective-permute-start(bf16[256,1536]{1,0:T(8,128)(2,1)S(1)} %copy-done.39), channel_id=1, source_target_pairs={{0,1},{1,0},{2,3},{3,2},{4,5},{5,4},{6,7},{7,6},{8,9},{9,8},{10,11... | collective-permute-start | bytes 2359304 | tf_op jit(solution)/shard_map/ppermute | solution.py:86
  305.3 61.5 %collective-permute-start.15 = (bf16[256,1536]{1,0:T(8,128)(2,1)S(1)}, bf16[256,1536]{1,0:T(8,128)(2,1)S(1)}, u32[]{:S(2)}, u32[]{:S(2)}) collective-permute-start(bf16[256,1536]{1,0:T(8,128)(2,1)S(1)} %copy-done.41), channel_id=1, source_target_pairs={{0,1},{1,0},{2,3},{3,2},{4,5},{5,4},{6,7},{7,6},{8,9},{9,8},{10,11... | collective-permute-start | bytes 2359304 | tf_op jit(solution)/shard_map/ppermute | solution.py:86
  305.5 60.3 %collective-permute-start.14 = (bf16[256,1536]{1,0:T(8,128)(2,1)}, bf16[256,1536]{1,0:T(8,128)(2,1)S(1)}, u32[]{:S(2)}, u32[]{:S(2)}) collective-permute-start(bf16[256,1536]{1,0:T(8,128)(2,1)} %collective-permute-done.2), channel_id=1, source_target_pairs={{0,1},{1,0},{2,3},{3,2},{4,5},{5,4},{6,7},{7,6},{8,9},{9,8},{10,11... | collective-permute-start | bytes 2359304 | tf_op jit(solution)/shard_map/ppermute | solution.py:86
  319.3 51.4 %collective-permute-start.12 = (bf16[256,1536]{1,0:T(8,128)(2,1)S(1)}, bf16[256,1536]{1,0:T(8,128)(2,1)S(1)}, u32[]{:S(2)}, u32[]{:S(2)}) collective-permute-start(bf16[256,1536]{1,0:T(8,128)(2,1)S(1)} %copy-done.31), channel_id=1, source_target_pairs={{0,20},{2,22},{4,16},{6,18},{8,28},{10,30},{12,24},{14,26},{16,4},... | collective-permute-start | bytes 2359304 | tf_op jit(solution)/shard_map/ppermute | solution.py:568
  559.1 213.6 %reduce-scatter.6.cloned.1.call-start = ((), (), s32[]{:S(2)}) async-start(), calls=%async_computation.13 | async-start | bytes 8912896 | tf_op jit(solution)/shard_map/reduce_scatter | solution.py:676
  559.9 73.7 %collective-permute-start.23 = (bf16[2,256,1536]{2,1,0:T(8,128)(2,1)}, bf16[2,256,1536]{2,1,0:T(8,128)(2,1)}, u32[]{:S(2)}, u32[]{:S(2)}) collective-permute-start(bf16[2,256,1536]{2,1,0:T(8,128)(2,1)} %get-tuple-element.94), channel_id=1, source_target_pairs={{0,1},{1,0},{2,3},{3,2},{4,5},{5,4},{6,7},{7,6},{8,9},{9,8},{10,11... | collective-permute-start | bytes 4718600 | tf_op jit(solution)/shard_map/ppermute | solution.py:86
  569.8 82.2 %collective-permute-start.21 = (bf16[256,1536]{1,0:T(8,128)(2,1)}, bf16[256,1536]{1,0:T(8,128)(2,1)}, u32[]{:S(2)}, u32[]{:S(2)}) collective-permute-start(bf16[256,1536]{1,0:T(8,128)(2,1)} %get-tuple-element.236), channel_id=1, source_target_pairs={{0,16},{2,18},{4,20},{6,22},{8,24},{10,26},{12,28},{14,30},{16,0},... | collective-permute-start | bytes 2359304 | tf_op jit(solution)/shard_map/ppermute | solution.py:714
  667.8 53.0 %collective-permute-start.29 = (bf16[256,1536]{1,0:T(8,128)(2,1)}, bf16[256,1536]{1,0:T(8,128)(2,1)S(1)}, u32[]{:S(2)}, u32[]{:S(2)}) collective-permute-start(bf16[256,1536]{1,0:T(8,128)(2,1)} %get-tuple-element.234), channel_id=1, source_target_pairs={{0,24},{2,26},{4,28},{6,30},{8,16},{10,18},{12,20},{14,22},{16,8},... | collective-permute-start | bytes 2359304 | tf_op jit(solution)/shard_map/ppermute | solution.py:714
  679.6 54.1 %collective-permute-start.26 = (bf16[128,2048]{1,0:T(8,128)(2,1)}, bf16[128,2048]{1,0:T(8,128)(2,1)}, u32[]{:S(2)}, u32[]{:S(2)}) collective-permute-start(bf16[128,2048]{1,0:T(8,128)(2,1)} %slice.314), channel_id=1, source_target_pairs={{0,1},{1,0},{2,3},{3,2},{4,5},{5,4},{6,7},{7,6},{8,9},{9,8},{10,11... | collective-permute-start | bytes 1572872 | tf_op jit(solution)/shard_map/ppermute | solution.py:86
  742.3 62.9 %collective-permute-start.36 = (bf16[256,1536]{1,0:T(8,128)(2,1)}, bf16[256,1536]{1,0:T(8,128)(2,1)}, u32[]{:S(2)}, u32[]{:S(2)}) collective-permute-start(bf16[256,1536]{1,0:T(8,128)(2,1)} %get-tuple-element.232), channel_id=1, source_target_pairs={{0,20},{2,22},{4,16},{6,18},{8,28},{10,30},{12,24},{14,26},{16,4},... | collective-permute-start | bytes 2359304 | tf_op jit(solution)/shard_map/ppermute | solution.py:714
  743.5 67.3 %collective-permute-start.41 = (bf16[256,1536]{1,0:T(8,128)(2,1)}, bf16[256,1536]{1,0:T(8,128)(2,1)}, u32[]{:S(2)}, u32[]{:S(2)}) collective-permute-start(bf16[256,1536]{1,0:T(8,128)(2,1)} %get-tuple-element.235), channel_id=1, source_target_pairs={{0,4},{2,6},{4,0},{6,2},{8,12},{10,14},{12,8},{14,10},{16,20},{18,... | collective-permute-start | bytes 2359304 | tf_op jit(solution)/shard_map/ppermute | solution.py:714
  743.6 57.4 %collective-permute-start.33 = (bf16[256,3072]{1,0:T(8,128)(2,1)}, bf16[256,3072]{1,0:T(8,128)(2,1)}, u32[]{:S(2)}, u32[]{:S(2)}) collective-permute-start(bf16[256,3072]{1,0:T(8,128)(2,1)} %get-tuple-element.217), channel_id=1, source_target_pairs={{0,2},{2,0},{4,6},{6,4},{8,10},{10,8},{12,14},{14,12},{16,18},{18,... | collective-permute-start | bytes 4718600 | tf_op jit(solution)/shard_map/ppermute | solution.py:82
  781.9 192.0 %reduce-scatter.8.cloned.1.call-start = ((), (), s32[]{:S(2)}) async-start(), calls=%async_computation.14 | async-start | bytes 4456448 | tf_op jit(solution)/shard_map/reduce_scatter | solution.py:750
  782.0 46.2 %collective-permute-start.32 = (bf16[256,3072]{1,0:T(8,128)(2,1)}, bf16[256,3072]{1,0:T(8,128)(2,1)}, u32[]{:S(2)}, u32[]{:S(2)}) collective-permute-start(bf16[256,3072]{1,0:T(8,128)(2,1)} %get-tuple-element.218), channel_id=1, source_target_pairs={{0,2},{2,0},{4,6},{6,4},{8,10},{10,8},{12,14},{14,12},{16,18},{18,... | collective-permute-start | bytes 4718600 | tf_op jit(solution)/shard_map/ppermute | solution.py:82
  807.5 78.8 %collective-permute-start.42 = (bf16[256,1536]{1,0:T(8,128)(2,1)}, bf16[256,1536]{1,0:T(8,128)(2,1)}, u32[]{:S(2)}, u32[]{:S(2)}) collective-permute-start(bf16[256,1536]{1,0:T(8,128)(2,1)} %get-tuple-element.233), channel_id=1, source_target_pairs={{0,8},{2,10},{4,12},{6,14},{8,0},{10,2},{12,4},{14,6},{16,24},{18,... | collective-permute-start | bytes 2359304 | tf_op jit(solution)/shard_map/ppermute | solution.py:714
  807.6 83.9 %collective-permute-start.43 = (bf16[256,1536]{1,0:T(8,128)(2,1)}, bf16[256,1536]{1,0:T(8,128)(2,1)S(1)}, u32[]{:S(2)}, u32[]{:S(2)}) collective-permute-start(bf16[256,1536]{1,0:T(8,128)(2,1)} %get-tuple-element.231), channel_id=1, source_target_pairs={{0,12},{2,14},{4,8},{6,10},{8,4},{10,6},{12,0},{14,2},{16,28},{18,... | collective-permute-start | bytes 2359304 | tf_op jit(solution)/shard_map/ppermute | solution.py:714
  817.4 67.7 %all-to-all-start.2 = ((bf16[16,8,2048]{2,1,0:T(8,128)(2,1)}), bf16[16,8,2048]{2,1,0:T(8,128)(2,1)}, u32[]{:S(2)}, u32[]{:S(2)}) async-start(bf16[16,8,2048]{2,1,0:T(8,128)(2,1)} %bitcast.56), calls=%async_computation.4 | async-start | bytes 1048576 | tf_op jit(solution)/shard_map/all_to_all | solution.py:794
  824.5 109.6 %collective-permute-start.31 = (bf16[256,3072]{1,0:T(8,128)(2,1)S(1)}, bf16[256,3072]{1,0:T(8,128)(2,1)}, u32[]{:S(2)}, u32[]{:S(2)}) collective-permute-start(bf16[256,3072]{1,0:T(8,128)(2,1)S(1)} %copy-done.26), channel_id=1, source_target_pairs={{0,2},{2,0},{4,6},{6,4},{8,10},{10,8},{12,14},{14,12},{16,18},{18,... | collective-permute-start | bytes 4718600 | tf_op jit(solution)/shard_map/ppermute | solution.py:82
  844.3 89.8 %collective-permute-start.38 = (bf16[256,3072]{1,0:T(8,128)(2,1)}, bf16[256,3072]{1,0:T(8,128)(2,1)}, u32[]{:S(2)}, u32[]{:S(2)}) collective-permute-start(bf16[256,3072]{1,0:T(8,128)(2,1)} %add_convert_fusion.1), channel_id=1, source_target_pairs={{0,8},{2,6},{8,16},{10,2},{16,24},{18,10},{24,28},{26,18},{28,20},... | collective-permute-start | bytes 4718600 | tf_op jit(solution)/shard_map/ppermute | solution.py:112
  886.3 45.9 %collective-permute-start.44 = (bf16[256,1536]{1,0:T(8,128)(2,1)}, bf16[256,1536]{1,0:T(8,128)(2,1)S(1)}, u32[]{:S(2)}, u32[]{:S(2)}) collective-permute-start(bf16[256,1536]{1,0:T(8,128)(2,1)} %get-tuple-element.230), channel_id=1, source_target_pairs={{0,28},{2,30},{4,24},{6,26},{8,20},{10,22},{12,16},{14,18},{16,12}... | collective-permute-start | bytes 2359304 | tf_op jit(solution)/shard_map/ppermute | solution.py:714
  (93 other events, 2144.2 us)
Sparse Core Ops, SparseCore 0:
  11.7 168.5 all-gather.4
  183.1 55.0 all-gather.6
  240.3 112.7 all-gather.10
  355.8 76.9 all-gather.8
  489.6 125.7 reduce-scatter.3
  619.4 133.5 reduce-scatter.5
  817.5 91.4 reduce-scatter.7

commit v6 on v5

--- a/solution.py
+++ b/solution.py
@@ -798,7 +798,7 @@
     block_out = send_back(after(out_rows, qkv_grad))
     token_grad = send_back(rows_grad.astype(BF16))
     qkv_wgrad = after(qkv_wgrad, wgrad_chunks[0], wgrad_chunks[2], summed[6])
-    qkv_wgrad = ring_scatter(pieces_of(qkv_wgrad, chips), chips, BF16, ((by_rows, wgrad_chunks[4]), token_grad, block_out))
+    qkv_wgrad = ring_scatter(pieces_of(qkv_wgrad, chips), chips, BF16, ((by_rows, wgrad_chunks[4]), (token_grad, wgrad_chunks[6]), block_out))
     returned = jnp.stack(wgrad_chunks).reshape(moe_chips, 2, -1, 3 * hidden_half)
     of_sibling = to_sibling(lax.dynamic_index_in_dim(returned, 1 - core, 1, keepdims=False))
     gate_weight_grad, up_weight_grad, down_weight_grad = unpack_experts(

time: 995 us -> 994 us (level)
    all_to_all x2, waiting for transfers between devices: 36.6 us -> 18.3 us  [send_back(): back = lax.all_to_all(back, 'dp', split_axis=0, concat_axis=0, tiled=True)]
    ppermute x3, waiting for transfers between devices: 27.1 us -> 41.6 us  [ring_scatter(): flow = lax.ppermute(flow, 'dp', pairs).astype(F32)]
  transfers between devices with their start and end apart: 58 -> 58, of which waited for: 29 -> 30; matrix products, arithmetic and copies ran while one was open for 16% -> 16% of each run, Pallas kernels for 10% -> 10%
where the time goes in v6:
time: 994 us; the launch traced here: 980 us
  waiting for transfers between devices  554 us (56%)
  Pallas kernels  158 us (16%)
  local copies, waits for them, and re-layouts  85.5 us (9%)
  starting transfers between devices  71.3 us (7%)
  other arithmetic  56.4 us (6%)
  matrix products  38.9 us (4%)
  between operations  15.8 us (2%)
    ppermute x21, waiting for transfers between devices, to_peer(): return lax.ppermute(values, 'tensor', [(0, 1), (1, 0)])  183 us
    ppermute x7, waiting for transfers between devices, fetch_experts(): lax.ppermute(packed_experts[step], 'dp', chip_pairs(step))  141 us
    pallas_call x1, Pallas kernels, expert_rows(): pl.pallas_call(rows_kernel, grid_spec=pltpu.PrefetchScalarGridSpec(num_sc...  55.8 us
    ppermute x7, waiting for transfers between devices, return_wgrads(): lax.ppermute(chunk, 'dp', chip_pairs(step))  44 us
    ppermute x3, waiting for transfers between devices, ring_scatter(): flow = lax.ppermute(flow, 'dp', pairs).astype(F32)  41.6 us
    pallas_call x1, Pallas kernels, expert_wgrads(): pl.pallas_call(wgrad_kernel, grid_spec=pltpu.PrefetchScalarGridSpec(num_s...  37.6 us
    all_to_all x1, waiting for transfers between devices, body(): got = lax.all_to_all(sent, 'dp', split_axis=0, concat_axis=0, tiled=True)  30 us
    all_gather x1, waiting for transfers between devices, body(): lax.all_gather(after(normed_two, own_chunks[7]), 'dp', axis=0, tiled=True...  29.8 us
  transfers between devices with their start and end apart: 58, of which 30 were waited for; matrix products, arithmetic and copies ran while one was open for 16% of the time, Pallas kernels for 10%

profile of v6, /device:TPU:17, one launch (start us, length us, event | category | flops | bytes accessed | tf_op | source)
XLA Modules:
  0.0 980.2 jit_solution(3524170710306391849)
XLA Ops:
  13.1 10.3 %shard_map.272 = (bf16[8,128,1536]{2,1,0:T(8,128)(2,1)}, bf16[8,128,1536]{2,1,0:T(8,128)(2,1)}) custom-call(s32[2]{0:T(128)} %pad_add_fusion.3.place_ref, f32[16,128,512]{2,1,0:T(8,128)} %gate_ref.1, f32[16,128,512]{2,1,0:T(8,128)} %up_ref.1, f32[16,512,128]{2,1,0:T(8,128)} %down_ref.1), custom_call_target="tpu_custom_call" | custom-call | tf_op jit(solution)/shard_map/pallas_call | solution.py:142
  36.2 8.6 shard_map.273
  44.9 30.0 %all-to-all-done = bf16[16,16,2208]{2,1,0:T(8,128)(2,1)S(1)} async-done(((bf16[16,16,2208]{2,1,0:T(8,128)(2,1)}), bf16[16,16,2208]{2,1,0:T(8,128)(2,1)S(1)}, u32[]{:S(2)}, u32[]{:S(2)}) %all-to-all-start) | async-done | bytes 1130528 | tf_op jit(solution)/shard_map/all_to_all | solution.py:532
  92.7 79.3 %collective-permute-done.6 = bf16[256,1536]{1,0:T(8,128)(2,1)S(1)} collective-permute-done((bf16[256,1536]{1,0:T(8,128)(2,1)S(1)}, bf16[256,1536]{1,0:T(8,128)(2,1)S(1)}, u32[]{:S(2)}, u32[]{:S(2)}) %collective-permute-start.6) | collective-permute-done | bytes 786464 | tf_op jit(solution)/shard_map/ppermute | solution.py:568
  172.0 19.6 %collective-permute-done.5 = bf16[256,1536]{1,0:T(8,128)(2,1)} collective-permute-done((bf16[256,1536]{1,0:T(8,128)(2,1)S(1)}, bf16[256,1536]{1,0:T(8,128)(2,1)}, u32[]{:S(2)}, u32[]{:S(2)}) %collective-permute-start.5) | collective-permute-done | bytes 786464 | tf_op jit(solution)/shard_map/ppermute | solution.py:568
  208.4 8.8 shard_map.274
  217.3 20.9 %all-gather.7.cloned.1.call-done = bf16[2048,1024]{0,1:T(8,128)(2,1)} async-done(((bf16[128,1024]{0,1:T(8,128)(2,1)}), bf16[2048,1024]{0,1:T(8,128)(2,1)}) %all-gather.7.cloned.1.call-update) | async-done | bytes 4194320 | tf_op jit(solution)/shard_map/all_gather | solution.py:576
  243.1 12.0 %collective-permute-done.10 = bf16[128,2048]{1,0:T(8,128)(2,1)S(1)} collective-permute-done((bf16[128,2048]{1,0:T(8,128)(2,1)S(1)}, bf16[128,2048]{1,0:T(8,128)(2,1)S(1)}, u32[]{:S(2)}, u32[]{:S(2)}) %collective-permute-start.10) | collective-permute-done | bytes 524320 | tf_op jit(solution)/shard_map/ppermute | solution.py:86
  255.5 40.9 %collective-permute-done.11 = bf16[256,1536]{1,0:T(8,128)(2,1)S(1)} collective-permute-done((bf16[256,1536]{1,0:T(8,128)(2,1)S(1)}, bf16[256,1536]{1,0:T(8,128)(2,1)S(1)}, u32[]{:S(2)}, u32[]{:S(2)}) %collective-permute-start.11) | collective-permute-done | bytes 786464 | tf_op jit(solution)/shard_map/ppermute | solution.py:568
  319.3 46.5 %collective-permute-done.14 = bf16[256,1536]{1,0:T(8,128)(2,1)S(1)} collective-permute-done((bf16[256,1536]{1,0:T(8,128)(2,1)}, bf16[256,1536]{1,0:T(8,128)(2,1)S(1)}, u32[]{:S(2)}, u32[]{:S(2)}) %collective-permute-start.14) | collective-permute-done | bytes 786464 | tf_op jit(solution)/shard_map/ppermute | solution.py:86
  377.1 8.0 collective-permute-done.17
  388.2 13.8 %collective-permute-done.18 = bf16[256,1536]{1,0:T(8,128)(2,1)S(1)} collective-permute-done((bf16[256,1536]{1,0:T(8,128)(2,1)S(1)}, bf16[256,1536]{1,0:T(8,128)(2,1)S(1)}, u32[]{:S(2)}, u32[]{:S(2)}) %collective-permute-start.18) | collective-permute-done | bytes 786464 | tf_op jit(solution)/shard_map/ppermute | solution.py:86
  402.9 29.8 %all-gather.9.cloned.1.call-done.rows_ref = bf16[2048,2048]{1,0:T(8,128)(2,1)} async-done(((bf16[128,2048]{1,0:T(8,128)(2,1)}), bf16[2048,2048]{1,0:T(8,128)(2,1)}) %all-gather.9.cloned.1.call-update) | async-done | bytes 8388624 | tf_op jit(solution)/shard_map/all_gather | solution.py:662
  432.7 55.8 %shard_map.275 = (bf16[2048,2048]{1,0:T(8,128)(2,1)}, bf16[2048,1024]{1,0:T(8,128)(2,1)}, bf16[2048,2048]{1,0:T(8,128)(2,1)}, bf16[2048,2048]{1,0:T(8,128)(2,1)}, f32[2048,1]{1,0:T(8,128)S(1)}) custom-call(s32[1]{0:T(128)} %bitcast.33.expert_ref, bf16[2048,2048]{1,0:T(8,128)(2,1)} %all-gather.9.cloned.1.call-done.rows_ref, ...), custom_call_target="tpu_custom_call" | custom-call | flops 1024 | bytes 1024 | tf_op jit(solution)/shard_map/pallas_call | solution.py:253
  490.2 37.6 %shard_map.277 = (bf16[2,256,1536]{2,1,0:T(8,128)(2,1)S(1)}, bf16[2,256,1536]{2,1,0:T(8,128)(2,1)S(1)}, bf16[2,256,1536]{2,1,0:T(8,128)(2,1)S(1)}, bf16[2,256,15...) custom-call(s32[8]{0:T(128)S(1)} %stack.112.order_ref, ...), custom_call_target="tpu_custom_call" | custom-call | flops 1024 | bytes 1024 | tf_op jit(solution)/shard_map/pallas_call | solution.py:330
  534.5 16.4 %shard_map.276 = (bf16[2048,2048]{1,0:T(8,128)(2,1)}, f32[2048,1]{1,0:T(8,128)S(1)}) custom-call(bf16[2048,1024]{1,0:T(8,128)(2,1)} %get-tuple-element.77.active_ref, bf16[2048,2048]{1,0:T(8,128)(2,1)} %all-gather.11.cloned.1.call-done.cot_ref, f32[2048,1]{1,0:T(8,128)S(1)} %copy-done.6, bf16[2048,1536]{1,0:T(8,128)(2,1)} %constant_dynamic-update-slice_fusion.17.own_ref, ...), custom_call_target="tpu_custom_call" | custom-call | flops 1024 | bytes 1024 | tf_op jit(solution)/shard_map/pallas_call | solution.py:283
  571.4 28.5 %collective-permute-done.22 = bf16[2,256,1536]{2,1,0:T(8,128)(2,1)} collective-permute-done((bf16[2,256,1536]{2,1,0:T(8,128)(2,1)}, bf16[2,256,1536]{2,1,0:T(8,128)(2,1)}, u32[]{:S(2)}, u32[]{:S(2)}) %collective-permute-start.22) | collective-permute-done | bytes 1572896 | tf_op jit(solution)/shard_map/ppermute | solution.py:86
  603.0 30.6 %collective-permute-done.23 = bf16[2,256,1536]{2,1,0:T(8,128)(2,1)} collective-permute-done((bf16[2,256,1536]{2,1,0:T(8,128)(2,1)}, bf16[2,256,1536]{2,1,0:T(8,128)(2,1)}, u32[]{:S(2)}, u32[]{:S(2)}) %collective-permute-start.23) | collective-permute-done | bytes 1572896 | tf_op jit(solution)/shard_map/ppermute | solution.py:86
  642.1 9.8 %collective-permute-done.19 = bf16[128,2048]{1,0:T(8,128)(2,1)S(1)} collective-permute-done((bf16[128,2048]{1,0:T(8,128)(2,1)S(1)}, bf16[128,2048]{1,0:T(8,128)(2,1)S(1)}, u32[]{:S(2)}, u32[]{:S(2)}) %collective-permute-start.19) | collective-permute-done | bytes 524320 | tf_op jit(solution)/shard_map/ppermute | solution.py:86
  654.2 11.3 %shard_map.278 = (f32[256,1024]{1,0:T(8,128)}, f32[256,1024]{1,0:T(8,128)}, bf16[256,1024]{1,0:T(8,128)(2,1)}, f32[2,1024]{1,0:T(2,128)}, f32[2,256,1]{2,1,0:T(8,128)}) custom-call(f32[256,3072]{1,0:T(8,128)} %copy-done.8, f32[256,3072]{1,0:T(8,128)} %copy-done.8, f32[256,3072]{1,0:T(8,128)} %copy-done.8, f32[2,256,1]{2,1,0:T(8,128)} %rsqrt.33.scale_ref, ...), custom_call_target="tpu_custom_call" | custom-call | flops 1024 | bytes 1024 | tf_op jit(solution)/shard_map/pallas_call | solution.py:440
  687.7 14.2 %collective-permute-done.30 = bf16[2,256,1536]{2,1,0:T(8,128)(2,1)S(1)} collective-permute-done((bf16[2,256,1536]{2,1,0:T(8,128)(2,1)}, bf16[2,256,1536]{2,1,0:T(8,128)(2,1)S(1)}, u32[]{:S(2)}, u32[]{:S(2)}) %collective-permute-start.30) | collective-permute-done | bytes 1572896 | tf_op jit(solution)/shard_map/ppermute | solution.py:86
  703.5 17.2 %collective-permute-done.29 = bf16[256,1536]{1,0:T(8,128)(2,1)S(1)} collective-permute-done((bf16[256,1536]{1,0:T(8,128)(2,1)}, bf16[256,1536]{1,0:T(8,128)(2,1)S(1)}, u32[]{:S(2)}, u32[]{:S(2)}) %collective-permute-start.29) | collective-permute-done | bytes 786464 | tf_op jit(solution)/shard_map/ppermute | solution.py:714
  744.3 24.2 %all-to-all-done.4 = f32[16,1,2432]{2,1,0:T(1,128)S(1)} async-done(((f32[16,1,2432]{2,1,0:T(1,128)}), f32[16,1,2432]{2,1,0:T(1,128)S(1)}, u32[]{:S(2)}, u32[]{:S(2)}) %all-to-all-start.4) | async-done | bytes 155680 | tf_op jit(solution)/shard_map/all_to_all | solution.py:784
  782.4 18.5 %collective-permute-done.35 = bf16[128,3072]{1,0:T(8,128)(2,1)} collective-permute-done((bf16[128,3072]{1,0:T(8,128)(2,1)}, bf16[128,3072]{1,0:T(8,128)(2,1)}, u32[]{:S(2)}, u32[]{:S(2)}) %collective-permute-start.35) | collective-permute-done | bytes 786464 | tf_op jit(solution)/shard_map/ppermute | solution.py:106
  817.4 7.1 all-to-all-start.2
  829.8 10.5 %collective-permute-done.37 = bf16[256,3072]{1,0:T(8,128)(2,1)} collective-permute-done((bf16[256,3072]{1,0:T(8,128)(2,1)}, bf16[256,3072]{1,0:T(8,128)(2,1)}, u32[]{:S(2)}, u32[]{:S(2)}) %collective-permute-start.37) | collective-permute-done | bytes 1572896 | tf_op jit(solution)/shard_map/ppermute | solution.py:112
  844.6 26.8 %collective-permute-done.38 = bf16[256,1536]{1,0:T(8,128)(2,1)} collective-permute-done((bf16[256,1536]{1,0:T(8,128)(2,1)}, bf16[256,1536]{1,0:T(8,128)(2,1)}, u32[]{:S(2)}, u32[]{:S(2)}) %collective-permute-start.38) | collective-permute-done | bytes 786464 | tf_op jit(solution)/shard_map/ppermute | solution.py:714
  875.3 18.3 %all-to-all-done.2 = bf16[16,8,2048]{2,1,0:T(8,128)(2,1)} async-done(((bf16[16,8,2048]{2,1,0:T(8,128)(2,1)}), bf16[16,8,2048]{2,1,0:T(8,128)(2,1)}, u32[]{:S(2)}, u32[]{:S(2)}) %all-to-all-start.2) | async-done | bytes 524320 | tf_op jit(solution)/shard_map/all_to_all | solution.py:794
  900.0 7.5 collective-permute-done.25
  913.0 16.1 %collective-permute-done.39 = bf16[256,3072]{1,0:T(8,128)(2,1)} collective-permute-done((bf16[256,3072]{1,0:T(8,128)(2,1)}, bf16[256,3072]{1,0:T(8,128)(2,1)}, u32[]{:S(2)}, u32[]{:S(2)}) %collective-permute-start.39) | collective-permute-done | bytes 1572896 | tf_op jit(solution)/shard_map/ppermute | solution.py:112
  936.9 15.0 %collective-permute-done.40 = bf16[256,3072]{1,0:T(8,128)(2,1)S(1)} collective-permute-done((bf16[256,3072]{1,0:T(8,128)(2,1)S(1)}, bf16[256,3072]{1,0:T(8,128)(2,1)S(1)}, u32[]{:S(2)}, u32[]{:S(2)}) %collective-permute-start.40) | collective-permute-done | bytes 1572896 | tf_op jit(solution)/shard_map/ppermute | solution.py:112
  958.8 9.5 shard_map.279
  (423 shorter events, 260.9 us)
Async XLA Ops:
  7.2 186.9 %all-gather.5.cloned.1.call-start = ((), (), s32[]{:S(2)}) async-start(), calls=%async_computation.8 | async-start | bytes 13369344 | tf_op jit(solution)/shard_map/all_gather | solution.py:575
  11.6 226.6 %all-gather.7.cloned.1.call-start = ((), (), s32[]{:S(2)}) async-start(), calls=%async_computation.9 | async-start | bytes 4456448 | tf_op jit(solution)/shard_map/all_gather | solution.py:576
  30.3 44.6 %all-to-all-start = ((bf16[16,16,2208]{2,1,0:T(8,128)(2,1)}), bf16[16,16,2208]{2,1,0:T(8,128)(2,1)S(1)}, u32[]{:S(2)}, u32[]{:S(2)}) async-start(bf16[16,16,2208]{2,1,0:T(8,128)(2,1)} %concatenate.100), calls=%async_computation | async-start | bytes 2359296 | tf_op jit(solution)/shard_map/all_to_all | solution.py:532
  36.2 366.8 %all-gather.11.cloned.1.call-start = ((), (), s32[]{:S(2)}) async-start(), calls=%async_computation.11 | async-start | bytes 8912896 | tf_op jit(solution)/shard_map/all_gather | solution.py:663
  75.8 356.9 %all-gather.9.cloned.1.call-start = ((), (), s32[]{:S(2)}) async-start(), calls=%async_computation.10 | async-start | bytes 8912896 | tf_op jit(solution)/shard_map/all_gather | solution.py:662
  83.4 88.7 %collective-permute-start.6 = (bf16[256,1536]{1,0:T(8,128)(2,1)S(1)}, bf16[256,1536]{1,0:T(8,128)(2,1)S(1)}, u32[]{:S(2)}, u32[]{:S(2)}) collective-permute-start(bf16[256,1536]{1,0:T(8,128)(2,1)S(1)} %get-tuple-element.222), channel_id=1, source_target_pairs={{0,24},{2,26},{4,28},{6,30},{8,16},{10,18},{12,20},{14,22},{16,8},... | collective-permute-start | bytes 2359304 | tf_op jit(solution)/shard_map/ppermute | solution.py:568
  83.4 108.3 %collective-permute-start.5 = (bf16[256,1536]{1,0:T(8,128)(2,1)S(1)}, bf16[256,1536]{1,0:T(8,128)(2,1)}, u32[]{:S(2)}, u32[]{:S(2)}) collective-permute-start(bf16[256,1536]{1,0:T(8,128)(2,1)S(1)} %get-tuple-element.223), channel_id=1, source_target_pairs={{0,16},{2,18},{4,20},{6,22},{8,24},{10,26},{12,28},{14,30},{16,0},... | collective-permute-start | bytes 2359304 | tf_op jit(solution)/shard_map/ppermute | solution.py:568
  84.1 107.5 %collective-permute-start.4 = (bf16[256,1536]{1,0:T(8,128)(2,1)S(1)}, bf16[256,1536]{1,0:T(8,128)(2,1)S(1)}, u32[]{:S(2)}, u32[]{:S(2)}) collective-permute-start(bf16[256,1536]{1,0:T(8,128)(2,1)S(1)} %get-tuple-element.224), channel_id=1, source_target_pairs={{0,12},{2,14},{4,8},{6,10},{8,4},{10,6},{12,0},{14,2},{16,28},{18,... | collective-permute-start | bytes 2359304 | tf_op jit(solution)/shard_map/ppermute | solution.py:568
  86.3 107.0 %collective-permute-start.3 = (bf16[256,1536]{1,0:T(8,128)(2,1)S(1)}, bf16[256,1536]{1,0:T(8,128)(2,1)S(1)}, u32[]{:S(2)}, u32[]{:S(2)}) collective-permute-start(bf16[256,1536]{1,0:T(8,128)(2,1)S(1)} %get-tuple-element.225), channel_id=1, source_target_pairs={{0,8},{2,10},{4,12},{6,14},{8,0},{10,2},{12,4},{14,6},{16,24},{18,... | collective-permute-start | bytes 2359304 | tf_op jit(solution)/shard_map/ppermute | solution.py:568
  91.0 103.1 %collective-permute-start.2 = (bf16[256,1536]{1,0:T(8,128)(2,1)S(1)}, bf16[256,1536]{1,0:T(8,128)(2,1)}, u32[]{:S(2)}, u32[]{:S(2)}) collective-permute-start(bf16[256,1536]{1,0:T(8,128)(2,1)S(1)} %get-tuple-element.226), channel_id=1, source_target_pairs={{0,4},{2,6},{4,0},{6,2},{8,12},{10,14},{12,8},{14,10},{16,20},{18,... | collective-permute-start | bytes 2359304 | tf_op jit(solution)/shard_map/ppermute | solution.py:568
  243.1 53.3 %collective-permute-start.11 = (bf16[256,1536]{1,0:T(8,128)(2,1)S(1)}, bf16[256,1536]{1,0:T(8,128)(2,1)S(1)}, u32[]{:S(2)}, u32[]{:S(2)}) collective-permute-start(bf16[256,1536]{1,0:T(8,128)(2,1)S(1)} %copy-done.32), channel_id=1, source_target_pairs={{0,28},{2,30},{4,24},{6,26},{8,20},{10,22},{12,16},{14,18},{16,12}... | collective-permute-start | bytes 2359304 | tf_op jit(solution)/shard_map/ppermute | solution.py:568
  298.3 338.3 %reduce-scatter.4.cloned.1.call-start = ((), (), s32[]{:S(2)}) async-start(), calls=%async_computation.12 | async-start | bytes 8912896 | tf_op jit(solution)/shard_map/reduce_scatter | solution.py:676
  304.1 63.7 %collective-permute-start.16 = (bf16[256,1536]{1,0:T(8,128)(2,1)S(1)}, bf16[256,1536]{1,0:T(8,128)(2,1)S(1)}, u32[]{:S(2)}, u32[]{:S(2)}) collective-permute-start(bf16[256,1536]{1,0:T(8,128)(2,1)S(1)} %copy-done.39), channel_id=1, source_target_pairs={{0,1},{1,0},{2,3},{3,2},{4,5},{5,4},{6,7},{7,6},{8,9},{9,8},{10,11... | collective-permute-start | bytes 2359304 | tf_op jit(solution)/shard_map/ppermute | solution.py:86
  305.3 61.5 %collective-permute-start.15 = (bf16[256,1536]{1,0:T(8,128)(2,1)S(1)}, bf16[256,1536]{1,0:T(8,128)(2,1)S(1)}, u32[]{:S(2)}, u32[]{:S(2)}) collective-permute-start(bf16[256,1536]{1,0:T(8,128)(2,1)S(1)} %copy-done.41), channel_id=1, source_target_pairs={{0,1},{1,0},{2,3},{3,2},{4,5},{5,4},{6,7},{7,6},{8,9},{9,8},{10,11... | collective-permute-start | bytes 2359304 | tf_op jit(solution)/shard_map/ppermute | solution.py:86
  305.5 60.3 %collective-permute-start.14 = (bf16[256,1536]{1,0:T(8,128)(2,1)}, bf16[256,1536]{1,0:T(8,128)(2,1)S(1)}, u32[]{:S(2)}, u32[]{:S(2)}) collective-permute-start(bf16[256,1536]{1,0:T(8,128)(2,1)} %collective-permute-done.2), channel_id=1, source_target_pairs={{0,1},{1,0},{2,3},{3,2},{4,5},{5,4},{6,7},{7,6},{8,9},{9,8},{10,11... | collective-permute-start | bytes 2359304 | tf_op jit(solution)/shard_map/ppermute | solution.py:86
  319.3 51.4 %collective-permute-start.12 = (bf16[256,1536]{1,0:T(8,128)(2,1)S(1)}, bf16[256,1536]{1,0:T(8,128)(2,1)S(1)}, u32[]{:S(2)}, u32[]{:S(2)}) collective-permute-start(bf16[256,1536]{1,0:T(8,128)(2,1)S(1)} %copy-done.31), channel_id=1, source_target_pairs={{0,20},{2,22},{4,16},{6,18},{8,28},{10,30},{12,24},{14,26},{16,4},... | collective-permute-start | bytes 2359304 | tf_op jit(solution)/shard_map/ppermute | solution.py:568
  559.1 213.6 %reduce-scatter.6.cloned.1.call-start = ((), (), s32[]{:S(2)}) async-start(), calls=%async_computation.13 | async-start | bytes 8912896 | tf_op jit(solution)/shard_map/reduce_scatter | solution.py:676
  559.9 73.7 %collective-permute-start.23 = (bf16[2,256,1536]{2,1,0:T(8,128)(2,1)}, bf16[2,256,1536]{2,1,0:T(8,128)(2,1)}, u32[]{:S(2)}, u32[]{:S(2)}) collective-permute-start(bf16[2,256,1536]{2,1,0:T(8,128)(2,1)} %get-tuple-element.94), channel_id=1, source_target_pairs={{0,1},{1,0},{2,3},{3,2},{4,5},{5,4},{6,7},{7,6},{8,9},{9,8},{10,11... | collective-permute-start | bytes 4718600 | tf_op jit(solution)/shard_map/ppermute | solution.py:86
  569.8 82.2 %collective-permute-start.21 = (bf16[256,1536]{1,0:T(8,128)(2,1)}, bf16[256,1536]{1,0:T(8,128)(2,1)}, u32[]{:S(2)}, u32[]{:S(2)}) collective-permute-start(bf16[256,1536]{1,0:T(8,128)(2,1)} %get-tuple-element.236), channel_id=1, source_target_pairs={{0,16},{2,18},{4,20},{6,22},{8,24},{10,26},{12,28},{14,30},{16,0},... | collective-permute-start | bytes 2359304 | tf_op jit(solution)/shard_map/ppermute | solution.py:714
  667.8 52.9 %collective-permute-start.29 = (bf16[256,1536]{1,0:T(8,128)(2,1)}, bf16[256,1536]{1,0:T(8,128)(2,1)S(1)}, u32[]{:S(2)}, u32[]{:S(2)}) collective-permute-start(bf16[256,1536]{1,0:T(8,128)(2,1)} %get-tuple-element.234), channel_id=1, source_target_pairs={{0,24},{2,26},{4,28},{6,30},{8,16},{10,18},{12,20},{14,22},{16,8},... | collective-permute-start | bytes 2359304 | tf_op jit(solution)/shard_map/ppermute | solution.py:714
  679.6 54.1 %collective-permute-start.26 = (bf16[128,2048]{1,0:T(8,128)(2,1)}, bf16[128,2048]{1,0:T(8,128)(2,1)}, u32[]{:S(2)}, u32[]{:S(2)}) collective-permute-start(bf16[128,2048]{1,0:T(8,128)(2,1)} %slice.314), channel_id=1, source_target_pairs={{0,1},{1,0},{2,3},{3,2},{4,5},{5,4},{6,7},{7,6},{8,9},{9,8},{10,11... | collective-permute-start | bytes 1572872 | tf_op jit(solution)/shard_map/ppermute | solution.py:86
  742.3 62.9 %collective-permute-start.36 = (bf16[256,1536]{1,0:T(8,128)(2,1)}, bf16[256,1536]{1,0:T(8,128)(2,1)}, u32[]{:S(2)}, u32[]{:S(2)}) collective-permute-start(bf16[256,1536]{1,0:T(8,128)(2,1)} %get-tuple-element.232), channel_id=1, source_target_pairs={{0,20},{2,22},{4,16},{6,18},{8,28},{10,30},{12,24},{14,26},{16,4},... | collective-permute-start | bytes 2359304 | tf_op jit(solution)/shard_map/ppermute | solution.py:714
  743.5 67.3 %collective-permute-start.42 = (bf16[256,1536]{1,0:T(8,128)(2,1)}, bf16[256,1536]{1,0:T(8,128)(2,1)}, u32[]{:S(2)}, u32[]{:S(2)}) collective-permute-start(bf16[256,1536]{1,0:T(8,128)(2,1)} %get-tuple-element.235), channel_id=1, source_target_pairs={{0,4},{2,6},{4,0},{6,2},{8,12},{10,14},{12,8},{14,10},{16,20},{18,... | collective-permute-start | bytes 2359304 | tf_op jit(solution)/shard_map/ppermute | solution.py:714
  743.6 57.3 %collective-permute-start.33 = (bf16[256,3072]{1,0:T(8,128)(2,1)}, bf16[256,3072]{1,0:T(8,128)(2,1)}, u32[]{:S(2)}, u32[]{:S(2)}) collective-permute-start(bf16[256,3072]{1,0:T(8,128)(2,1)} %get-tuple-element.217), channel_id=1, source_target_pairs={{0,2},{2,0},{4,6},{6,4},{8,10},{10,8},{12,14},{14,12},{16,18},{18,... | collective-permute-start | bytes 4718600 | tf_op jit(solution)/shard_map/ppermute | solution.py:82
  781.9 186.4 %reduce-scatter.8.cloned.1.call-start = ((), (), s32[]{:S(2)}) async-start(), calls=%async_computation.14 | async-start | bytes 4456448 | tf_op jit(solution)/shard_map/reduce_scatter | solution.py:750
  782.0 46.4 %collective-permute-start.32 = (bf16[256,3072]{1,0:T(8,128)(2,1)}, bf16[256,3072]{1,0:T(8,128)(2,1)}, u32[]{:S(2)}, u32[]{:S(2)}) collective-permute-start(bf16[256,3072]{1,0:T(8,128)(2,1)} %get-tuple-element.218), channel_id=1, source_target_pairs={{0,2},{2,0},{4,6},{6,4},{8,10},{10,8},{12,14},{14,12},{16,18},{18,... | collective-permute-start | bytes 4718600 | tf_op jit(solution)/shard_map/ppermute | solution.py:82
  807.5 87.3 %collective-permute-start.43 = (bf16[256,1536]{1,0:T(8,128)(2,1)}, bf16[256,1536]{1,0:T(8,128)(2,1)}, u32[]{:S(2)}, u32[]{:S(2)}) collective-permute-start(bf16[256,1536]{1,0:T(8,128)(2,1)} %get-tuple-element.233), channel_id=1, source_target_pairs={{0,8},{2,10},{4,12},{6,14},{8,0},{10,2},{12,4},{14,6},{16,24},{18,... | collective-permute-start | bytes 2359304 | tf_op jit(solution)/shard_map/ppermute | solution.py:714
  807.6 91.5 %collective-permute-start.44 = (bf16[256,1536]{1,0:T(8,128)(2,1)}, bf16[256,1536]{1,0:T(8,128)(2,1)S(1)}, u32[]{:S(2)}, u32[]{:S(2)}) collective-permute-start(bf16[256,1536]{1,0:T(8,128)(2,1)} %get-tuple-element.231), channel_id=1, source_target_pairs={{0,12},{2,14},{4,8},{6,10},{8,4},{10,6},{12,0},{14,2},{16,28},{18,... | collective-permute-start | bytes 2359304 | tf_op jit(solution)/shard_map/ppermute | solution.py:714
  817.4 76.2 %all-to-all-start.2 = ((bf16[16,8,2048]{2,1,0:T(8,128)(2,1)}), bf16[16,8,2048]{2,1,0:T(8,128)(2,1)}, u32[]{:S(2)}, u32[]{:S(2)}) async-start(bf16[16,8,2048]{2,1,0:T(8,128)(2,1)} %bitcast.56), calls=%async_computation.4 | async-start | bytes 1048576 | tf_op jit(solution)/shard_map/all_to_all | solution.py:794
  824.4 46.9 %collective-permute-start.38 = (bf16[256,1536]{1,0:T(8,128)(2,1)}, bf16[256,1536]{1,0:T(8,128)(2,1)}, u32[]{:S(2)}, u32[]{:S(2)}) collective-permute-start(bf16[256,1536]{1,0:T(8,128)(2,1)} %get-tuple-element.230), channel_id=1, source_target_pairs={{0,28},{2,30},{4,24},{6,26},{8,20},{10,22},{12,16},{14,18},{16,12}... | collective-permute-start | bytes 2359304 | tf_op jit(solution)/shard_map/ppermute | solution.py:714
  828.4 84.6 %collective-permute-start.31 = (bf16[256,3072]{1,0:T(8,128)(2,1)S(1)}, bf16[256,3072]{1,0:T(8,128)(2,1)}, u32[]{:S(2)}, u32[]{:S(2)}) collective-permute-start(bf16[256,3072]{1,0:T(8,128)(2,1)S(1)} %copy-done.26), channel_id=1, source_target_pairs={{0,2},{2,0},{4,6},{6,4},{8,10},{10,8},{12,14},{14,12},{16,18},{18,... | collective-permute-start | bytes 4718600 | tf_op jit(solution)/shard_map/ppermute | solution.py:82
  871.3 57.8 %collective-permute-start.39 = (bf16[256,3072]{1,0:T(8,128)(2,1)}, bf16[256,3072]{1,0:T(8,128)(2,1)}, u32[]{:S(2)}, u32[]{:S(2)}) collective-permute-start(bf16[256,3072]{1,0:T(8,128)(2,1)} %add_convert_fusion.1), channel_id=1, source_target_pairs={{0,8},{2,6},{8,16},{10,2},{16,24},{18,10},{24,28},{26,18},{28,20},... | collective-permute-start | bytes 4718600 | tf_op jit(solution)/shard_map/ppermute | solution.py:112
  (93 other events, 2145.2 us)
Sparse Core Ops, SparseCore 0:
  11.7 168.5 all-gather.4
  183.1 55.0 all-gather.6
  240.3 112.7 all-gather.10
  355.8 76.9 all-gather.8
  489.6 125.7 reduce-scatter.3
  619.4 133.5 reduce-scatter.5
  817.5 96.5 reduce-scatter.7
